TPU v7x, 512 devices: a whole 4x8x8 slice. The times are simulated.
512 devices in a mesh: sec: 128 (over x_lo, z, y), tp: 4 (over x_hi, core).
Axes of the slice: x: 4 (x_hi: 2, x_lo: 2; x = x_hi * 2 + x_lo), y: 8, z: 8, core: 2. Of those that a mesh axis runs over, the one named last changes fastest.
Arguments:
- store: bfloat16 [128, 4, 2359296], P('sec', 'tp'), may hold values from -9 to 9
- queries: bfloat16 [256, 128, 576], P('sec'), may hold values from -54 to 54
- new_latent: bfloat16 [256, 576], P('sec'), may hold values from -6 to 6
- cached_len: int32 [256], P('sec'), may hold values from 512 to 2048
- rows: bfloat16 [2048, 7168], P('sec', 'tp'), may hold values from -6 to 6
- expert_ids: int32 [2048, 8], P('sec'), may hold values from 0 to 255, all different within a row; in each aligned block of 16 rows (0 to 15, 16 to 31, ...) at most 5 rows name the same one
- route_gates: float32 [2048, 8], P('sec'), may hold values from 0.05 to 0.6
- capacity: int32 [128, 32], P('sec'), may hold values from 2 to 3
Outputs:
- attended: bfloat16 [256, 128, 512], P('sec', 'tp')
- mixed: bfloat16 [2048, 7168], P('sec', 'tp')
Inputs may be any that keep to these rules, and one draw needn't show every extreme that they name: `expert_ids`: each row names 8 different experts; at most 5 of the rows of one sec index name the same expert.
All inputs are finite; a program needn't handle non-finite values.
Results may differ from a plain program's by a relative error of at most 0.017.
Values may be sent and summed in bfloat16 or wider, within the bound.
No kernel may reach another device: no remote copies, remote signals or barrier semaphores. Data moves between devices by JAX's collectives and lax.ppermute only.
A program may use at most 128 MiB of HBM per device.

v0:
```python
import math

import jax
import jax.numpy as jnp
from jax import lax
from jax.sharding import PartitionSpec as P

LATENT = 512
FF_WIN = 1152
LEN = 2048
CAP = 3


softmax_scale = 1.0 / math.sqrt(192.0)


def shifted(value, axis, steps):
    count = lax.axis_size(axis)
    first, last = (max(0, -steps), min(count, count - steps))
    return lax.ppermute(value, axis, [(source, source + steps) for source in range(first, last)])


def per_device(store, queries, new_latent, cached_len, rows, expert_ids, route_gates, capacity):
    groups = lax.axis_size("sec")
    servers = groups // 4
    parts = lax.axis_size("tp")
    place = lax.axis_index("sec")
    part_index = lax.axis_index("tp")
    memory = store[0, 0]
    slices = rows.shape[1]
    width = slices * parts
    per_row = queries.shape[0]
    heads = queries.shape[1]
    entry = queries.shape[2]
    span = LEN // parts
    hidden_part = FF_WIN // (3 * parts)
    serving = place < servers
    served = 4 * per_row
    incoming = [(queries, new_latent, cached_len)]
    for step in range(1, 4):
        incoming.append(shifted((queries, new_latent, cached_len), "sec", -step * servers))
    asked = jnp.concatenate([item[0] for item in incoming], axis=0)
    fresh = jnp.concatenate([item[1] for item in incoming], axis=0)
    lengths = jnp.concatenate([item[2] for item in incoming], axis=0)
    cache = memory.reshape(served, span, entry)
    offset = part_index * span
    fresh_score = (
        jnp.einsum("rhk,rk->rh", asked, fresh, preferred_element_type=jnp.float32) * softmax_scale
    )

    def block_scores(count):
        scores = (
            jnp.einsum("rhk,rpk->rhp", asked, cache, preferred_element_type=jnp.float32)
            * softmax_scale
        )
        position = offset + jnp.arange(count, dtype=jnp.int32)
        live = position[None, :] < lengths[:, None]
        return (jnp.where(live[:, None, :], scores, -1e30), cache)

    def full_scores():
        return block_scores(span)[0]

    masked = lax.cond(
        serving, full_scores, lambda: jnp.full((served, heads, span), -1e30, jnp.float32)
    )
    local_top = jnp.max(masked, axis=2)
    local_top = jnp.maximum(local_top, fresh_score)
    top = lax.pmax(local_top, "tp")
    empty_pair = (
        jnp.zeros((served, heads, LATENT), jnp.float32),
        jnp.zeros((served, heads), jnp.float32),
    )

    def weigh(scored, keys):
        weights = jnp.exp(scored - top[:, :, None]).astype(jnp.bfloat16)
        total = jnp.sum(lax.optimization_barrier(weights).astype(jnp.float32), axis=2)
        summed = jnp.einsum(
            "rhp,rpc->rhc", weights, keys[:, :, :LATENT], preferred_element_type=jnp.float32
        )
        return (summed, total)

    summed, total = lax.cond(serving, lambda: weigh(masked, cache), lambda: empty_pair)
    first = (part_index == 0).astype(jnp.float32)
    own_weight = jnp.exp(fresh_score - top).astype(jnp.bfloat16)
    own_weight = lax.optimization_barrier(own_weight).astype(jnp.float32) * first
    total = total + own_weight
    summed = summed + own_weight[:, :, None] * fresh[:, None, :LATENT].astype(jnp.float32)
    summed, total = lax.psum((summed, total), "tp")
    share = heads // parts
    summed = lax.dynamic_slice_in_dim(summed, part_index * share, share, 1)
    total = lax.dynamic_slice_in_dim(total, part_index * share, share, 1)
    total = jnp.where(serving, total, 1.0)
    answer = (
        (summed / total[:, :, None])
        .astype(jnp.bfloat16)
        .reshape(4, per_row, heads // parts, LATENT)
    )
    answers = [answer[0]]
    for step in range(1, 4):
        answers.append(shifted(answer[step], "sec", step * servers))
    attended = jnp.stack(answers)[place // servers]
    experts = capacity.shape[1]
    limits = capacity[0]
    labels = jnp.arange(experts, dtype=jnp.int32)
    match = expert_ids[:, :, None] == labels[None, None, :]
    hits = jnp.any(match, axis=1).astype(jnp.int32)
    gate_of = jnp.sum(jnp.where(match, route_gates[:, :, None], 0.0), axis=1)
    rank = jnp.cumsum(hits, axis=0) - hits
    keep = (hits == 1) & (rank < limits[None, :])
    slots = jnp.arange(CAP, dtype=jnp.int32)
    pick = keep[:, :, None] & (rank[:, :, None] == slots[None, None, :])
    pick_mark = pick.astype(jnp.bfloat16)
    whole_rows = lax.all_gather(rows, "tp", axis=1, tiled=True)
    chosen = jnp.einsum(
        "rec,rd->ecd", pick_mark, whole_rows, preferred_element_type=jnp.float32
    ).astype(jnp.bfloat16)
    outgoing = jnp.concatenate(
        [jnp.zeros((servers, CAP, width), jnp.bfloat16), jnp.repeat(chosen, 3, axis=0)], axis=0
    )
    arrived = lax.all_to_all(outgoing, "sec", split_axis=0, concat_axis=0, tiled=True)
    slab = arrived.reshape(groups * CAP, width)
    expert_side = jnp.logical_not(serving)
    span_w = width * hidden_part

    def project():
        gate_w = memory[:span_w].reshape(width, hidden_part)
        up_w = memory[span_w : 2 * span_w].reshape(width, hidden_part)
        gate = jnp.dot(slab, gate_w, preferred_element_type=jnp.float32)
        upper = jnp.dot(slab, up_w, preferred_element_type=jnp.float32)
        return (jax.nn.silu(gate) * upper).astype(jnp.bfloat16)

    hidden = lax.cond(
        expert_side, project, lambda: jnp.zeros((groups * CAP, hidden_part), jnp.bfloat16)
    )
    hidden = lax.all_gather(hidden, "tp", axis=1, tiled=True)

    def descend():
        down_w = memory[2 * span_w : 3 * span_w].reshape(hidden_part * parts, slices)
        return jnp.dot(hidden, down_w, preferred_element_type=jnp.float32).astype(jnp.bfloat16)

    partial_out = lax.cond(
        expert_side, descend, lambda: jnp.zeros((groups * CAP, slices), jnp.bfloat16)
    )
    returned = lax.all_to_all(
        partial_out.reshape(groups, CAP, slices), "sec", split_axis=0, concat_axis=0, tiled=True
    )
    per_expert = jnp.sum(
        returned[servers:].astype(jnp.float32).reshape(experts, 3, CAP, slices), axis=1
    )
    scaled = pick.astype(jnp.float32) * gate_of[:, :, None]
    mixed = jnp.einsum(
        "rec,ecd->rd", scaled, per_expert, preferred_element_type=jnp.float32
    ).astype(jnp.bfloat16)
    return (attended, mixed)


def solution(mesh):
    placed = (
        P("sec", "tp", None),
        P("sec", None, None),
        P("sec", None),
        P("sec"),
        P("sec", "tp"),
        P("sec", None),
        P("sec", None),
        P("sec", None),
    )
    return jax.shard_map(
        per_device,
        mesh=mesh,
        in_specs=placed,
        out_specs=(P("sec", "tp", None), P("sec", "tp")),
        check_vma=False,
    )
```

profile of v0, /device:TPU:16, one launch (start us, length us, event | category | flops | bytes accessed | tf_op | source)
XLA Modules:
  0.0 412.9 jit_solution(5909807761466974284)
XLA Ops:
  8.7 7.4 %all_gather.6 = bf16[16,7168]{1,0:T(8,128)(2,1)S(1)} all-gather(bf16[16,1792]{1,0:T(8,128)(2,1)} %param.20), channel_id=1, replica_groups=mesh['sec'=128,'tp'=4] {'tp'}, dimensions={1}, use_global_device_ids=true | all-gather | bytes 286720 | tf_op jit(solution)/shard_map/all_gather | solution.py:113
  17.9 3.8 broadcast_in_dim.58
  21.7 8.2 %concatenate.15 = bf16[128,3,7168]{2,1,0:T(4,128)(2,1)} pad(bf16[96,3,7168]{2,1,0:T(4,128)(2,1)} %bitcast.32, bf16[]{:T(256)} %constant.73.clone.1), padding=32_0x0_0x0_0 | pad | bytes 9633794 | tf_op jit(solution)/shard_map/concatenate | solution.py:117
  29.9 18.7 %all-to-all-start = ((bf16[128,3,7168]{2,1,0:T(4,128)(2,1)}), bf16[128,3,7168]{2,1,0:T(4,128)(2,1)}, u32[]{:S(2)}, u32[]{:S(2)}) async-start(bf16[128,3,7168]{2,1,0:T(4,128)(2,1)} %concatenate.15), calls=%async_computation | async-start | bytes 14680064 | tf_op jit(solution)/shard_map/all_to_all | solution.py:120
  55.4 101.1 %reduce = bf16[2359296]{0:T(1024)(128)(2,1)} reduce(bf16[1,1,2359296]{2,1,0:T(2,128)(2,1)} %param.16, bf16[]{:T(256)} %constant.84), dimensions={0,1}, to_apply=%param.16.reduce_sub_computation | reduce | bytes 9437186 | tf_op args[0]
  156.4 9.4 %reshape_squeeze.3 = bf16[8,512,576]{2,1,0:T(8,128)(2,1)} reshape(bf16[2359296]{0:T(1024)(128)(2,1)} %reduce) | data formatting | bytes 9437184 | tf_op jit(solution)/shard_map/reshape;squeeze | solution.py:45
  165.9 28.8 %collective-permute-done = s32[2]{0:T(128)S(1)} collective-permute-done((s32[2]{0:T(128)S(1)}, s32[2]{0:T(128)S(1)}, u32[]{:S(2)}, u32[]{:S(2)}) %collective-permute-start) | collective-permute-done | bytes 40 | tf_op jit(solution)/shard_map/ppermute | solution.py:20
  197.3 41.3 %collective-permute-done.2 = s32[2]{0:T(128)S(1)} collective-permute-done((s32[2]{0:T(128)S(1)}, s32[2]{0:T(128)S(1)}, u32[]{:S(2)}, u32[]{:S(2)}) %collective-permute-start.2) | collective-permute-done | bytes 40 | tf_op jit(solution)/shard_map/ppermute | solution.py:20
  240.0 4.5 %collective-permute-done.6 = bf16[2,576]{1,0:T(2,128)(2,1)S(1)} collective-permute-done((bf16[2,576]{1,0:T(2,128)(2,1)S(1)}, bf16[2,576]{1,0:T(2,128)(2,1)S(1)}, u32[]{:S(2)}, u32[]{:S(2)}) %collective-permute-start.6) | collective-permute-done | bytes 2336 | tf_op jit(solution)/shard_map/ppermute | solution.py:20
  247.3 3.5 collective-permute-done.8
  250.9 16.4 %collective-permute-done.5 = bf16[2,128,576]{1,2,0:T(8,128)(2,1)S(1)} collective-permute-done((bf16[2,128,576]{1,2,0:T(8,128)(2,1)S(1)}, bf16[2,128,576]{1,2,0:T(8,128)(2,1)S(1)}, u32[]{:S(2)}, u32[]{:S(2)}) %collective-permute-start.5) | collective-permute-done | bytes 294944 | tf_op jit(solution)/shard_map/ppermute | solution.py:20
  267.4 4.5 %conditional.4 = (f32[8,128,512]{2,1,0:T(8,128)S(1)}, f32[8,128]{1,0:T(8,128)S(1)}) conditional(s32[]{:T(128)} %convert_element_type.55, () %tuple.42, (s32[]{:T(128)}, s32[8]{0:T(128)S(1)}, bf16[8,128,576]{1,2,0:T(8,128)(2,1)S(1)}, bf16[8,512,576]{2,1,0:T(8,128)(2,1)}) %tuple.43), branch_computations={%region_0.0_spmd, %region_1.0_spmd} | conditional | flops 605556224 | bytes 8011840 | solution.py:63
  267.5 4.4 %fusion.26 = (f32[8,128]{1,0:T(8,128)S(1)}, f32[8,128,512]{2,1,0:T(8,128)S(1)}) fusion(bf16[8,128,576]{1,2,0:T(8,128)(2,1)S(1)} %get-tuple-element.43, bf16[8,512,576]{2,1,0:T(8,128)(2,1)} %get-tuple-element.79, pred[8,512]{1,0:T(8,128)(4,1)S(1)} %broadcast_compare_fusion), kind=kOutput, calls=%fused_computation.57 | convolution fusion | flops 605551616 | bytes 8003584 | tf_op jit(solution)/shard_map/cond/branch_1_fun/rhk,rpk->rhp/dot_general | solution.py:53
  272.2 7.2 %pmax.7 = f32[8,128]{1,0:T(8,128)S(1)} all-reduce(f32[8,128]{1,0:T(8,128)S(1)} %multiply_maximum_fusion), channel_id=1, replica_groups=mesh['sec'=128,'tp'=4] {'tp'}, use_global_device_ids=true, to_apply=%region_3.4 | all-reduce | flops 1024 | bytes 8192 | tf_op jit(solution)/shard_map/pmax | solution.py:68
  279.4 3.5 conditional.5
  279.8 2.9 fusion
  282.9 1.6 multiply_add_fusion
  284.8 7.4 %all_gather.7 = bf16[384,384]{0,1:T(8,128)(2,1)S(1)} all-gather(bf16[384,96]{0,1:T(8,128)(2,1)S(1)} %get-tuple-element.102), channel_id=1, replica_groups=mesh['sec'=128,'tp'=4] {'tp'}, dimensions={1}, use_global_device_ids=true | all-gather | bytes 368640 | tf_op jit(solution)/shard_map/all_gather | solution.py:135
  292.3 2.1 reshape.112
  294.4 59.2 %all-to-all-start.1 = ((bf16[128,3,1792]{2,1,0:T(4,128)(2,1)}), bf16[128,3,1792]{2,1,0:T(4,128)(2,1)S(1)}, u32[]{:S(2)}, u32[]{:S(2)}) async-start(bf16[128,3,1792]{2,1,0:T(4,128)(2,1)} %reshape.112), calls=%async_computation.1 | async-start | bytes 3670016 | tf_op jit(solution)/shard_map/all_to_all | solution.py:144
  353.7 8.3 %psum.15 = f32[8,128]{1,0:T(8,128)S(1)} all-reduce(f32[8,128]{1,0:T(8,128)S(1)} %get-tuple-element.92), channel_id=1, replica_groups=mesh['sec'=128,'tp'=4] {'tp'}, use_global_device_ids=true, to_apply=%region_8.9 | all-reduce | flops 1024 | bytes 8192 | tf_op jit(solution)/shard_map/psum | solution.py:88
  362.1 24.0 %all-reduce.3.cloned.1.call-done = f32[8,128,512]{2,1,0:T(8,128)} async-done(((f32[8,128,512]{2,1,0:T(8,128)}), f32[8,128,512]{2,1,0:T(8,128)}) %all-reduce.3.cloned.1.call-update) | async-done | bytes 2097168 | tf_op jit(solution)/shard_map/psum | solution.py:88
  387.3 10.6 %collective-permute-start.9 = (bf16[2,32,512]{2,1,0:T(8,128)(2,1)S(1)}, bf16[2,32,512]{2,1,0:T(8,128)(2,1)S(1)}, u32[]{:S(2)}, u32[]{:S(2)}) collective-permute-start(bf16[2,32,512]{2,1,0:T(8,128)(2,1)S(1)} %get-tuple-element.88), channel_id=1, source_target_pairs={{0,128},{4,132},{8,136},{12,140},{16,144},{20,148},{24,152},{28,15... | collective-permute-start | bytes 196616 | tf_op jit(solution)/shard_map/ppermute | solution.py:20
  397.8 2.3 collective-permute-start.10
  (65 shorter events, 25.5 us)
Async XLA Ops:
  29.9 18.8 %copy-start = (bf16[2,128,576]{1,2,0:T(8,128)(2,1)S(1)}, bf16[2,128,576]{1,2,0:T(8,128)(2,1)}, u32[]{:S(2)}) copy-start(bf16[2,128,576]{1,2,0:T(8,128)(2,1)} %param.17) | copy-start | bytes 884740
  29.9 21.4 %copy-start.3 = (s32[2]{0:T(128)S(1)}, s32[2]{0:T(128)}, u32[]{:S(2)}) copy-start(s32[2]{0:T(128)} %param.19) | copy-start | bytes 28
  29.9 254.7 %all-to-all-start = ((bf16[128,3,7168]{2,1,0:T(4,128)(2,1)}), bf16[128,3,7168]{2,1,0:T(4,128)(2,1)}, u32[]{:S(2)}, u32[]{:S(2)}) async-start(bf16[128,3,7168]{2,1,0:T(4,128)(2,1)} %concatenate.15), calls=%async_computation | async-start | bytes 14680064 | tf_op jit(solution)/shard_map/all_to_all | solution.py:120
  48.6 337.5 %all-reduce.3.cloned.1.call-start = ((), (), s32[]{:S(2)}) async-start(), calls=%async_computation.2 | async-start | bytes 4194304 | tf_op jit(solution)/shard_map/psum | solution.py:88
  48.7 202.1 %collective-permute-start.3 = (bf16[2,128,576]{1,2,0:T(8,128)(2,1)S(1)}, bf16[2,128,576]{1,2,0:T(8,128)(2,1)S(1)}, u32[]{:S(2)}, u32[]{:S(2)}) collective-permute-start(bf16[2,128,576]{1,2,0:T(8,128)(2,1)S(1)} %copy-done), channel_id=1, source_target_pairs={{128,0},{132,4},{136,8},{140,12},{144,16},{148,20},{152,24},{156,2... | collective-permute-start | bytes 884744 | tf_op jit(solution)/shard_map/ppermute | solution.py:20
  50.0 200.9 %collective-permute-start.4 = (bf16[2,128,576]{1,2,0:T(8,128)(2,1)S(1)}, bf16[2,128,576]{1,2,0:T(8,128)(2,1)S(1)}, u32[]{:S(2)}, u32[]{:S(2)}) collective-permute-start(bf16[2,128,576]{1,2,0:T(8,128)(2,1)S(1)} %copy-done), channel_id=1, source_target_pairs={{256,0},{260,4},{264,8},{268,12},{272,16},{276,20},{280,24},{284,2... | collective-permute-start | bytes 884744 | tf_op jit(solution)/shard_map/ppermute | solution.py:20
  51.3 143.4 %collective-permute-start = (s32[2]{0:T(128)S(1)}, s32[2]{0:T(128)S(1)}, u32[]{:S(2)}, u32[]{:S(2)}) collective-permute-start(s32[2]{0:T(128)S(1)} %copy-done.3), channel_id=1, source_target_pairs={{128,0},{132,4},{136,8},{140,12},{144,16},{148,20},{152,24},{156,2... | collective-permute-start | bytes 32 | tf_op jit(solution)/shard_map/ppermute | solution.py:20
  52.6 143.4 %collective-permute-start.1 = (s32[2]{0:T(128)S(1)}, s32[2]{0:T(128)S(1)}, u32[]{:S(2)}, u32[]{:S(2)}) collective-permute-start(s32[2]{0:T(128)S(1)} %copy-done.3), channel_id=1, source_target_pairs={{256,0},{260,4},{264,8},{268,12},{272,16},{276,20},{280,24},{284,2... | collective-permute-start | bytes 32 | tf_op jit(solution)/shard_map/ppermute | solution.py:20
  53.9 184.8 %collective-permute-start.2 = (s32[2]{0:T(128)S(1)}, s32[2]{0:T(128)S(1)}, u32[]{:S(2)}, u32[]{:S(2)}) collective-permute-start(s32[2]{0:T(128)S(1)} %copy-done.3), channel_id=1, source_target_pairs={{384,0},{388,4},{392,8},{396,12},{400,16},{404,20},{408,24},{412,2... | collective-permute-start | bytes 32 | tf_op jit(solution)/shard_map/ppermute | solution.py:20
  156.4 38.3 %copy-start.2 = (bf16[2,576]{1,0:T(2,128)(2,1)S(1)}, bf16[2,576]{1,0:T(2,128)(2,1)}, u32[]{:S(2)}) copy-start(bf16[2,576]{1,0:T(2,128)(2,1)} %param.18) | copy-start | bytes 6916
  194.7 49.8 %collective-permute-start.6 = (bf16[2,576]{1,0:T(2,128)(2,1)S(1)}, bf16[2,576]{1,0:T(2,128)(2,1)S(1)}, u32[]{:S(2)}, u32[]{:S(2)}) collective-permute-start(bf16[2,576]{1,0:T(2,128)(2,1)S(1)} %copy-done.2), channel_id=1, source_target_pairs={{128,0},{132,4},{136,8},{140,12},{144,16},{148,20},{152,24},{156,2... | collective-permute-start | bytes 6920 | tf_op jit(solution)/shard_map/ppermute | solution.py:20
  196.0 51.2 %collective-permute-start.7 = (bf16[2,576]{1,0:T(2,128)(2,1)S(1)}, bf16[2,576]{1,0:T(2,128)(2,1)S(1)}, u32[]{:S(2)}, u32[]{:S(2)}) collective-permute-start(bf16[2,576]{1,0:T(2,128)(2,1)S(1)} %copy-done.2), channel_id=1, source_target_pairs={{256,0},{260,4},{264,8},{268,12},{272,16},{276,20},{280,24},{284,2... | collective-permute-start | bytes 6920 | tf_op jit(solution)/shard_map/ppermute | solution.py:20
  238.7 12.1 %collective-permute-start.8 = (bf16[2,576]{1,0:T(2,128)(2,1)S(1)}, bf16[2,576]{1,0:T(2,128)(2,1)S(1)}, u32[]{:S(2)}, u32[]{:S(2)}) collective-permute-start(bf16[2,576]{1,0:T(2,128)(2,1)S(1)} %copy-done.2), channel_id=1, source_target_pairs={{384,0},{388,4},{392,8},{396,12},{400,16},{404,20},{408,24},{412,2... | collective-permute-start | bytes 6920 | tf_op jit(solution)/shard_map/ppermute | solution.py:20
  244.5 22.8 %collective-permute-start.5 = (bf16[2,128,576]{1,2,0:T(8,128)(2,1)S(1)}, bf16[2,128,576]{1,2,0:T(8,128)(2,1)S(1)}, u32[]{:S(2)}, u32[]{:S(2)}) collective-permute-start(bf16[2,128,576]{1,2,0:T(8,128)(2,1)S(1)} %copy-done), channel_id=1, source_target_pairs={{384,0},{388,4},{392,8},{396,12},{400,16},{404,20},{408,24},{412,2... | collective-permute-start | bytes 884744 | tf_op jit(solution)/shard_map/ppermute | solution.py:20
  294.4 59.2 %copy-start.1 = (f32[16,8]{0,1:T(8,128)S(1)}, f32[16,8]{0,1:T(8,128)}, u32[]{:S(2)}) copy-start(f32[16,8]{0,1:T(8,128)} %param.22) | copy-start | bytes 1540
  294.4 109.6 %all-to-all-start.1 = ((bf16[128,3,1792]{2,1,0:T(4,128)(2,1)}), bf16[128,3,1792]{2,1,0:T(4,128)(2,1)S(1)}, u32[]{:S(2)}, u32[]{:S(2)}) async-start(bf16[128,3,1792]{2,1,0:T(4,128)(2,1)} %reshape.112), calls=%async_computation.1 | async-start | bytes 3670016 | tf_op jit(solution)/shard_map/all_to_all | solution.py:144
  387.3 14.3 %collective-permute-start.9 = (bf16[2,32,512]{2,1,0:T(8,128)(2,1)S(1)}, bf16[2,32,512]{2,1,0:T(8,128)(2,1)S(1)}, u32[]{:S(2)}, u32[]{:S(2)}) collective-permute-start(bf16[2,32,512]{2,1,0:T(8,128)(2,1)S(1)} %get-tuple-element.88), channel_id=1, source_target_pairs={{0,128},{4,132},{8,136},{12,140},{16,144},{20,148},{24,152},{28,15... | collective-permute-start | bytes 196616 | tf_op jit(solution)/shard_map/ppermute | solution.py:20
  397.8 4.2 %collective-permute-start.10 = (bf16[2,32,512]{2,1,0:T(8,128)(2,1)S(1)}, bf16[2,32,512]{2,1,0:T(8,128)(2,1)S(1)}, u32[]{:S(2)}, u32[]{:S(2)}) collective-permute-start(bf16[2,32,512]{2,1,0:T(8,128)(2,1)S(1)} %get-tuple-element.87), channel_id=1, source_target_pairs={{0,256},{4,260},{8,264},{12,268},{16,272},{20,276},{24,280},{28,28... | collective-permute-start | bytes 196616 | tf_op jit(solution)/shard_map/ppermute | solution.py:20
  400.1 3.2 collective-permute-start.11
Sparse Core Ops, SparseCore 0:
  284.7 101.3 all-reduce.2
where the time goes:
time: 414 us; the launch traced here: 413 us
  waiting for transfers between devices  122 us (29%)
  other arithmetic  107 us (26%)
  starting transfers between devices  104 us (25%)
  blocking collectives  30.3 us (7%)
  local copies, waits for them, and re-layouts  26.2 us (6%)
  between operations  14.4 us (3%)
  matrix products  9.03 us (2%)
    unnamed x1, other arithmetic  101 us
    ppermute x12, waiting for transfers between devices, shifted(): lax.ppermute(value, axis, [(source, source + steps) for source in range(f...  97.8 us
    all_to_all x1, starting transfers between devices, per_device(): lax.all_to_all(partial_out.reshape(groups, CAP, slices), 'sec', split_axi...  59.2 us
    ppermute x12, starting transfers between devices, shifted(): lax.ppermute(value, axis, [(source, source + steps) for source in range(f...  25.9 us
    psum x1, waiting for transfers between devices, per_device(): summed, total = lax.psum((summed, total), 'tp')  24 us
    all_to_all x1, starting transfers between devices, per_device(): lax.all_to_all(outgoing, 'sec', split_axis=0, concat_axis=0, tiled=True)  18.7 us
    another operation x1, local copies, waits for them, and re-layouts, per_device(): cache = memory.reshape(served, span, entry)  9.43 us
    psum x1, blocking collectives, per_device(): summed, total = lax.psum((summed, total), 'tp')  8.33 us
  transfers between devices with their start and end apart: 15, of which 9 were waited for; matrix products, arithmetic and copies ran while one was open for 30% of the time, Pallas kernels for 0%

commit v1 on v0

v1 whole, which is shorter than its diff:
```python
import functools
import math

import jax
import jax.numpy as jnp
from jax import lax
from jax.experimental import pallas as pl
from jax.experimental.pallas import tpu as pltpu
from jax.sharding import PartitionSpec as P

LATENT = 512
KV = 576
LP = 512
CAP = 3
HD = 96
DQ = 1792
PART = 640
f32 = jnp.float32
bf16 = jnp.bfloat16
VM = 48 << 20

softmax_scale = 1.0 / math.sqrt(192.0)


def dot(a, b, dims=((1,), (0,))):
    return lax.dot_general(a, b, (dims, ((), ())), preferred_element_type=f32)


def pieces(value):
    high = value.astype(bf16).astype(f32)
    middle = (value - high).astype(bf16).astype(f32)
    return high, middle, value - high - middle


def flat_rows(s_ref, scr):
    scr[...] = s_ref[...].astype(f32).reshape(scr.shape)


def dispatch_kernel(sel_ref, rows_ref, out_ref):
    source = lax.broadcasted_iota(jnp.int32, (256, 256), 0)
    target = lax.broadcasted_iota(jnp.int32, (256, 256), 1)
    order = (source == 4 * (target % 64) + target // 64).astype(f32).astype(bf16)
    for b in range(DQ // 256):
        span = slice(256 * b, 256 * b + 256)
        turned = dot(rows_ref[:, span], order).astype(bf16)
        for c in range(CAP):
            out_ref[:, DQ * c + 256 * b : DQ * c + 256 * b + 256] = dot(sel_ref[c], turned).astype(bf16)


def attend_kernel(info_ref, s_ref, q_ref, p_ref, scr, keys):
    row = pl.program_id(0)
    flat_rows(s_ref, scr)
    for m in range(9):
        keys[:, 128 * m : 128 * m + 128] = scr[pl.ds(m, LP // 2, stride=9), :].astype(bf16)
    lane = lax.broadcasted_iota(jnp.int32, (128, PART), 1)
    even_q = jnp.where(lane < KV, q_ref[0].astype(f32), 0.0)
    odd_q = pltpu.roll(even_q, 64, 1).astype(bf16)
    even_q = even_q.astype(bf16)
    even = dot(even_q, keys[:, :640], ((1,), (1,))) * softmax_scale
    odd = dot(odd_q, keys[:, 512:], ((1,), (1,))) * softmax_scale
    left = info_ref[row] - info_ref[8]
    position = 2 * lax.broadcasted_iota(jnp.int32, (128, LP // 2), 1)
    even = jnp.where(position < left, even, -1e30)
    odd = jnp.where(position + 1 < left, odd, -1e30)
    top = jnp.maximum(jnp.max(even, axis=1, keepdims=True), jnp.max(odd, axis=1, keepdims=True))
    even = jnp.where(position < left, jnp.exp(even - top), 0.0).astype(bf16)
    odd = jnp.where(position + 1 < left, jnp.exp(odd - top), 0.0).astype(bf16)
    total = jnp.sum(even.astype(f32), axis=1, keepdims=True) + jnp.sum(odd.astype(f32), axis=1, keepdims=True)
    summed = dot(even, keys[:, :LATENT]) + dot(odd, keys[:, 512:])[:, 64 : 64 + LATENT]
    summed = summed.astype(bf16)
    lane = lax.broadcasted_iota(jnp.int32, (128, 128), 1)
    stats = jnp.zeros((128, 128), f32)
    for at, piece in enumerate(pieces(top) + pieces(total)):
        stats = jnp.where(lane == at, piece, stats)
    stats = stats.astype(bf16)
    first = pl.ds(pl.multiple_of(row * 32, 32), 32)
    second = pl.ds(pl.multiple_of(256 + row * 32, 32), 32)
    for t in range(4):
        heads = slice(32 * t, 32 * t + 32)
        p_ref[t, first, :] = summed[heads, :384]
        p_ref[t, second, 0:128] = summed[heads, 384:]
        p_ref[t, second, 128:256] = stats[heads]


def attend(store, asked, info):
    return pl.pallas_call(
        attend_kernel,
        grid_spec=pltpu.PrefetchScalarGridSpec(
            num_scalar_prefetch=1,
            grid=(8,),
            in_specs=[
                pl.BlockSpec((1, 1, LP * KV), lambda i, info: (0, 0, i)),
                pl.BlockSpec((1, 128, PART), lambda i, info: (i, 0, 0)),
            ],
            out_specs=pl.BlockSpec((4, 896, 384), lambda i, info: (0, 0, 0)),
            scratch_shapes=[pltpu.VMEM((LP * KV // 128, 128), f32), pltpu.VMEM((LP // 2, 2 * KV), bf16)],
        ),
        out_shape=jax.ShapeDtypeStruct((4, 896, 384), bf16),
        compiler_params=pltpu.CompilerParams(vmem_limit_bytes=VM),
    )(info, store, asked)


def unpack_kernel(s_ref, p_ref, w_ref, scr):
    step = pl.program_id(0)
    flat_rows(s_ref, scr)

    @pl.when(step < 8)
    def _():
        for m in range(3):
            p_ref[0, :, 128 * m : 128 * m + 128] = scr[pl.ds(m, 448, stride=3), :].astype(bf16)

    @pl.when(step >= 8)
    def _():
        for m in range(14):
            at = 128 * (m % 5)
            w_ref[m // 5, :, at : at + 128] = scr[pl.ds(m, HD, stride=14), :].astype(bf16)
        w_ref[2, :, 512:640] = jnp.zeros((HD, 128), bf16)


def unpack(store):
    return pl.pallas_call(
        unpack_kernel,
        grid=(12,),
        in_specs=[pl.BlockSpec((1, 1, DQ * HD), lambda i: (0, 0, i))],
        out_specs=[
            pl.BlockSpec((1, 448, 384), lambda i: (jnp.where(i < 8, i % 4, 3), jnp.where(i < 4, 0, 1), 0)),
            pl.BlockSpec((3, HD, PART), lambda i: (0, jnp.maximum(i - 8, 0), 0)),
        ],
        out_shape=[jax.ShapeDtypeStruct((4, 896, 384), bf16), jax.ShapeDtypeStruct((3, 384, PART), bf16)],
        scratch_shapes=[pltpu.VMEM((DQ * HD // 128, 128), f32)],
        compiler_params=pltpu.CompilerParams(vmem_limit_bytes=VM),
    )(store)


def weights_kernel(p_ref, w_ref):
    for half in range(2):
        for r in range(4):
            span = slice(HD * r, HD * r + HD)
            rows = slice(448 * half, 448 * half + 448)
            found = jnp.concatenate([p_ref[t, rows, span] for t in range(4)], axis=1)
            for b in range(7):
                w_ref[half, 256 * b + 64 * r : 256 * b + 64 * r + 64, :] = found[64 * b : 64 * b + 64]


def arrange(arrived):
    return pl.pallas_call(
        weights_kernel,
        out_shape=jax.ShapeDtypeStruct((2, DQ, 384), bf16),
        compiler_params=pltpu.CompilerParams(vmem_limit_bytes=VM),
    )(arrived)


def join_kernel(p_ref, out_ref):
    tops, totals = [], []
    for t in range(4):
        stats = p_ref[t, 256:512, 128:256].astype(f32)
        tops.append(stats[:, 0:1] + stats[:, 1:2] + stats[:, 2:3])
        totals.append(stats[:, 3:4] + stats[:, 4:5] + stats[:, 5:6])
    top = functools.reduce(jnp.maximum, tops)
    scales = [jnp.exp(own - top) for own in tops]
    total = sum(scale * own for scale, own in zip(scales, totals))
    scales = [scale / total for scale in scales]
    out_ref[:, :384] = sum(scales[t] * p_ref[t, 0:256, :].astype(f32) for t in range(4)).astype(bf16)
    out_ref[:, 384:512] = sum(scales[t] * p_ref[t, 256:512, 0:128].astype(f32) for t in range(4)).astype(bf16)
    lane = lax.broadcasted_iota(jnp.int32, (256, 128), 1)
    stats = jnp.zeros((256, 128), f32)
    for at, piece in enumerate(pieces(top + jnp.log(total))):
        stats = jnp.where(lane == at, piece, stats)
    out_ref[:, 512:640] = stats.astype(bf16)


def join(arrived):
    return pl.pallas_call(
        join_kernel,
        out_shape=jax.ShapeDtypeStruct((256, PART), bf16),
        compiler_params=pltpu.CompilerParams(vmem_limit_bytes=VM),
    )(arrived)


def project_kernel(x_ref, w_ref, z_ref):
    for half in range(2):
        turned = dot(x_ref[...], w_ref[half]).T.astype(bf16)
        for t in range(4):
            z_ref[t, HD * half : HD * half + HD, :] = turned[HD * t : HD * t + HD]


def project(slab, weights):
    return pl.pallas_call(
        project_kernel,
        grid=(CAP,),
        in_specs=[
            pl.BlockSpec((128, DQ), lambda c: (0, c)),
            pl.BlockSpec((2, DQ, 384), lambda c: (0, 0, 0)),
        ],
        out_specs=pl.BlockSpec((4, 2 * HD, 128), lambda c: (0, 0, c)),
        out_shape=jax.ShapeDtypeStruct((4, 2 * HD, 384), bf16),
        compiler_params=pltpu.CompilerParams(vmem_limit_bytes=VM),
    )(slab, weights)


def descend_kernel(h_ref, w0_ref, w1_ref, w2_ref, out_ref, scr):
    result = jnp.zeros((384, PART), f32)
    for d, w_ref in enumerate((w0_ref, w1_ref, w2_ref)):
        for t in range(4):
            scr[HD * t : HD * t + HD, :] = h_ref[t, d]
        result = result + dot(scr[...], w_ref[...], ((0,), (0,)))
    for c in range(CAP):
        out_ref[:, PART * c : PART * c + PART] = result[128 * c : 128 * c + 128].astype(bf16)


def descend(hidden, w0, w1, w2):
    return pl.pallas_call(
        descend_kernel,
        out_shape=jax.ShapeDtypeStruct((128, CAP * PART), bf16),
        scratch_shapes=[pltpu.VMEM((384, 384), bf16)],
        compiler_params=pltpu.CompilerParams(vmem_limit_bytes=VM),
    )(hidden, w0, w1, w2)


def combine_kernel(a_ref, x_ref, out_ref):
    result = jnp.zeros((48, PART), f32)
    for c in range(CAP):
        block = x_ref[:, PART * c : PART * c + PART]
        both = dot(a_ref[c], block)
        result = result + (both[:48] + both[48:])
    result = result.astype(bf16)
    out_ref[:, 0:640] = result[0:16]
    out_ref[:, 640:1280] = result[16:32]
    out_ref[:, 1280:1792] = result[32:48, :512]


def per_device(store, queries, new_latent, cached_len, rows, expert_ids, route_gates, capacity):
    groups = lax.axis_size("sec")
    servers = groups // 4
    place = lax.axis_index("sec")
    part = lax.axis_index("tp")
    serving = place < servers
    both = ("sec", "tp")
    core = part % 2

    experts = capacity.shape[1]
    labels = jnp.arange(experts, dtype=jnp.int32)
    match = expert_ids[:, :, None] == labels[None, None, :]
    hits = jnp.any(match, axis=1).astype(jnp.int32)
    gate_of = jnp.sum(jnp.where(match, route_gates[:, :, None], 0.0), axis=1)
    rank = jnp.cumsum(hits, axis=0) - hits
    keep = (hits == 1) & (rank < capacity[0][None, :])
    slots = jnp.arange(CAP, dtype=jnp.int32)
    pick = (keep[None] & (rank[None] == slots[:, None, None])).astype(f32)
    spread = jnp.pad(jnp.repeat(pick, 3, axis=2), ((0, 0), (0, 0), (servers, 0)))
    sel = jnp.swapaxes(spread, 1, 2).astype(bf16)
    outgoing = pl.pallas_call(
        dispatch_kernel, out_shape=jax.ShapeDtypeStruct((groups, CAP * DQ), bf16)
    )(sel, rows)
    arrived = lax.all_to_all(outgoing, "sec", split_axis=0, concat_axis=0, tiled=True)

    digits = jnp.stack([cached_len // 64, cached_len % 64], axis=1).astype(bf16)
    digits = jnp.pad(digits, ((0, 0), (0, PART - KV - 2)))
    asked = jnp.concatenate([queries, jnp.broadcast_to(digits[:, None, :], (2, 128, PART - KV))], axis=2)
    half = lax.dynamic_slice_in_dim(asked, core * 64, 64, 1)
    incoming = [half]
    for k in range(1, 4):
        incoming.append(lax.ppermute(half, "sec", [(k * servers + a, a) for a in range(servers)]))
    half = jnp.concatenate(incoming, axis=0)
    other = lax.ppermute(half, both, [(4 * a + t, 4 * a + (t ^ 1)) for a in range(servers) for t in range(4)])
    asked = jnp.concatenate([jnp.where(core == 0, half, other), jnp.where(core == 0, other, half)], axis=1)
    lengths = asked[:, 0, KV].astype(jnp.int32) * 64 + asked[:, 0, KV + 1].astype(jnp.int32)
    info = jnp.concatenate([lengths, (part * LP).reshape(1).astype(jnp.int32)])

    def serve():
        return attend(store, asked, info), jnp.zeros((3, 384, PART), bf16)

    payload, down = lax.cond(serving, serve, lambda: tuple(unpack(store)))
    arranged = lax.all_to_all(payload, "tp", split_axis=0, concat_axis=0, tiled=True)

    def sibling(value, step):
        return lax.ppermute(
            value,
            "sec",
            [(servers + 3 * e + j, servers + 3 * e + (j + step) % 3) for e in range(experts) for j in range(3)],
        )

    third = (place - servers) % 3
    downs = [lax.dynamic_index_in_dim(down, third, 0, keepdims=False)]
    for step in (1, 2):
        downs.append(sibling(lax.dynamic_index_in_dim(down, (third + step) % 3, 0, keepdims=False), step))

    answer, weights = lax.cond(
        serving,
        lambda: (join(arranged), jnp.zeros((2, DQ, 384), bf16)),
        lambda: (jnp.zeros((256, PART), bf16), arrange(arranged)),
    )

    answer = answer.reshape(4, 64, PART)
    returned = answer[0]
    for k in range(1, 4):
        returned = returned + lax.ppermute(answer[k], "sec", [(a, k * servers + a) for a in range(servers)])
    mine = lax.dynamic_slice_in_dim(queries, part * 32, 32, 1)
    own = jnp.einsum("rhk,rk->rh", mine, new_latent, preferred_element_type=f32) * softmax_scale
    own = own[:, :, None]
    returned = returned.reshape(2, 32, PART).astype(f32)
    others = returned[:, :, 512:513] + returned[:, :, 513:514] + returned[:, :, 514:515]
    top = jnp.maximum(own, others)
    own, others = jnp.exp(own - top), jnp.exp(others - top)
    attended = (others * returned[:, :, :LATENT] + own * new_latent[:, None, :LATENT].astype(f32)) / (own + others)
    attended = attended.astype(bf16)

    partial = lax.cond(
        serving, lambda: jnp.zeros((4, 2 * HD, 384), bf16), lambda: project(arrived, weights)
    )
    partial = lax.all_to_all(partial, "tp", split_axis=0, concat_axis=0, tiled=True)
    partial = jnp.sum(partial.astype(f32), axis=0)
    hidden = (jax.nn.silu(partial[:HD]) * partial[HD:]).astype(bf16)
    hidden = jnp.stack([hidden, sibling(hidden, 1), sibling(hidden, 2)])
    hidden = lax.all_gather(hidden, "tp", axis=0)
    result = lax.cond(
        serving, lambda: jnp.zeros((groups, CAP * PART), bf16), lambda: descend(hidden, *downs)
    )
    result = lax.all_to_all(result, "sec", split_axis=0, concat_axis=0, tiled=True)

    scaled = spread * jnp.pad(jnp.repeat(gate_of, 3, axis=1), ((0, 0), (servers, 0)))[None]
    holder = (jnp.arange(groups) - servers) % 3
    scaled = jnp.where(holder == jnp.arange(3)[:, None, None, None], scaled[None], 0.0)
    scaled = jnp.swapaxes(scaled, 0, 1).reshape(CAP, 48, groups)
    high = lax.reduce_precision(scaled, 8, 7)
    weight = jnp.concatenate([high, scaled - high], axis=1).astype(bf16)
    mixed = pl.pallas_call(
        combine_kernel, out_shape=jax.ShapeDtypeStruct((16, DQ), bf16)
    )(weight, result)
    return (attended, mixed)


def solution(mesh):
    placed = (
        P("sec", "tp", None),
        P("sec", None, None),
        P("sec", None),
        P("sec"),
        P("sec", "tp"),
        P("sec", None),
        P("sec", None),
        P("sec", None),
    )
    return jax.shard_map(
        per_device,
        mesh=mesh,
        in_specs=placed,
        out_specs=(P("sec", "tp", None), P("sec", "tp")),
        check_vma=False,
    )
```

time: 414 us -> 217 us (0.52)
  the two profiles are of different devices: /device:TPU:16 before, /device:TPU:8 now
where the time goes in v1:
time: 217 us; the launch traced here: 215 us
  starting transfers between devices  80.7 us (37%)
  waiting for transfers between devices  75.8 us (35%)
  local copies, waits for them, and re-layouts  20.5 us (9%)
  Pallas kernels  18.3 us (8%)
  blocking collectives  10 us (5%)
  other arithmetic  8.57 us (4%)
    all_to_all x1, starting transfers between devices, per_device(): lax.all_to_all(result, 'sec', split_axis=0, concat_axis=0, tiled=True)  34.2 us
    ppermute x3, waiting for transfers between devices, per_device(): lax.ppermute(half, 'sec', [(k * servers + a, a) for a in range(servers)])  33.9 us
    all_to_all x1, waiting for transfers between devices, per_device(): lax.all_to_all(payload, 'tp', split_axis=0, concat_axis=0, tiled=True)  23.7 us
    all_to_all x1, starting transfers between devices, per_device(): lax.all_to_all(outgoing, 'sec', split_axis=0, concat_axis=0, tiled=True)  18.8 us
    unnamed x21, local copies, waits for them, and re-layouts  15.7 us
    pallas_call x1, Pallas kernels, attend(): pl.pallas_call(attend_kernel, grid_spec=pltpu.PrefetchScalarGridSpec(num_...  12.3 us
    ppermute x3, starting transfers between devices, per_device(): lax.ppermute(answer[k], 'sec', [(a, k * servers + a) for a in range(serve...  10.1 us
    all_gather x1, blocking collectives, per_device(): hidden = lax.all_gather(hidden, 'tp', axis=0)  10 us
  transfers between devices with their start and end apart: 15, of which 8 were waited for; matrix products, arithmetic and copies ran while one was open for 7% of the time, Pallas kernels for 6%

profile of v1, /device:TPU:8, one launch (start us, length us, event | category | flops | bytes accessed | tf_op | source)
XLA Modules:
  0.0 215.3 jit_solution(7429971798723669601)
XLA Ops:
  3.2 3.3 %shard_map.101 = bf16[128,5376]{1,0:T(8,128)(2,1)} custom-call(bf16[3,128,16]{2,1,0:T(8,128)(2,1)} %fusion.7.sel_ref, bf16[16,1792]{1,0:T(8,128)(2,1)} %rows_ref.1), custom_call_target="tpu_custom_call" | custom-call | tf_op jit(solution)/shard_map/pallas_call | solution.py:252
  7.1 3.0 %reduce.8 = bf16[128,5376]{1,0:T(8,128)(2,1)S(1)} reduce(bf16[128,1,5376]{2,0,1:T(8,128)(2,1)} %bitcast.47, bf16[]{:T(256)} %broadcast.136), dimensions={1}, to_apply=%copy.71.reduce_sub_computation | reduce | bytes 2752514 | tf_op jit(solution)/shard_map/all_to_all | solution.py:255
  11.4 18.8 %all-to-all-start.1 = ((bf16[128,2,2688]{2,1,0:T(2,128)(2,1)}), bf16[128,2,2688]{2,1,0:T(2,128)(2,1)}, u32[]{:S(2)}, u32[]{:S(2)}) async-start(bf16[128,2,2688]{2,1,0:T(2,128)(2,1)} %reshape.117), calls=%async_computation.1 | async-start | bytes 2752512 | tf_op jit(solution)/shard_map/all_to_all | solution.py:255
  34.7 32.6 %collective-permute-done = bf16[2,64,640]{2,1,0:T(8,128)(2,1)S(1)} collective-permute-done((bf16[2,64,640]{2,1,0:T(8,128)(2,1)S(1)}, bf16[2,64,640]{2,1,0:T(8,128)(2,1)S(1)}, u32[]{:S(2)}, u32[]{:S(2)}) %collective-permute-start) | collective-permute-done | bytes 163872 | tf_op jit(solution)/shard_map/ppermute | solution.py:263
  67.3 1.3 collective-permute-done.2
  68.7 1.9 collective-permute-start.3
  70.6 2.1 collective-permute-done.3
  73.4 12.5 %conditional.4 = ((bf16[4,896,384]{2,1,0:T(8,128)(2,1)}, bf16[3,384,640]{2,1,0:T(8,128)(2,1)S(1)})) conditional(s32[]{:T(128)} %convert_element_type.59, bf16[1,1,2359296]{2,1,0:T(2,128)(2,1)} %param.16, (s32[9]{0:T(128)S(1)}, bf16[1,1,2359296]{2,1,0:T(2,128)(2,1)}, bf16[8,128,640]{2,1,0:T(8,128)(2,1)S(1)}) %tuple.37), branch_computations={%region_0.1_spmd, %region_1.2_spmd} | conditional | bytes 1474586 | solution.py:273
  73.4 12.3 %branch_1_fun.2 = bf16[4,896,384]{2,1,0:T(8,128)(2,1)} custom-call(s32[9]{0:T(128)S(1)} %get-tuple-element.56.info_ref, bf16[1,1,2359296]{2,1,0:T(2,128)(2,1)} %get-tuple-element.57.s_ref, bf16[8,128,640]{2,1,0:T(8,128)(2,1)S(1)} %get-tuple-element.58.q_ref), custom_call_target="tpu_custom_call" | custom-call | tf_op jit(solution)/shard_map/cond/branch_1_fun/pallas_call | solution.py:86
  87.0 4.0 %all-to-all-start = ((bf16[4,896,384]{2,1,0:T(8,128)(2,1)}), bf16[4,896,384]{2,1,0:T(8,128)(2,1)S(1)}, u32[]{:S(2)}, u32[]{:S(2)}) async-start(bf16[4,896,384]{2,1,0:T(8,128)(2,1)} %get-tuple-element.72), calls=%async_computation | async-start | bytes 5505024 | tf_op jit(solution)/shard_map/all_to_all | solution.py:274
  92.2 9.3 %reshape.118 = bf16[128,1,5376]{2,1,0:T(2,128)(2,1)} reshape(bf16[128,2,2688]{2,1,0:T(2,128)(2,1)} %all-to-all-done.1) | data formatting | bytes 2752512
  101.5 23.7 %all-to-all-done = bf16[4,896,384]{2,1,0:T(8,128)(2,1)S(1)} async-done(((bf16[4,896,384]{2,1,0:T(8,128)(2,1)}), bf16[4,896,384]{2,1,0:T(8,128)(2,1)S(1)}, u32[]{:S(2)}, u32[]{:S(2)}) %all-to-all-start) | async-done | bytes 2752544 | tf_op jit(solution)/shard_map/all_to_all | solution.py:274
  127.1 3.6 %all-to-all-start.2 = ((bf16[4,192,384]{2,1,0:T(8,128)(2,1)}), bf16[4,192,384]{2,1,0:T(8,128)(2,1)S(1)}, u32[]{:S(2)}, u32[]{:S(2)}) async-start(bf16[4,192,384]{2,1,0:T(8,128)(2,1)} %get-tuple-element.107), calls=%async_computation.2 | async-start | bytes 1179648 | tf_op jit(solution)/shard_map/all_to_all | solution.py:311
  132.7 1.4 collective-permute-start.10
  134.1 1.4 collective-permute-start.9
  135.6 6.2 %all-to-all-done.2 = bf16[4,192,384]{2,1,0:T(8,128)(2,1)S(1)} async-done(((bf16[4,192,384]{2,1,0:T(8,128)(2,1)}), bf16[4,192,384]{2,1,0:T(8,128)(2,1)S(1)}, u32[]{:S(2)}, u32[]{:S(2)}) %all-to-all-start.2) | async-done | bytes 589856 | tf_op jit(solution)/shard_map/all_to_all | solution.py:311
  143.3 10.0 %all-gather = bf16[12,96,384]{2,1,0:T(8,128)(2,1)S(1)} all-gather(bf16[3,96,384]{2,1,0:T(8,128)(2,1)S(1)} %pad_maximum_fusion.2), channel_id=2, replica_groups=mesh['sec'=128,'tp'=4] {'tp'}, dimensions={0}, use_global_device_ids=true | all-gather | bytes 1105920 | tf_op jit(solution)/shard_map/all_gather | solution.py:315
  155.7 34.2 %all-to-all-start.3 = ((bf16[128,2,960]{2,1,0:T(2,128)(2,1)}), bf16[128,2,960]{2,1,0:T(2,128)(2,1)S(1)}, u32[]{:S(2)}, u32[]{:S(2)}) async-start(bf16[128,2,960]{2,1,0:T(2,128)(2,1)} %reshape.119), calls=%async_computation.3 | async-start | bytes 1048576 | tf_op jit(solution)/shard_map/all_to_all | solution.py:319
  190.2 7.4 %collective-permute-start.4 = (bf16[64,640]{1,0:T(8,128)(2,1)S(1)}, bf16[64,640]{1,0:T(8,128)(2,1)S(1)}, u32[]{:S(2)}, u32[]{:S(2)}) collective-permute-start(bf16[64,640]{1,0:T(8,128)(2,1)S(1)} %get-tuple-element.91), channel_id=1, source_target_pairs={{0,128},{4,132},{8,136},{12,140},{16,144},{20,148},{24,152},{28,15... | collective-permute-start | bytes 245768 | tf_op jit(solution)/shard_map/ppermute | solution.py:297
  198.9 1.4 collective-permute-start.6
  200.9 2.6 %collective-permute-done.4 = bf16[64,640]{1,0:T(8,128)(2,1)S(1)} collective-permute-done((bf16[64,640]{1,0:T(8,128)(2,1)S(1)}, bf16[64,640]{1,0:T(8,128)(2,1)S(1)}, u32[]{:S(2)}, u32[]{:S(2)}) %collective-permute-start.4) | collective-permute-done | bytes 81952 | tf_op jit(solution)/shard_map/ppermute | solution.py:297
  203.5 2.4 %collective-permute-done.6 = bf16[64,640]{1,0:T(8,128)(2,1)S(1)} collective-permute-done((bf16[64,640]{1,0:T(8,128)(2,1)S(1)}, bf16[64,640]{1,0:T(8,128)(2,1)S(1)}, u32[]{:S(2)}, u32[]{:S(2)}) %collective-permute-start.6) | collective-permute-done | bytes 81952 | tf_op jit(solution)/shard_map/ppermute | solution.py:297
  206.8 5.0 %all-to-all-done.3 = bf16[128,2,960]{2,1,0:T(2,128)(2,1)S(1)} async-done(((bf16[128,2,960]{2,1,0:T(2,128)(2,1)}), bf16[128,2,960]{2,1,0:T(2,128)(2,1)S(1)}, u32[]{:S(2)}, u32[]{:S(2)}) %all-to-all-start.3) | async-done | bytes 491552 | tf_op jit(solution)/shard_map/all_to_all | solution.py:319
  213.4 1.9 shard_map.102
  (89 shorter events, 26.1 us)
Async XLA Ops:
  11.4 18.9 %copy-start.7 = (s32[2]{0:T(128)S(1)}, s32[2]{0:T(128)}, u32[]{:S(2)}) copy-start(s32[2]{0:T(128)} %param.19) | copy-start | bytes 28
  11.4 19.0 %copy-start.4 = (bf16[2,128,576]{1,2,0:T(8,128)(2,1)S(1)}, bf16[2,128,576]{1,2,0:T(8,128)(2,1)}, u32[]{:S(2)}) copy-start(bf16[2,128,576]{1,2,0:T(8,128)(2,1)} %param.17) | copy-start | bytes 884740
  11.4 74.5 %all-to-all-start.1 = ((bf16[128,2,2688]{2,1,0:T(2,128)(2,1)}), bf16[128,2,2688]{2,1,0:T(2,128)(2,1)}, u32[]{:S(2)}, u32[]{:S(2)}) async-start(bf16[128,2,2688]{2,1,0:T(2,128)(2,1)} %reshape.117), calls=%async_computation.1 | async-start | bytes 2752512 | tf_op jit(solution)/shard_map/all_to_all | solution.py:255
  30.8 36.5 %collective-permute-start = (bf16[2,64,640]{2,1,0:T(8,128)(2,1)S(1)}, bf16[2,64,640]{2,1,0:T(8,128)(2,1)S(1)}, u32[]{:S(2)}, u32[]{:S(2)}) collective-permute-start(bf16[2,64,640]{2,1,0:T(8,128)(2,1)S(1)} %fusion.2), channel_id=1, source_target_pairs={{128,0},{132,4},{136,8},{140,12},{144,16},{148,20},{152,24},{156,2... | collective-permute-start | bytes 491528 | tf_op jit(solution)/shard_map/ppermute | solution.py:263
  32.1 35.2 %collective-permute-start.1 = (bf16[2,64,640]{2,1,0:T(8,128)(2,1)S(1)}, bf16[2,64,640]{2,1,0:T(8,128)(2,1)S(1)}, u32[]{:S(2)}, u32[]{:S(2)}) collective-permute-start(bf16[2,64,640]{2,1,0:T(8,128)(2,1)S(1)} %fusion.2), channel_id=1, source_target_pairs={{256,0},{260,4},{264,8},{268,12},{272,16},{276,20},{280,24},{284,2... | collective-permute-start | bytes 491528 | tf_op jit(solution)/shard_map/ppermute | solution.py:263
  33.4 35.2 %collective-permute-start.2 = (bf16[2,64,640]{2,1,0:T(8,128)(2,1)S(1)}, bf16[2,64,640]{2,1,0:T(8,128)(2,1)S(1)}, u32[]{:S(2)}, u32[]{:S(2)}) collective-permute-start(bf16[2,64,640]{2,1,0:T(8,128)(2,1)S(1)} %fusion.2), channel_id=1, source_target_pairs={{384,0},{388,4},{392,8},{396,12},{400,16},{404,20},{408,24},{412,2... | collective-permute-start | bytes 491528 | tf_op jit(solution)/shard_map/ppermute | solution.py:263
  68.7 4.0 %collective-permute-start.3 = (bf16[8,64,640]{2,1,0:T(8,128)(2,1)S(1)}, bf16[8,64,640]{2,1,0:T(8,128)(2,1)S(1)}, u32[]{:S(2)}, u32[]{:S(2)}) collective-permute-start(bf16[8,64,640]{2,1,0:T(8,128)(2,1)S(1)} %pad_maximum_fusion.1), channel_id=1, source_target_pairs={{0,1},{1,0},{2,3},{3,2},{4,5},{5,4},{6,7},{7,6},{8,9},{9,8},{10,11... | collective-permute-start | bytes 1966088 | tf_op jit(solution)/shard_map/ppermute | solution.py:265
  85.9 1.1 copy-start.2
  85.9 5.1 %copy-start.6 = (f32[16,8]{0,1:T(8,128)S(1)}, f32[16,8]{0,1:T(8,128)}, u32[]{:S(2)}) copy-start(f32[16,8]{0,1:T(8,128)} %param.22) | copy-start | bytes 1540
  85.9 6.0 %copy-start.5 = (bf16[2,576]{1,0:T(2,128)(2,1)S(1)}, bf16[2,576]{1,0:T(2,128)(2,1)}, u32[]{:S(2)}) copy-start(bf16[2,576]{1,0:T(2,128)(2,1)} %param.18) | copy-start | bytes 6916
  87.0 38.2 %all-to-all-start = ((bf16[4,896,384]{2,1,0:T(8,128)(2,1)}), bf16[4,896,384]{2,1,0:T(8,128)(2,1)S(1)}, u32[]{:S(2)}, u32[]{:S(2)}) async-start(bf16[4,896,384]{2,1,0:T(8,128)(2,1)} %get-tuple-element.72), calls=%async_computation | async-start | bytes 5505024 | tf_op jit(solution)/shard_map/all_to_all | solution.py:274
  127.1 4.5 %copy-start.3 = (bf16[3,384,640]{2,1,0:T(8,128)(2,1)S(1)}, bf16[3,384,640]{2,1,0:T(8,128)(2,1)}, u32[]{:S(2)}) copy-start(bf16[3,384,640]{2,1,0:T(8,128)(2,1)} %copy-done.2) | copy-start | bytes 4423684
  127.1 14.6 %all-to-all-start.2 = ((bf16[4,192,384]{2,1,0:T(8,128)(2,1)}), bf16[4,192,384]{2,1,0:T(8,128)(2,1)S(1)}, u32[]{:S(2)}, u32[]{:S(2)}) async-start(bf16[4,192,384]{2,1,0:T(8,128)(2,1)} %get-tuple-element.107), calls=%async_computation.2 | async-start | bytes 1179648 | tf_op jit(solution)/shard_map/all_to_all | solution.py:311
  132.7 20.7 %collective-permute-start.10 = (bf16[384,640]{1,0:T(8,128)(2,1)}, bf16[384,640]{1,0:T(8,128)(2,1)}, u32[]{:S(2)}, u32[]{:S(2)}) collective-permute-start(bf16[384,640]{1,0:T(8,128)(2,1)} %get-tuple-element.87), channel_id=1, source_target_pairs={{128,136},{132,128},{136,132},{140,148},{144,140},{148,144},{152,1... | collective-permute-start | bytes 1474568 | tf_op jit(solution)/shard_map/ppermute | solution.py:277
  134.1 19.3 %collective-permute-start.9 = (bf16[384,640]{1,0:T(8,128)(2,1)}, bf16[384,640]{1,0:T(8,128)(2,1)}, u32[]{:S(2)}, u32[]{:S(2)}) collective-permute-start(bf16[384,640]{1,0:T(8,128)(2,1)} %get-tuple-element.88), channel_id=1, source_target_pairs={{128,132},{132,136},{136,128},{140,144},{144,148},{148,140},{152,1... | collective-permute-start | bytes 1474568 | tf_op jit(solution)/shard_map/ppermute | solution.py:277
  141.8 1.4 collective-permute-start.7
  142.5 0.7 collective-permute-start.8
  155.7 56.1 %all-to-all-start.3 = ((bf16[128,2,960]{2,1,0:T(2,128)(2,1)}), bf16[128,2,960]{2,1,0:T(2,128)(2,1)S(1)}, u32[]{:S(2)}, u32[]{:S(2)}) async-start(bf16[128,2,960]{2,1,0:T(2,128)(2,1)} %reshape.119), calls=%async_computation.3 | async-start | bytes 1048576 | tf_op jit(solution)/shard_map/all_to_all | solution.py:319
  190.2 13.3 %collective-permute-start.4 = (bf16[64,640]{1,0:T(8,128)(2,1)S(1)}, bf16[64,640]{1,0:T(8,128)(2,1)S(1)}, u32[]{:S(2)}, u32[]{:S(2)}) collective-permute-start(bf16[64,640]{1,0:T(8,128)(2,1)S(1)} %get-tuple-element.91), channel_id=1, source_target_pairs={{0,128},{4,132},{8,136},{12,140},{16,144},{20,148},{24,152},{28,15... | collective-permute-start | bytes 245768 | tf_op jit(solution)/shard_map/ppermute | solution.py:297
  197.6 5.9 %collective-permute-start.5 = (bf16[64,640]{1,0:T(8,128)(2,1)S(1)}, bf16[64,640]{1,0:T(8,128)(2,1)S(1)}, u32[]{:S(2)}, u32[]{:S(2)}) collective-permute-start(bf16[64,640]{1,0:T(8,128)(2,1)S(1)} %get-tuple-element.93), channel_id=1, source_target_pairs={{0,256},{4,260},{8,264},{12,268},{16,272},{20,276},{24,280},{28,28... | collective-permute-start | bytes 245768 | tf_op jit(solution)/shard_map/ppermute | solution.py:297
  198.9 7.0 %collective-permute-start.6 = (bf16[64,640]{1,0:T(8,128)(2,1)S(1)}, bf16[64,640]{1,0:T(8,128)(2,1)S(1)}, u32[]{:S(2)}, u32[]{:S(2)}) collective-permute-start(bf16[64,640]{1,0:T(8,128)(2,1)S(1)} %get-tuple-element.92), channel_id=1, source_target_pairs={{0,384},{4,388},{8,392},{12,396},{16,400},{20,404},{24,408},{28,41... | collective-permute-start | bytes 245768 | tf_op jit(solution)/shard_map/ppermute | solution.py:297

commit v2 on v1

v2 whole, which is shorter than its diff:
```python
import functools
import math

import jax
import jax.numpy as jnp
from jax import lax
from jax.experimental import pallas as pl
from jax.experimental.pallas import tpu as pltpu
from jax.sharding import PartitionSpec as P

LATENT = 512
KV = 576
LP = 512
CAP = 3
HD = 96
DQ = 1792
PART = 640
f32 = jnp.float32
bf16 = jnp.bfloat16
VM = 48 << 20

softmax_scale = 1.0 / math.sqrt(192.0)


def dot(a, b, dims=((1,), (0,))):
    return lax.dot_general(a, b, (dims, ((), ())), preferred_element_type=f32)


def pieces(value):
    high = value.astype(bf16).astype(f32)
    middle = (value - high).astype(bf16).astype(f32)
    return high, middle, value - high - middle


def flat_rows(s_ref, scr):
    scr[...] = s_ref[...].astype(f32).reshape(scr.shape)


def dispatch_kernel(sel_ref, rows_ref, out_ref, scr):
    source = lax.broadcasted_iota(jnp.int32, (256, 256), 0)
    target = lax.broadcasted_iota(jnp.int32, (256, 256), 1)
    order = (source == 4 * (target % 64) + target // 64).astype(f32).astype(bf16)
    count = out_ref.shape[0]
    for b in range(DQ // 256):
        turned = dot(rows_ref[:, 256 * b : 256 * b + 256], order).astype(bf16)
        for c in range(CAP):
            sent = dot(sel_ref[c], turned)
            for k in range(2):
                scr[pl.ds(16 * c + 2 * b + k, count, stride=48), :] = sent[:, 128 * k : 128 * k + 128]
    for c in range(CAP):
        for k in range(14, 16):
            scr[pl.ds(16 * c + k, count, stride=48), :] = jnp.zeros((count, 128), f32)
    out_ref[...] = scr[...].astype(bf16).reshape(out_ref.shape)


def dispatch(sel, rows):
    groups = sel.shape[1]
    return pl.pallas_call(
        dispatch_kernel,
        out_shape=jax.ShapeDtypeStruct((groups, 48, 128), bf16),
        scratch_shapes=[pltpu.VMEM((groups * 48, 128), f32)],
        compiler_params=pltpu.CompilerParams(vmem_limit_bytes=VM),
    )(sel, rows)


def attend_kernel(info_ref, s_ref, q_ref, *refs):
    p_refs, (scr, keys, found) = refs[:4], refs[4:]
    row = pl.program_id(0)
    flat_rows(s_ref, scr)
    for m in range(9):
        keys[:, 128 * m : 128 * m + 128] = scr[pl.ds(m, LP // 2, stride=9), :].astype(bf16)
    lane = lax.broadcasted_iota(jnp.int32, (128, PART), 1)
    even_q = jnp.where(lane < KV, q_ref[0].astype(f32), 0.0)
    odd_q = pltpu.roll(even_q, 64, 1).astype(bf16)
    even_q = even_q.astype(bf16)
    even = dot(even_q, keys[:, :640], ((1,), (1,))) * softmax_scale
    odd = dot(odd_q, keys[:, 512:], ((1,), (1,))) * softmax_scale
    left = info_ref[row] - info_ref[8]
    position = 2 * lax.broadcasted_iota(jnp.int32, (128, LP // 2), 1)
    even = jnp.where(position < left, even, -1e30)
    odd = jnp.where(position + 1 < left, odd, -1e30)
    top = jnp.maximum(jnp.max(even, axis=1, keepdims=True), jnp.max(odd, axis=1, keepdims=True))
    even = jnp.where(position < left, jnp.exp(even - top), 0.0).astype(bf16)
    odd = jnp.where(position + 1 < left, jnp.exp(odd - top), 0.0).astype(bf16)
    total = jnp.sum(even.astype(f32), axis=1, keepdims=True) + jnp.sum(odd.astype(f32), axis=1, keepdims=True)
    summed = dot(even, keys[:, :LATENT]) + dot(odd, keys[:, 512:])[:, 64 : 64 + LATENT]
    lane = lax.broadcasted_iota(jnp.int32, (128, 128), 1)
    stats = jnp.zeros((128, 128), f32)
    for at, piece in enumerate(pieces(top) + pieces(total)):
        stats = jnp.where(lane == at, piece, stats)
    found[:, :LATENT] = summed.astype(bf16)
    found[:, LATENT:] = stats.astype(bf16)
    span = pl.ds(pl.multiple_of(row * 32, 32), 32)
    for d, p_ref in enumerate(p_refs):
        share = pl.multiple_of(jnp.bitwise_xor(info_ref[9], d) * 32, 32)
        p_ref[span, :] = found[pl.ds(share, 32), :]


def attend(store, asked, info):
    shape = (256, PART)
    return pl.pallas_call(
        attend_kernel,
        grid_spec=pltpu.PrefetchScalarGridSpec(
            num_scalar_prefetch=1,
            grid=(8,),
            in_specs=[
                pl.BlockSpec((1, 1, LP * KV), lambda i, info: (0, 0, i)),
                pl.BlockSpec((1, 128, PART), lambda i, info: (i, 0, 0)),
            ],
            out_specs=[pl.BlockSpec(shape, lambda i, info: (0, 0))] * 4,
            scratch_shapes=[
                pltpu.VMEM((LP * KV // 128, 128), f32),
                pltpu.VMEM((LP // 2, 2 * KV), bf16),
                pltpu.VMEM((128, PART), bf16),
            ],
        ),
        out_shape=[jax.ShapeDtypeStruct(shape, bf16)] * 4,
        compiler_params=pltpu.CompilerParams(vmem_limit_bytes=VM),
    )(info, store, asked)


def unpack_kernel(tp_ref, s_ref, p0_ref, p1_ref, p2_ref, p3_ref, w_ref, scr):
    step = pl.program_id(0)
    flat_rows(s_ref, scr)
    for d, p_ref in enumerate((p0_ref, p1_ref, p2_ref, p3_ref)):

        @pl.when(step // 2 == d)
        def _():
            for m in range(3):
                p_ref[:, 128 * m : 128 * m + 128] = scr[pl.ds(m, 448, stride=3), :].astype(bf16)

    @pl.when(step >= 8)
    def _():
        for m in range(14):
            at = 128 * (m % 5)
            w_ref[m // 5, :, at : at + 128] = scr[pl.ds(m, HD, stride=14), :].astype(bf16)
        w_ref[2, :, 512:640] = jnp.zeros((HD, 128), bf16)


def unpack(store, part):
    def block(i, tp):
        return 0, 0, jnp.where(i < 8, jnp.bitwise_xor(i // 2, tp[0]) + 4 * (i % 2), i)

    def piece(d):
        return pl.BlockSpec((448, 384), lambda i, tp: (jnp.clip(i - 2 * d, 0, 1), 0))

    return pl.pallas_call(
        unpack_kernel,
        grid_spec=pltpu.PrefetchScalarGridSpec(
            num_scalar_prefetch=1,
            grid=(12,),
            in_specs=[pl.BlockSpec((1, 1, DQ * HD), block)],
            out_specs=[piece(d) for d in range(4)]
            + [pl.BlockSpec((3, HD, PART), lambda i, tp: (0, jnp.maximum(i - 8, 0), 0))],
            scratch_shapes=[pltpu.VMEM((DQ * HD // 128, 128), f32)],
        ),
        out_shape=[jax.ShapeDtypeStruct((896, 384), bf16)] * 4 + [jax.ShapeDtypeStruct((3, 384, PART), bf16)],
        compiler_params=pltpu.CompilerParams(vmem_limit_bytes=VM),
    )(part.reshape(1).astype(jnp.int32), store)


def weights_kernel(p0_ref, p1_ref, p2_ref, p3_ref, w_ref):
    for half in range(2):
        for r in range(4):
            span = slice(HD * r, HD * r + HD)
            rows = slice(448 * half, 448 * half + 448)
            found = jnp.concatenate([p_ref[rows, span] for p_ref in (p0_ref, p1_ref, p2_ref, p3_ref)], axis=1)
            for b in range(7):
                w_ref[half, 256 * b + 64 * r : 256 * b + 64 * r + 64, :] = found[64 * b : 64 * b + 64]


def arrange(quarters):
    return pl.pallas_call(
        weights_kernel,
        out_shape=jax.ShapeDtypeStruct((2, DQ, 384), bf16),
        compiler_params=pltpu.CompilerParams(vmem_limit_bytes=VM),
    )(*quarters)


def join_kernel(p0_ref, p1_ref, p2_ref, p3_ref, out_ref):
    refs = (p0_ref, p1_ref, p2_ref, p3_ref)
    tops, totals = [], []
    for p_ref in refs:
        stats = p_ref[:, LATENT:].astype(f32)
        tops.append(stats[:, 0:1] + stats[:, 1:2] + stats[:, 2:3])
        totals.append(stats[:, 3:4] + stats[:, 4:5] + stats[:, 5:6])
    top = functools.reduce(jnp.maximum, tops)
    scales = [jnp.exp(own - top) for own in tops]
    total = sum(scale * own for scale, own in zip(scales, totals))
    scales = [scale / total for scale in scales]
    out_ref[:, :LATENT] = sum(
        scale * p_ref[:, :LATENT].astype(f32) for scale, p_ref in zip(scales, refs)
    ).astype(bf16)
    lane = lax.broadcasted_iota(jnp.int32, (256, 128), 1)
    stats = jnp.zeros((256, 128), f32)
    for at, piece in enumerate(pieces(top + jnp.log(total))):
        stats = jnp.where(lane == at, piece, stats)
    out_ref[:, LATENT:] = stats.astype(bf16)


def join(parts):
    return pl.pallas_call(
        join_kernel,
        out_shape=jax.ShapeDtypeStruct((256, PART), bf16),
        compiler_params=pltpu.CompilerParams(vmem_limit_bytes=VM),
    )(*parts)


def project_kernel(tp_ref, x_ref, w_ref, z_ref, scr, slab):
    count = x_ref.shape[0]
    scr[...] = x_ref[...].astype(f32).reshape(scr.shape)
    for c in range(CAP):
        for k in range(14):
            slab[:, 128 * k : 128 * k + 128] = scr[pl.ds(16 * c + k, count, stride=48), :].astype(bf16)
        for half in range(2):
            turned = dot(slab[...], w_ref[half]).T.astype(bf16)
            for d in range(4):
                z_ref[jnp.bitwise_xor(tp_ref[0], d), HD * half : HD * half + HD, 128 * c : 128 * c + 128] = turned[
                    HD * d : HD * d + HD
                ]


def project(part, arrived, weights):
    count = arrived.shape[0]
    return pl.pallas_call(
        project_kernel,
        in_specs=[pl.BlockSpec(memory_space=pltpu.SMEM)] + [pl.BlockSpec(memory_space=pltpu.VMEM)] * 2,
        out_shape=jax.ShapeDtypeStruct((4, 2 * HD, CAP * count), bf16),
        scratch_shapes=[pltpu.VMEM((count * 48, 128), f32), pltpu.VMEM((count, DQ), bf16)],
        compiler_params=pltpu.CompilerParams(vmem_limit_bytes=VM),
    )(part.reshape(1).astype(jnp.int32), arrived, weights)


def descend_kernel(h_ref, w0_ref, w1_ref, w2_ref, out_ref, scr, turned):
    count = out_ref.shape[0]
    result = jnp.zeros((CAP * count, PART), f32)
    for d, w_ref in enumerate((w0_ref, w1_ref, w2_ref)):
        for t in range(4):
            scr[HD * t : HD * t + HD, :] = h_ref[t, d]
        result = result + dot(scr[...], w_ref[...], ((0,), (0,)))
    for c in range(CAP):
        for m in range(5):
            turned[pl.ds(5 * c + m, count, stride=16), :] = result[count * c : count * c + count, 128 * m : 128 * m + 128]
    turned[pl.ds(15, count, stride=16), :] = jnp.zeros((count, 128), f32)
    out_ref[...] = turned[...].astype(bf16).reshape(out_ref.shape)


def descend(hidden, downs):
    count = hidden.shape[3] // CAP
    return pl.pallas_call(
        descend_kernel,
        out_shape=jax.ShapeDtypeStruct((count, 16, 128), bf16),
        scratch_shapes=[pltpu.VMEM((4 * HD, CAP * count), bf16), pltpu.VMEM((count * 16, 128), f32)],
        compiler_params=pltpu.CompilerParams(vmem_limit_bytes=VM),
    )(hidden, *downs)


def combine_kernel(a_ref, x_ref, out_ref, scr):
    count = x_ref.shape[0]
    scr[...] = x_ref[...].astype(f32).reshape(scr.shape)
    for m in range(5):
        result = jnp.zeros((96, 128), f32)
        for c in range(CAP):
            result = result + dot(a_ref[c], scr[pl.ds(5 * c + m, count, stride=16), :].astype(bf16))
        result = (result[:48] + result[48:]).astype(bf16)
        for j in range(3 if m < 4 else 2):
            at = 640 * j + 128 * m
            out_ref[:, at : at + 128] = result[16 * j : 16 * j + 16]


def combine(weight, result):
    return pl.pallas_call(
        combine_kernel,
        out_shape=jax.ShapeDtypeStruct((16, DQ), bf16),
        scratch_shapes=[pltpu.VMEM((result.shape[0] * 16, 128), f32)],
        compiler_params=pltpu.CompilerParams(vmem_limit_bytes=VM),
    )(weight, result)


def per_device(store, queries, new_latent, cached_len, rows, expert_ids, route_gates, capacity):
    groups = lax.axis_size("sec")
    servers = groups // 4
    place = lax.axis_index("sec")
    part = lax.axis_index("tp")
    serving = place < servers
    both = ("sec", "tp")
    core = part % 2

    experts = capacity.shape[1]
    labels = jnp.arange(experts, dtype=jnp.int32)
    match = expert_ids[:, :, None] == labels[None, None, :]
    hits = jnp.any(match, axis=1).astype(jnp.int32)
    gate_of = jnp.sum(jnp.where(match, route_gates[:, :, None], 0.0), axis=1)
    rank = jnp.cumsum(hits, axis=0) - hits
    keep = (hits == 1) & (rank < capacity[0][None, :])
    slots = jnp.arange(CAP, dtype=jnp.int32)
    pick = (keep[None] & (rank[None] == slots[:, None, None])).astype(f32)
    spread = jnp.pad(jnp.repeat(pick, 3, axis=2), ((0, 0), (0, 0), (servers, 0)))
    sel = jnp.swapaxes(spread, 1, 2).astype(bf16)
    outgoing = dispatch(sel, rows)
    arrived = lax.all_to_all(outgoing, "sec", split_axis=0, concat_axis=0, tiled=True)

    def across(value, d, first, last):
        return lax.ppermute(value, both, [(4 * q + t, 4 * q + (t ^ d)) for q in range(first, last) for t in range(4)])

    def sibling(value, step):
        return lax.ppermute(
            value,
            "sec",
            [(servers + 3 * e + j, servers + 3 * e + (j + step) % 3) for e in range(experts) for j in range(3)],
        )

    *quarters, down = unpack(store, part)
    quarters = [quarters[0]] + [across(quarters[d], d, servers, groups) for d in range(1, 4)]
    third = (place - servers) % 3
    downs = [lax.dynamic_index_in_dim(down, third, 0, keepdims=False)]
    for step in (1, 2):
        downs.append(sibling(lax.dynamic_index_in_dim(down, (third + step) % 3, 0, keepdims=False), step))
    weights = arrange(quarters)

    digits = jnp.stack([cached_len // 64, cached_len % 64], axis=1).astype(bf16)
    digits = jnp.pad(digits, ((0, 0), (0, PART - KV - 2)))
    asked = jnp.concatenate([queries, jnp.broadcast_to(digits[:, None, :], (2, 128, PART - KV))], axis=2)
    half = lax.dynamic_slice_in_dim(asked, core * 64, 64, 1)
    incoming = [half]
    for k in range(1, 4):
        incoming.append(lax.ppermute(half, "sec", [(k * servers + a, a) for a in range(servers)]))
    half = jnp.concatenate(incoming, axis=0)
    other = across(half, 1, 0, servers)
    asked = jnp.concatenate([jnp.where(core == 0, half, other), jnp.where(core == 0, other, half)], axis=1)
    lengths = asked[:, 0, KV].astype(jnp.int32) * 64 + asked[:, 0, KV + 1].astype(jnp.int32)
    info = jnp.concatenate([lengths, jnp.stack([part * LP, part]).astype(jnp.int32)])

    parts = lax.cond(
        serving, lambda: tuple(attend(store, asked, info)), lambda: (jnp.zeros((256, PART), bf16),) * 4
    )
    parts = [parts[0]] + [across(parts[d], d, 0, servers) for d in range(1, 4)]
    answer = lax.cond(serving, lambda: join(parts), lambda: jnp.zeros((256, PART), bf16))

    answer = answer.reshape(4, 64, PART)
    returned = answer[0]
    for k in range(1, 4):
        returned = returned + lax.ppermute(answer[k], "sec", [(a, k * servers + a) for a in range(servers)])
    mine = lax.dynamic_slice_in_dim(queries, part * 32, 32, 1)
    own = jnp.einsum("rhk,rk->rh", mine, new_latent, preferred_element_type=f32) * softmax_scale
    own = own[:, :, None]
    returned = returned.reshape(2, 32, PART).astype(f32)
    others = returned[:, :, 512:513] + returned[:, :, 513:514] + returned[:, :, 514:515]
    top = jnp.maximum(own, others)
    own, others = jnp.exp(own - top), jnp.exp(others - top)
    attended = (others * returned[:, :, :LATENT] + own * new_latent[:, None, :LATENT].astype(f32)) / (own + others)
    attended = attended.astype(bf16)

    partial = project(part, arrived, weights)
    partial = lax.all_to_all(partial, "tp", split_axis=0, concat_axis=0, tiled=True)
    partial = jnp.sum(partial.astype(f32), axis=0)
    hidden = (jax.nn.silu(partial[:HD]) * partial[HD:]).astype(bf16)
    hidden = jnp.stack([hidden, sibling(hidden, 1), sibling(hidden, 2)])
    hidden = lax.all_gather(hidden, "tp", axis=0)
    result = descend(hidden, downs)
    result = lax.all_to_all(result, "sec", split_axis=0, concat_axis=0, tiled=True)

    scaled = spread * jnp.pad(jnp.repeat(gate_of, 3, axis=1), ((0, 0), (servers, 0)))[None]
    holder = (jnp.arange(groups) - servers) % 3
    scaled = jnp.where(holder == jnp.arange(3)[:, None, None, None], scaled[None], 0.0)
    scaled = jnp.swapaxes(scaled, 0, 1).reshape(CAP, 48, groups)
    high = lax.reduce_precision(scaled, 8, 7)
    weight = jnp.concatenate([high, scaled - high], axis=1).astype(bf16)
    mixed = combine(weight, result)
    return (attended, mixed)


def solution(mesh):
    placed = (
        P("sec", "tp", None),
        P("sec", None, None),
        P("sec", None),
        P("sec"),
        P("sec", "tp"),
        P("sec", None),
        P("sec", None),
        P("sec", None),
    )
    return jax.shard_map(
        per_device,
        mesh=mesh,
        in_specs=placed,
        out_specs=(P("sec", "tp", None), P("sec", "tp")),
        check_vma=False,
    )
```

time: 217 us -> 179 us (0.82)
  the two profiles are of different devices: /device:TPU:8 before, /device:TPU:4 now
where the time goes in v2:
time: 179 us; the launch traced here: 177 us
  starting transfers between devices  69.3 us (39%)
  Pallas kernels  36.6 us (20%)
  waiting for transfers between devices  34.3 us (19%)
  blocking collectives  22.1 us (12%)
  other arithmetic  6.89 us (4%)
  local copies, waits for them, and re-layouts  6.69 us (4%)
    ppermute x3, waiting for transfers between devices, per_device(): lax.ppermute(half, 'sec', [(k * servers + a, a) for a in range(servers)])  23.7 us
    all_gather x1, blocking collectives, per_device(): hidden = lax.all_gather(hidden, 'tp', axis=0)  22.1 us
    all_to_all x1, starting transfers between devices, per_device(): lax.all_to_all(outgoing, 'sec', split_axis=0, concat_axis=0, tiled=True)  19 us
    all_to_all x1, starting transfers between devices, per_device(): lax.all_to_all(result, 'sec', split_axis=0, concat_axis=0, tiled=True)  14.3 us
    ppermute x7, starting transfers between devices, across(): lax.ppermute(value, both, [(4 * q + t, 4 * q + (t ^ d)) for q in range(fi...  13.9 us
    pallas_call x1, Pallas kernels, attend(): pl.pallas_call(attend_kernel, grid_spec=pltpu.PrefetchScalarGridSpec(num_...  11.5 us
    pallas_call x1, Pallas kernels, unpack(): pl.pallas_call(unpack_kernel, grid_spec=pltpu.PrefetchScalarGridSpec(num_...  9.95 us
    ppermute x3, starting transfers between devices, per_device(): lax.ppermute(answer[k], 'sec', [(a, k * servers + a) for a in range(serve...  9.01 us
  transfers between devices with their start and end apart: 20, of which 5 were waited for; matrix products, arithmetic and copies ran while one was open for 5% of the time, Pallas kernels for 18%

profile of v2, /device:TPU:4, one launch (start us, length us, event | category | flops | bytes accessed | tf_op | source)
XLA Modules:
  0.0 177.4 jit_solution(12516930612039270017)
XLA Ops:
  3.4 3.1 %shard_map.98 = bf16[128,48,128]{2,1,0:T(8,128)(2,1)} custom-call(bf16[3,128,16]{2,1,0:T(8,128)(2,1)S(1)} %fusion.7.sel_ref, bf16[16,1792]{1,0:T(8,128)(2,1)S(1)} %copy-done.4), custom_call_target="tpu_custom_call" | custom-call | tf_op jit(solution)/shard_map/pallas_call | solution.py:58
  6.5 19.0 %all-to-all-start = ((bf16[128,48,128]{2,1,0:T(8,128)(2,1)}), bf16[128,48,128]{2,1,0:T(8,128)(2,1)}, u32[]{:S(2)}, u32[]{:S(2)}) async-start(bf16[128,48,128]{2,1,0:T(8,128)(2,1)} %shard_map.98), calls=%async_computation | async-start | bytes 3145728 | tf_op jit(solution)/shard_map/all_to_all | solution.py:301
  30.0 10.0 %shard_map.99 = (bf16[896,384]{1,0:T(8,128)(2,1)S(1)}, bf16[896,384]{1,0:T(8,128)(2,1)}, bf16[896,384]{1,0:T(8,128)(2,1)}, bf16[896,384]{1,0:T(8,128)(2,1)S(1)}, bf16[3,384,640]{2,1,0:T(8,128)(2,1)S(1)}) custom-call(s32[1]{0:T(128)} %bitcast.3.tp_ref, bf16[1,1,2359296]{2,1,0:T(2,128)(2,1)} %s_ref.1), custom_call_target="tpu_custom_call" | custom-call | tf_op jit(solution)/shard_map/pallas_call | solution.py:147
  41.5 1.5 collective-permute-start.11
  44.9 21.8 %collective-permute-done = bf16[2,64,640]{2,1,0:T(8,128)(2,1)} collective-permute-done((bf16[2,64,640]{2,1,0:T(8,128)(2,1)S(1)}, bf16[2,64,640]{2,1,0:T(8,128)(2,1)}, u32[]{:S(2)}, u32[]{:S(2)}) %collective-permute-start) | collective-permute-done | bytes 163872 | tf_op jit(solution)/shard_map/ppermute | solution.py:327
  68.9 1.9 %collective-permute-done.2 = bf16[2,64,640]{2,1,0:T(8,128)(2,1)} collective-permute-done((bf16[2,64,640]{2,1,0:T(8,128)(2,1)S(1)}, bf16[2,64,640]{2,1,0:T(8,128)(2,1)}, u32[]{:S(2)}, u32[]{:S(2)}) %collective-permute-start.2) | collective-permute-done | bytes 163872 | tf_op jit(solution)/shard_map/ppermute | solution.py:327
  70.8 2.0 %pad_maximum_fusion.1 = bf16[8,64,640]{2,1,0:T(8,128)(2,1)} fusion(bf16[2,64,640]{2,1,0:T(8,128)(2,1)} %collective-permute-done.2, bf16[2,64,640]{2,1,0:T(8,128)(2,1)} %collective-permute-done.1, bf16[2,64,640]{2,1,0:T(8,128)(2,1)} %collective-permute-done, bf16[2,64,640]{2,1,0:T(8,128)(2,1)S(1)} %fusion.2), kind=kLoop, calls=%fused_computation.2 | loop fusion | flops 983040 | bytes 1310720 | tf_op jit(solution)/shard_map/concatenate | solution.py:328
  72.8 1.9 %collective-permute-start.3 = (bf16[8,64,640]{2,1,0:T(8,128)(2,1)}, bf16[8,64,640]{2,1,0:T(8,128)(2,1)}, u32[]{:S(2)}, u32[]{:S(2)}) collective-permute-start(bf16[8,64,640]{2,1,0:T(8,128)(2,1)} %pad_maximum_fusion.1), channel_id=1, source_target_pairs={{0,1},{1,0},{2,3},{3,2},{4,5},{5,4},{6,7},{7,6},{8,9},{9,8},{10,11... | collective-permute-start | bytes 1966088 | tf_op jit(solution)/shard_map/ppermute | solution.py:304
  76.3 1.5 collective-permute-start.16
  78.9 2.2 %shard_map.100.w_ref = bf16[2,1792,384]{2,1,0:T(8,128)(2,1)S(1)} custom-call(bf16[896,384]{1,0:T(8,128)(2,1)S(1)} %copy-done.1, bf16[896,384]{1,0:T(8,128)(2,1)S(1)} %copy-done.3, bf16[896,384]{1,0:T(8,128)(2,1)} %collective-permute-done.11.p2_ref, bf16[896,384]{1,0:T(8,128)(2,1)S(1)} %collective-permute-done.12.p3_ref), custom_call_target="tpu_custom_call" | custom-call | tf_op jit(solution)/shard_map/pallas_call | solution.py:173
  81.1 4.6 %shard_map.101 = bf16[4,192,384]{2,1,0:T(8,128)(2,1)} custom-call(s32[1]{0:T(128)} %bitcast.3.tp_ref, bf16[128,48,128]{2,1,0:T(8,128)(2,1)} %all-to-all-done.x_ref, bf16[2,1792,384]{2,1,0:T(8,128)(2,1)S(1)} %shard_map.100.w_ref), custom_call_target="tpu_custom_call" | custom-call | tf_op jit(solution)/shard_map/pallas_call | solution.py:225
  85.8 4.9 %all-to-all-start.1 = ((bf16[4,192,384]{2,1,0:T(8,128)(2,1)}), bf16[4,192,384]{2,1,0:T(8,128)(2,1)S(1)}, u32[]{:S(2)}, u32[]{:S(2)}) async-start(bf16[4,192,384]{2,1,0:T(8,128)(2,1)} %shard_map.101), calls=%async_computation.1 | async-start | bytes 1179648 | tf_op jit(solution)/shard_map/all_to_all | solution.py:355
  92.6 11.6 %conditional.2 = ((bf16[256,640]{1,0:T(8,128)(2,1)S(1)}, bf16[256,640]{1,0:T(8,128)(2,1)S(1)}, bf16[256,640]{1,0:T(8,128)(2,1)S(1)}, bf16[256,640]{1,0:T(8,128)(2,1)})) conditional(s32[]{:T(128)} %convert_element_type.57, () %tuple.22, (s32[10]{0:T(128)S(1)}, bf16[1,1,2359296]{2,1,0:T(2,128)(2,1)}, bf16[8,128,640]{2,1,0:T(8,128)(2,1)S(1)}) %tuple.23), branch_computations={%region_0.1_spmd, %region_1.2_spmd} | conditional | bytes 1310768 | solution.py:334
  92.6 11.5 %branch_1_fun.2 = (bf16[256,640]{1,0:T(8,128)(2,1)S(1)}, bf16[256,640]{1,0:T(8,128)(2,1)S(1)}, bf16[256,640]{1,0:T(8,128)(2,1)S(1)}, bf16[256,640]{1,0:T(8,128)(2,1)}) custom-call(s32[10]{0:T(128)S(1)} %get-tuple-element.9.info_ref, bf16[1,1,2359296]{2,1,0:T(2,128)(2,1)} %get-tuple-element.18.s_ref, bf16[8,128,640]{2,1,0:T(8,128)(2,1)S(1)} %get-tuple-element.19.q_ref), custom_call_target="tpu_custom_call" | custom-call | tf_op jit(solution)/shard_map/cond/branch_1_fun/pallas_call | solution.py:101
  104.2 2.1 %collective-permute-start.4 = (bf16[256,640]{1,0:T(8,128)(2,1)S(1)}, bf16[256,640]{1,0:T(8,128)(2,1)S(1)}, u32[]{:S(2)}, u32[]{:S(2)}) collective-permute-start(bf16[256,640]{1,0:T(8,128)(2,1)S(1)} %get-tuple-element.36), channel_id=1, source_target_pairs={{0,1},{1,0},{2,3},{3,2},{4,5},{5,4},{6,7},{7,6},{8,9},{9,8},{10,11... | collective-permute-start | bytes 983048 | tf_op jit(solution)/shard_map/ppermute | solution.py:304
  107.8 2.3 %collective-permute-start.5 = (bf16[256,640]{1,0:T(8,128)(2,1)S(1)}, bf16[256,640]{1,0:T(8,128)(2,1)S(1)}, u32[]{:S(2)}, u32[]{:S(2)}) collective-permute-start(bf16[256,640]{1,0:T(8,128)(2,1)S(1)} %get-tuple-element.37), channel_id=1, source_target_pairs={{0,2},{1,3},{2,0},{3,1},{4,6},{5,7},{6,4},{7,5},{8,10},{9,11},{10,... | collective-permute-start | bytes 983048 | tf_op jit(solution)/shard_map/ppermute | solution.py:304
  110.1 4.8 %collective-permute-start.6 = (bf16[256,640]{1,0:T(8,128)(2,1)}, bf16[256,640]{1,0:T(8,128)(2,1)S(1)}, u32[]{:S(2)}, u32[]{:S(2)}) collective-permute-start(bf16[256,640]{1,0:T(8,128)(2,1)} %get-tuple-element.38), channel_id=1, source_target_pairs={{0,3},{1,2},{2,1},{3,0},{4,7},{5,6},{6,5},{7,4},{8,11},{9,10},{10,... | collective-permute-start | bytes 983048 | tf_op jit(solution)/shard_map/ppermute | solution.py:304
  114.9 22.1 %all-gather = bf16[12,96,384]{2,1,0:T(8,128)(2,1)S(1)} all-gather(bf16[3,96,384]{2,1,0:T(8,128)(2,1)S(1)} %pad_maximum_fusion.2), channel_id=2, replica_groups=mesh['sec'=128,'tp'=4] {'tp'}, dimensions={0}, use_global_device_ids=true | all-gather | bytes 1105920 | tf_op jit(solution)/shard_map/all_gather | solution.py:359
  137.0 3.3 %shard_map.102 = bf16[128,16,128]{2,1,0:T(8,128)(2,1)} custom-call(bf16[4,3,96,384]{3,2,1,0:T(8,128)(2,1)S(1)} %bitcast.39, bf16[384,640]{1,0:T(8,128)(2,1)S(1)} %get-tuple-element.51.w0_ref, bf16[384,640]{1,0:T(8,128)(2,1)} %collective-permute-done.15.w1_ref, bf16[384,640]{1,0:T(8,128)(2,1)} %collective-permute-done.16.w2_ref), custom_call_target="tpu_custom_call" | custom-call | tf_op jit(solution)/shard_map/pallas_call | solution.py:250
  140.3 14.3 %all-to-all-start.2 = ((bf16[128,16,128]{2,1,0:T(8,128)(2,1)}), bf16[128,16,128]{2,1,0:T(8,128)(2,1)S(1)}, u32[]{:S(2)}, u32[]{:S(2)}) async-start(bf16[128,16,128]{2,1,0:T(8,128)(2,1)} %shard_map.102), calls=%async_computation.2 | async-start | bytes 1048576 | tf_op jit(solution)/shard_map/all_to_all | solution.py:361
  155.7 6.3 %collective-permute-start.7 = (bf16[64,640]{1,0:T(8,128)(2,1)S(1)}, bf16[64,640]{1,0:T(8,128)(2,1)S(1)}, u32[]{:S(2)}, u32[]{:S(2)}) collective-permute-start(bf16[64,640]{1,0:T(8,128)(2,1)S(1)} %get-tuple-element.54), channel_id=1, source_target_pairs={{0,128},{4,132},{8,136},{12,140},{16,144},{20,148},{24,152},{28,15... | collective-permute-start | bytes 245768 | tf_op jit(solution)/shard_map/ppermute | solution.py:343
  164.8 3.6 %collective-permute-done.7 = bf16[64,640]{1,0:T(8,128)(2,1)S(1)} collective-permute-done((bf16[64,640]{1,0:T(8,128)(2,1)S(1)}, bf16[64,640]{1,0:T(8,128)(2,1)S(1)}, u32[]{:S(2)}, u32[]{:S(2)}) %collective-permute-start.7) | collective-permute-done | bytes 81952 | tf_op jit(solution)/shard_map/ppermute | solution.py:343
  168.4 2.2 %collective-permute-done.9 = bf16[64,640]{1,0:T(8,128)(2,1)S(1)} collective-permute-done((bf16[64,640]{1,0:T(8,128)(2,1)S(1)}, bf16[64,640]{1,0:T(8,128)(2,1)S(1)}, u32[]{:S(2)}, u32[]{:S(2)}) %collective-permute-start.9) | collective-permute-done | bytes 81952 | tf_op jit(solution)/shard_map/ppermute | solution.py:343
  171.6 4.7 %all-to-all-done.2.x_ref = bf16[128,16,128]{2,1,0:T(8,128)(2,1)S(1)} async-done(((bf16[128,16,128]{2,1,0:T(8,128)(2,1)}), bf16[128,16,128]{2,1,0:T(8,128)(2,1)S(1)}, u32[]{:S(2)}, u32[]{:S(2)}) %all-to-all-start.2) | async-done | bytes 524320 | tf_op jit(solution)/shard_map/all_to_all | solution.py:361
  (103 shorter events, 25.2 us)
Async XLA Ops:
  6.5 19.1 %copy-start.12 = (s32[2]{0:T(128)S(1)}, s32[2]{0:T(128)}, u32[]{:S(2)}) copy-start(s32[2]{0:T(128)} %param.15) | copy-start | bytes 28
  6.5 19.2 %copy-start.7 = (bf16[2,128,576]{1,2,0:T(8,128)(2,1)S(1)}, bf16[2,128,576]{1,2,0:T(8,128)(2,1)}, u32[]{:S(2)}) copy-start(bf16[2,128,576]{1,2,0:T(8,128)(2,1)} %param.13) | copy-start | bytes 884740
  6.5 74.7 %all-to-all-start = ((bf16[128,48,128]{2,1,0:T(8,128)(2,1)}), bf16[128,48,128]{2,1,0:T(8,128)(2,1)}, u32[]{:S(2)}, u32[]{:S(2)}) async-start(bf16[128,48,128]{2,1,0:T(8,128)(2,1)} %shard_map.98), calls=%async_computation | async-start | bytes 3145728 | tf_op jit(solution)/shard_map/all_to_all | solution.py:301
  26.0 40.7 %collective-permute-start = (bf16[2,64,640]{2,1,0:T(8,128)(2,1)S(1)}, bf16[2,64,640]{2,1,0:T(8,128)(2,1)}, u32[]{:S(2)}, u32[]{:S(2)}) collective-permute-start(bf16[2,64,640]{2,1,0:T(8,128)(2,1)S(1)} %fusion.2), channel_id=1, source_target_pairs={{128,0},{132,4},{136,8},{140,12},{144,16},{148,20},{152,24},{156,2... | collective-permute-start | bytes 491528 | tf_op jit(solution)/shard_map/ppermute | solution.py:327
  27.3 40.1 %collective-permute-start.1 = (bf16[2,64,640]{2,1,0:T(8,128)(2,1)S(1)}, bf16[2,64,640]{2,1,0:T(8,128)(2,1)}, u32[]{:S(2)}, u32[]{:S(2)}) collective-permute-start(bf16[2,64,640]{2,1,0:T(8,128)(2,1)S(1)} %fusion.2), channel_id=1, source_target_pairs={{256,0},{260,4},{264,8},{268,12},{272,16},{276,20},{280,24},{284,2... | collective-permute-start | bytes 491528 | tf_op jit(solution)/shard_map/ppermute | solution.py:327
  28.6 42.1 %collective-permute-start.2 = (bf16[2,64,640]{2,1,0:T(8,128)(2,1)S(1)}, bf16[2,64,640]{2,1,0:T(8,128)(2,1)}, u32[]{:S(2)}, u32[]{:S(2)}) collective-permute-start(bf16[2,64,640]{2,1,0:T(8,128)(2,1)S(1)} %fusion.2), channel_id=1, source_target_pairs={{384,0},{388,4},{392,8},{396,12},{400,16},{404,20},{408,24},{412,2... | collective-permute-start | bytes 491528 | tf_op jit(solution)/shard_map/ppermute | solution.py:327
  40.8 34.6 %collective-permute-start.10 = (bf16[896,384]{1,0:T(8,128)(2,1)}, bf16[896,384]{1,0:T(8,128)(2,1)S(1)}, u32[]{:S(2)}, u32[]{:S(2)}) collective-permute-start(bf16[896,384]{1,0:T(8,128)(2,1)} %get-tuple-element.40), channel_id=1, source_target_pairs={{128,129},{129,128},{130,131},{131,130},{132,133},{133,132},{134,1... | collective-permute-start | bytes 2064392 | tf_op jit(solution)/shard_map/ppermute | solution.py:304
  41.5 36.3 %collective-permute-start.11 = (bf16[896,384]{1,0:T(8,128)(2,1)}, bf16[896,384]{1,0:T(8,128)(2,1)}, u32[]{:S(2)}, u32[]{:S(2)}) collective-permute-start(bf16[896,384]{1,0:T(8,128)(2,1)} %get-tuple-element.41), channel_id=1, source_target_pairs={{128,130},{129,131},{130,128},{131,129},{132,134},{133,135},{134,1... | collective-permute-start | bytes 2064392 | tf_op jit(solution)/shard_map/ppermute | solution.py:304
  43.7 31.0 %copy-start.6 = (f32[3,16,96]{1,2,0:T(8,128)S(1)}, f32[3,16,96]{1,2,0:T(8,128)}, u32[]{:S(2)}) copy-start(f32[3,16,96]{1,2,0:T(8,128)} %copy-done.5) | copy-start | bytes 55300
  44.9 32.9 %copy-start.1 = (bf16[896,384]{1,0:T(8,128)(2,1)S(1)}, bf16[896,384]{1,0:T(8,128)(2,1)}, u32[]{:S(2)}) copy-start(bf16[896,384]{1,0:T(8,128)(2,1)} %copy-done) | copy-start | bytes 2064388
  66.7 11.0 %collective-permute-start.12 = (bf16[896,384]{1,0:T(8,128)(2,1)S(1)}, bf16[896,384]{1,0:T(8,128)(2,1)S(1)}, u32[]{:S(2)}, u32[]{:S(2)}) collective-permute-start(bf16[896,384]{1,0:T(8,128)(2,1)S(1)} %get-tuple-element.42), channel_id=1, source_target_pairs={{128,131},{129,130},{130,129},{131,128},{132,135},{133,134},{134,1... | collective-permute-start | bytes 2064392 | tf_op jit(solution)/shard_map/ppermute | solution.py:304
  67.5 69.5 %collective-permute-start.15 = (bf16[384,640]{1,0:T(8,128)(2,1)}, bf16[384,640]{1,0:T(8,128)(2,1)}, u32[]{:S(2)}, u32[]{:S(2)}) collective-permute-start(bf16[384,640]{1,0:T(8,128)(2,1)} %get-tuple-element.50), channel_id=1, source_target_pairs={{128,132},{132,136},{136,128},{140,144},{144,148},{148,140},{152,1... | collective-permute-start | bytes 1474568 | tf_op jit(solution)/shard_map/ppermute | solution.py:307
  72.8 17.9 %collective-permute-start.3 = (bf16[8,64,640]{2,1,0:T(8,128)(2,1)}, bf16[8,64,640]{2,1,0:T(8,128)(2,1)}, u32[]{:S(2)}, u32[]{:S(2)}) collective-permute-start(bf16[8,64,640]{2,1,0:T(8,128)(2,1)} %pad_maximum_fusion.1), channel_id=1, source_target_pairs={{0,1},{1,0},{2,3},{3,2},{4,5},{5,4},{6,7},{7,6},{8,9},{9,8},{10,11... | collective-permute-start | bytes 1966088 | tf_op jit(solution)/shard_map/ppermute | solution.py:304
  76.3 60.7 %collective-permute-start.16 = (bf16[384,640]{1,0:T(8,128)(2,1)}, bf16[384,640]{1,0:T(8,128)(2,1)}, u32[]{:S(2)}, u32[]{:S(2)}) collective-permute-start(bf16[384,640]{1,0:T(8,128)(2,1)} %get-tuple-element.49), channel_id=1, source_target_pairs={{128,136},{132,128},{136,132},{140,148},{144,140},{148,144},{152,1... | collective-permute-start | bytes 1474568 | tf_op jit(solution)/shard_map/ppermute | solution.py:307
  85.8 20.4 %all-to-all-start.1 = ((bf16[4,192,384]{2,1,0:T(8,128)(2,1)}), bf16[4,192,384]{2,1,0:T(8,128)(2,1)S(1)}, u32[]{:S(2)}, u32[]{:S(2)}) async-start(bf16[4,192,384]{2,1,0:T(8,128)(2,1)} %shard_map.101), calls=%async_computation.1 | async-start | bytes 1179648 | tf_op jit(solution)/shard_map/all_to_all | solution.py:355
  104.2 50.7 %collective-permute-start.4 = (bf16[256,640]{1,0:T(8,128)(2,1)S(1)}, bf16[256,640]{1,0:T(8,128)(2,1)S(1)}, u32[]{:S(2)}, u32[]{:S(2)}) collective-permute-start(bf16[256,640]{1,0:T(8,128)(2,1)S(1)} %get-tuple-element.36), channel_id=1, source_target_pairs={{0,1},{1,0},{2,3},{3,2},{4,5},{5,4},{6,7},{7,6},{8,9},{9,8},{10,11... | collective-permute-start | bytes 983048 | tf_op jit(solution)/shard_map/ppermute | solution.py:304
  106.4 1.4 collective-permute-start.13
  107.0 3.0 %collective-permute-start.14 = (bf16[96,384]{1,0:T(8,128)(2,1)S(1)}, bf16[96,384]{1,0:T(8,128)(2,1)S(1)}, u32[]{:S(2)}, u32[]{:S(2)}) collective-permute-start(bf16[96,384]{1,0:T(8,128)(2,1)S(1)} %fusion.3), channel_id=1, source_target_pairs={{128,136},{132,128},{136,132},{140,148},{144,140},{148,144},{152,1... | collective-permute-start | bytes 221192 | tf_op jit(solution)/shard_map/ppermute | solution.py:307
  107.8 47.1 %collective-permute-start.5 = (bf16[256,640]{1,0:T(8,128)(2,1)S(1)}, bf16[256,640]{1,0:T(8,128)(2,1)S(1)}, u32[]{:S(2)}, u32[]{:S(2)}) collective-permute-start(bf16[256,640]{1,0:T(8,128)(2,1)S(1)} %get-tuple-element.37), channel_id=1, source_target_pairs={{0,2},{1,3},{2,0},{3,1},{4,6},{5,7},{6,4},{7,5},{8,10},{9,11},{10,... | collective-permute-start | bytes 983048 | tf_op jit(solution)/shard_map/ppermute | solution.py:304
  110.1 44.8 %collective-permute-start.6 = (bf16[256,640]{1,0:T(8,128)(2,1)}, bf16[256,640]{1,0:T(8,128)(2,1)S(1)}, u32[]{:S(2)}, u32[]{:S(2)}) collective-permute-start(bf16[256,640]{1,0:T(8,128)(2,1)} %get-tuple-element.38), channel_id=1, source_target_pairs={{0,3},{1,2},{2,1},{3,0},{4,7},{5,6},{6,5},{7,4},{8,11},{9,10},{10,... | collective-permute-start | bytes 983048 | tf_op jit(solution)/shard_map/ppermute | solution.py:304
  140.3 36.0 %all-to-all-start.2 = ((bf16[128,16,128]{2,1,0:T(8,128)(2,1)}), bf16[128,16,128]{2,1,0:T(8,128)(2,1)S(1)}, u32[]{:S(2)}, u32[]{:S(2)}) async-start(bf16[128,16,128]{2,1,0:T(8,128)(2,1)} %shard_map.102), calls=%async_computation.2 | async-start | bytes 1048576 | tf_op jit(solution)/shard_map/all_to_all | solution.py:361
  155.7 12.6 %collective-permute-start.7 = (bf16[64,640]{1,0:T(8,128)(2,1)S(1)}, bf16[64,640]{1,0:T(8,128)(2,1)S(1)}, u32[]{:S(2)}, u32[]{:S(2)}) collective-permute-start(bf16[64,640]{1,0:T(8,128)(2,1)S(1)} %get-tuple-element.54), channel_id=1, source_target_pairs={{0,128},{4,132},{8,136},{12,140},{16,144},{20,148},{24,152},{28,15... | collective-permute-start | bytes 245768 | tf_op jit(solution)/shard_map/ppermute | solution.py:343
  162.1 6.3 %collective-permute-start.8 = (bf16[64,640]{1,0:T(8,128)(2,1)S(1)}, bf16[64,640]{1,0:T(8,128)(2,1)S(1)}, u32[]{:S(2)}, u32[]{:S(2)}) collective-permute-start(bf16[64,640]{1,0:T(8,128)(2,1)S(1)} %get-tuple-element.56), channel_id=1, source_target_pairs={{0,256},{4,260},{8,264},{12,268},{16,272},{20,276},{24,280},{28,28... | collective-permute-start | bytes 245768 | tf_op jit(solution)/shard_map/ppermute | solution.py:343
  163.4 7.2 %collective-permute-start.9 = (bf16[64,640]{1,0:T(8,128)(2,1)S(1)}, bf16[64,640]{1,0:T(8,128)(2,1)S(1)}, u32[]{:S(2)}, u32[]{:S(2)}) collective-permute-start(bf16[64,640]{1,0:T(8,128)(2,1)S(1)} %get-tuple-element.55), channel_id=1, source_target_pairs={{0,384},{4,388},{8,392},{12,396},{16,400},{20,404},{24,408},{28,41... | collective-permute-start | bytes 245768 | tf_op jit(solution)/shard_map/ppermute | solution.py:343
  (9 other events, 64.9 us)

commit v3 on v2

v3 whole, which is shorter than its diff:
```python
import functools
import math

import jax
import jax.numpy as jnp
from jax import lax
from jax.experimental import pallas as pl
from jax.experimental.pallas import tpu as pltpu
from jax.sharding import PartitionSpec as P

LATENT = 512
KV = 576
LP = 512
CAP = 3
HD = 96
DQ = 1792
PART = 640
f32 = jnp.float32
bf16 = jnp.bfloat16
VM = 16 << 20

softmax_scale = 1.0 / math.sqrt(192.0)


whole = pl.BlockSpec(memory_space=pltpu.VMEM)
after = pl.BlockSpec(memory_space=pl.ANY)


def dot(a, b, dims=((1,), (0,))):
    return lax.dot_general(a, b, (dims, ((), ())), preferred_element_type=f32)


def pieces(value):
    high = value.astype(bf16).astype(f32)
    middle = (value - high).astype(bf16).astype(f32)
    return high, middle, value - high - middle


def flat_rows(s_ref, scr):
    scr[...] = s_ref[...].astype(f32).reshape(scr.shape)


def dispatch_kernel(sel_ref, rows_ref, *refs):
    out_ref, scr = refs[-2:]
    source = lax.broadcasted_iota(jnp.int32, (256, 256), 0)
    target = lax.broadcasted_iota(jnp.int32, (256, 256), 1)
    order = (source == 4 * (target % 64) + target // 64).astype(f32).astype(bf16)
    count = out_ref.shape[0]
    for b in range(DQ // 256):
        turned = dot(rows_ref[:, 256 * b : 256 * b + 256], order).astype(bf16)
        for c in range(CAP):
            sent = dot(sel_ref[c], turned)
            for k in range(2):
                scr[pl.ds(16 * c + 2 * b + k, count, stride=48), :] = sent[:, 128 * k : 128 * k + 128]
    for c in range(CAP):
        for k in range(14, 16):
            scr[pl.ds(16 * c + k, count, stride=48), :] = jnp.zeros((count, 128), f32)
    out_ref[...] = scr[...].astype(bf16).reshape(out_ref.shape)


def dispatch(sel, rows, *earlier):
    groups = sel.shape[1]
    return pl.pallas_call(
        dispatch_kernel,
        in_specs=[whole] * 2 + [after] * len(earlier),
        out_shape=jax.ShapeDtypeStruct((groups, 48, 128), bf16),
        scratch_shapes=[pltpu.VMEM((groups * 48, 128), f32)],
        compiler_params=pltpu.CompilerParams(vmem_limit_bytes=VM),
    )(sel, rows, *earlier)


def ask_kernel(tp_ref, length_ref, q_ref, out_ref):
    out_ref[:KV] = q_ref[0]
    length = length_ref[tp_ref[0] % 2]
    row = lax.broadcasted_iota(jnp.int32, (16, 128), 0)
    out_ref[KV:] = jnp.where(row == 0, length // 64, length % 64).astype(f32).astype(bf16)


def ask(part, lengths, queries):
    return pl.pallas_call(
        ask_kernel,
        grid_spec=pltpu.PrefetchScalarGridSpec(
            num_scalar_prefetch=2,
            grid=(1,),
            in_specs=[pl.BlockSpec((1, KV, 128), lambda i, tp, lengths: (tp[0] % 2, 0, 0))],
            out_specs=pl.BlockSpec((KV + 16, 128), lambda i, tp, lengths: (0, 0)),
        ),
        out_shape=jax.ShapeDtypeStruct((KV + 16, 128), bf16),
    )(part.reshape(1).astype(jnp.int32), lengths, queries)


def stack_kernel(*refs):
    for n in range(4):
        refs[-1][n] = refs[n][...]


def stack(rows, earlier):
    return pl.pallas_call(
        stack_kernel,
        in_specs=[whole] * 4 + [after],
        out_shape=jax.ShapeDtypeStruct((4,) + rows[0].shape, bf16),
    )(*rows, earlier)


def attend_kernel(tp_ref, s_ref, mine_ref, other_ref, *refs):
    p_refs, (scr, keys, found) = refs[:4], refs[4:]
    step = pl.program_id(0)
    row = served(step, tp_ref)
    flat_rows(s_ref, scr)
    for m in range(9):
        keys[:, 128 * m : 128 * m + 128] = scr[pl.ds(m, LP // 2, stride=9), :].astype(bf16)
    asked = jnp.where(step < 4, mine_ref[0].astype(f32), other_ref[0].astype(f32))
    left = asked[KV : KV + 1, 0:1] * 64.0 + asked[KV + 1 : KV + 2, 0:1] - (tp_ref[0] * LP).astype(f32)
    gap = jnp.zeros((64, 128), f32)
    even_q = jnp.concatenate([asked[:KV], gap], axis=0).T.astype(bf16)
    odd_q = jnp.concatenate([gap, asked[:KV]], axis=0).T.astype(bf16)
    even = dot(even_q, keys[:, :640], ((1,), (1,))) * softmax_scale
    odd = dot(odd_q, keys[:, 512:], ((1,), (1,))) * softmax_scale
    position = (2 * lax.broadcasted_iota(jnp.int32, (128, LP // 2), 1)).astype(f32)
    even = jnp.where(position < left, even, -1e30)
    odd = jnp.where(position + 1.0 < left, odd, -1e30)
    top = jnp.maximum(jnp.max(even, axis=1, keepdims=True), jnp.max(odd, axis=1, keepdims=True))
    even = jnp.where(position < left, jnp.exp(even - top), 0.0).astype(bf16)
    odd = jnp.where(position + 1.0 < left, jnp.exp(odd - top), 0.0).astype(bf16)
    total = jnp.sum(even.astype(f32), axis=1, keepdims=True) + jnp.sum(odd.astype(f32), axis=1, keepdims=True)
    summed = dot(even, keys[:, :LATENT]) + dot(odd, keys[:, 512:])[:, 64 : 64 + LATENT]
    lane = lax.broadcasted_iota(jnp.int32, (128, 128), 1)
    stats = jnp.zeros((128, 128), f32)
    for at, piece in enumerate(pieces(top) + pieces(total)):
        stats = jnp.where(lane == at, piece, stats)
    found[:, :LATENT] = summed.astype(bf16)
    found[:, LATENT:] = stats.astype(bf16)
    span = pl.ds(pl.multiple_of(row * 32, 32), 32)
    for d, p_ref in enumerate(p_refs):
        share = pl.multiple_of(jnp.bitwise_xor(tp_ref[0], d) * 32, 32)
        p_ref[span, :] = found[pl.ds(share, 32), :]


def served(step, tp):
    return 2 * (step % 4) + jnp.bitwise_xor(tp[0] % 2, step // 4)


def attend(store, mine, other, part):
    shape = (256, PART)
    rows = (1,) + mine.shape[1:]
    return pl.pallas_call(
        attend_kernel,
        grid_spec=pltpu.PrefetchScalarGridSpec(
            num_scalar_prefetch=1,
            grid=(8,),
            in_specs=[
                pl.BlockSpec((1, 1, LP * KV), lambda i, tp: (0, 0, served(i, tp))),
                pl.BlockSpec(rows, lambda i, tp: (jnp.minimum(i, 3), 0, 0)),
                pl.BlockSpec(rows, lambda i, tp: (jnp.maximum(i - 4, 0), 0, 0)),
            ],
            out_specs=[pl.BlockSpec(shape, lambda i, tp: (0, 0))] * 4,
            scratch_shapes=[
                pltpu.VMEM((LP * KV // 128, 128), f32),
                pltpu.VMEM((LP // 2, 2 * KV), bf16),
                pltpu.VMEM((128, PART), bf16),
            ],
        ),
        out_shape=[jax.ShapeDtypeStruct(shape, bf16)] * 4,
        compiler_params=pltpu.CompilerParams(vmem_limit_bytes=VM),
    )(part.reshape(1).astype(jnp.int32), store, mine, other)


def unpack_kernel(tp_ref, s_ref, _, p_ref, *refs):
    scr = refs[-1]
    step = pl.program_id(0)
    flat_rows(s_ref, scr)

    @pl.when(step < 4)
    def _():
        for m in range(3):
            p_ref[:, 128 * m : 128 * m + 128] = scr[pl.ds(m, 448, stride=3), :].astype(bf16)

    if len(refs) > 1:
        w_ref = refs[0]

        @pl.when(step >= 4)
        def _():
            for m in range(14):
                w_ref[:, 128 * m : 128 * m + 128] = scr[pl.ds(m, HD, stride=14), :].astype(bf16)


def unpack(store, part, far, earlier):
    def block(i, tp):
        x_hi = jnp.bitwise_xor(tp[0] // 2, 1 if far else 0)
        return 0, 0, jnp.where(i < 4, 4 * (i // 2) + 2 * x_hi + i % 2, i + 4)

    out_specs = [pl.BlockSpec((448, 384), lambda i, tp: (jnp.minimum(i, 3), 0))]
    out_shape = [jax.ShapeDtypeStruct((DQ, 384), bf16)]
    if not far:
        out_specs.append(pl.BlockSpec((HD, DQ), lambda i, tp: (jnp.maximum(i - 4, 0), 0)))
        out_shape.append(jax.ShapeDtypeStruct((4 * HD, DQ), bf16))
    return pl.pallas_call(
        unpack_kernel,
        grid_spec=pltpu.PrefetchScalarGridSpec(
            num_scalar_prefetch=1,
            grid=(4 if far else 8,),
            in_specs=[pl.BlockSpec((1, 1, DQ * HD), block), after],
            out_specs=out_specs,
            scratch_shapes=[pltpu.VMEM((DQ * HD // 128, 128), f32)],
        ),
        out_shape=out_shape,
        compiler_params=pltpu.CompilerParams(vmem_limit_bytes=VM),
    )(part.reshape(1).astype(jnp.int32), store, earlier)


def weights_kernel(tp_ref, here_ref, far_ref, w_ref, mark_ref):
    mark_ref[...] = jnp.zeros_like(mark_ref)

    def fill(refs):
        for half in range(2):
            for q in range(2):
                rows = slice(896 * half + 448 * q, 896 * half + 448 * q + 448)
                for r in range(4):
                    found = jnp.concatenate([ref[rows, HD * r : HD * r + HD] for ref in refs], axis=1)
                    for b in range(7):
                        at = DQ * q + 256 * b + 64 * r
                        w_ref[half, at : at + 64, :] = found[64 * b : 64 * b + 64]

    @pl.when(tp_ref[0] < 2)
    def _():
        fill((here_ref, far_ref))

    @pl.when(tp_ref[0] >= 2)
    def _():
        fill((far_ref, here_ref))


def arrange(part, here, far):
    return pl.pallas_call(
        weights_kernel,
        in_specs=[pl.BlockSpec(memory_space=pltpu.SMEM), whole, whole],
        out_shape=[jax.ShapeDtypeStruct((2, 2 * DQ, 2 * HD), bf16), jax.ShapeDtypeStruct((8, 128), f32)],
        compiler_params=pltpu.CompilerParams(vmem_limit_bytes=VM),
    )(part.reshape(1).astype(jnp.int32), here, far)


def join_kernel(p0_ref, p1_ref, p2_ref, p3_ref, out_ref):
    refs = (p0_ref, p1_ref, p2_ref, p3_ref)
    tops, totals = [], []
    for p_ref in refs:
        stats = p_ref[:, LATENT:].astype(f32)
        tops.append(stats[:, 0:1] + stats[:, 1:2] + stats[:, 2:3])
        totals.append(stats[:, 3:4] + stats[:, 4:5] + stats[:, 5:6])
    top = functools.reduce(jnp.maximum, tops)
    scales = [jnp.exp(own - top) for own in tops]
    total = sum(scale * own for scale, own in zip(scales, totals))
    scales = [scale / total for scale in scales]
    out_ref[:, :LATENT] = sum(
        scale * p_ref[:, :LATENT].astype(f32) for scale, p_ref in zip(scales, refs)
    ).astype(bf16)
    lane = lax.broadcasted_iota(jnp.int32, (256, 128), 1)
    stats = jnp.zeros((256, 128), f32)
    for at, piece in enumerate(pieces(top + jnp.log(total))):
        stats = jnp.where(lane == at, piece, stats)
    out_ref[:, LATENT:] = stats.astype(bf16)


def join(parts):
    return pl.pallas_call(
        join_kernel,
        out_shape=jax.ShapeDtypeStruct((256, PART), bf16),
        compiler_params=pltpu.CompilerParams(vmem_limit_bytes=VM),
    )(*parts)


def slab_kernel(x_ref, *refs):
    out_ref, scr = refs[-2:]
    count = x_ref.shape[0]
    scr[...] = x_ref[...].astype(f32).reshape(scr.shape)
    for c in range(CAP):
        for k in range(14):
            found = scr[pl.ds(16 * c + k, count, stride=48), :].astype(bf16)
            out_ref[count * c : count * c + count, 128 * k : 128 * k + 128] = found


def slots_of(arrived, *earlier):
    count = arrived.shape[0]
    return pl.pallas_call(
        slab_kernel,
        in_specs=[whole] + [after] * len(earlier),
        out_shape=jax.ShapeDtypeStruct((CAP * count, DQ), bf16),
        scratch_shapes=[pltpu.VMEM((count * 48, 128), f32)],
        compiler_params=pltpu.CompilerParams(vmem_limit_bytes=VM),
    )(arrived, *earlier)


def project_kernel(_, x_ref, w_ref, *refs):
    z_ref = refs[-1]
    for half in range(2):
        found = dot(x_ref[...], w_ref[half])
        if len(refs) > 1:
            found = found + refs[0][half]
            z_ref[2 * HD * half : 2 * HD * half + 2 * HD, :] = found.T.astype(bf16)
        else:
            z_ref[half] = found


def project(core, slab, weights, *other):
    slots = slab.shape[0]
    if other:
        shape = jax.ShapeDtypeStruct((4 * HD, slots), bf16)
    else:
        shape = jax.ShapeDtypeStruct((2, slots, 2 * HD), f32)
    full = lambda array: pl.BlockSpec(array.shape, lambda i, core: (0,) * len(array.shape))
    return pl.pallas_call(
        project_kernel,
        grid_spec=pltpu.PrefetchScalarGridSpec(
            num_scalar_prefetch=1,
            grid=(1,),
            in_specs=[full(slab), pl.BlockSpec((2, DQ, 2 * HD), lambda i, core: (0, core[0], 0))]
            + [full(sums) for sums in other],
            out_specs=full(shape),
        ),
        out_shape=shape,
        compiler_params=pltpu.CompilerParams(vmem_limit_bytes=VM),
    )(core.reshape(1).astype(jnp.int32), slab, weights, *other)


def descend_kernel(core_ref, h_ref, o_ref, w_ref, out_ref, scr, turned):
    count = out_ref.shape[0]
    core = core_ref[0]
    for x_hi in range(2):
        rows = slice(HD * x_hi, HD * x_hi + HD)
        for at, ref in ((2 * x_hi + core, h_ref), (2 * x_hi + 1 - core, o_ref)):
            scr[pl.ds(pl.multiple_of(at * HD, HD), HD), :] = ref[rows]
    for c in range(CAP):
        result = dot(scr[:, count * c : count * c + count], w_ref[...], ((0,), (0,)))
        for k in range(14):
            turned[pl.ds(16 * c + k, count, stride=48), :] = result[:, 128 * k : 128 * k + 128]
        for k in range(14, 16):
            turned[pl.ds(16 * c + k, count, stride=48), :] = jnp.zeros((count, 128), f32)
    out_ref[...] = turned[...].astype(bf16).reshape(out_ref.shape)


def descend(core, hidden, other, down):
    count = hidden.shape[1] // CAP
    return pl.pallas_call(
        descend_kernel,
        in_specs=[pl.BlockSpec(memory_space=pltpu.SMEM)] + [whole] * 3,
        out_shape=jax.ShapeDtypeStruct((count, 48, 128), bf16),
        scratch_shapes=[pltpu.VMEM((4 * HD, CAP * count), bf16), pltpu.VMEM((count * 48, 128), f32)],
        compiler_params=pltpu.CompilerParams(vmem_limit_bytes=VM),
    )(core.reshape(1).astype(jnp.int32), hidden, other, down)


def combine_kernel(a_ref, x_ref, out_ref, scr):
    count = x_ref.shape[0]
    scr[...] = x_ref[...].astype(f32).reshape(scr.shape)
    for k in range(14):
        result = jnp.zeros((32, 128), f32)
        for c in range(CAP):
            result = result + dot(a_ref[c], scr[pl.ds(16 * c + k, count, stride=48), :].astype(bf16))
        out_ref[:, 128 * k : 128 * k + 128] = (result[:16] + result[16:]).astype(bf16)


def combine(weight, result):
    return pl.pallas_call(
        combine_kernel,
        out_shape=jax.ShapeDtypeStruct((16, DQ), bf16),
        scratch_shapes=[pltpu.VMEM((result.shape[0] * 48, 128), f32)],
        compiler_params=pltpu.CompilerParams(vmem_limit_bytes=VM),
    )(weight, result)


def per_device(store, queries, new_latent, cached_len, rows, expert_ids, route_gates, capacity):
    groups = lax.axis_size("sec")
    servers = groups // 4
    place = lax.axis_index("sec")
    part = lax.axis_index("tp")
    serving = place < servers
    both = ("sec", "tp")
    core = part % 2
    experts = capacity.shape[1]

    def across(value, d, first, last):
        return lax.ppermute(value, both, [(4 * q + t, 4 * q + (t ^ d)) for q in range(first, last) for t in range(4)])

    labels = jnp.arange(experts, dtype=jnp.int32)
    match = expert_ids[:, :, None] == labels[None, None, :]
    hits = jnp.any(match, axis=1).astype(jnp.int32)
    gate_of = jnp.sum(jnp.where(match, route_gates[:, :, None], 0.0), axis=1)
    rank = jnp.cumsum(hits, axis=0) - hits
    keep = (hits == 1) & (rank < capacity[0][None, :])
    slots = jnp.arange(CAP, dtype=jnp.int32)
    pick = (keep[None] & (rank[None] == slots[:, None, None])).astype(f32)
    spread = jnp.pad(jnp.repeat(pick, 3, axis=2), ((0, 0), (0, 0), (servers, 0)))
    sel = jnp.swapaxes(spread, 1, 2).astype(bf16)

    asked = ask(part, cached_len, jnp.swapaxes(queries, 1, 2))
    mine = [asked]
    for k in range(1, 4):
        mine.append(lax.ppermute(asked, "sec", [(k * servers + a, a) for a in range(servers)]))
    outgoing = dispatch(sel, rows)
    mine = stack(mine, outgoing[0, :16])
    (far,) = unpack(store, part, True, mine[0, :16])
    far = across(far, 2, servers, groups)

    def window():
        arrived = lax.all_to_all(outgoing, "sec", split_axis=0, concat_axis=0, tiled=True)
        other = across(mine, 1, 0, servers)
        here, down = unpack(store, part, False, outgoing[0, :16])
        parts = lax.cond(
            serving,
            lambda: tuple(attend(store, mine, other, part)),
            lambda: (jnp.zeros((256, PART), bf16),) * 4,
        )
        parts = [parts[0]] + [across(parts[d], d, 0, servers) for d in range(1, 4)]
        answer = lax.cond(serving, lambda: join(parts), lambda: jnp.zeros((256, PART), bf16))
        return arrived, here, down, answer

    def experts_part():
        slab = slots_of(arrived)
        beside = across(slab, 1, servers, groups)
        partial = project(core, slab, weights)
        partial = project(1 - core, beside, weights, partial)
        partial = partial.astype(f32) + across(partial, 2, servers, groups).astype(f32)
        hidden = (jax.nn.silu(partial[: 2 * HD]) * partial[2 * HD :]).astype(bf16)
        return descend(core, hidden, across(hidden, 1, servers, groups), down)

    def way_back():
        back = lax.all_to_all(result, "sec", split_axis=0, concat_axis=0, tiled=True)
        shares = answer.reshape(4, 64, PART)
        returned = shares[0]
        for k in range(1, 4):
            returned = returned + lax.ppermute(shares[k], "sec", [(a, k * servers + a) for a in range(servers)])
        mine = lax.dynamic_slice_in_dim(queries, part * 32, 32, 1)
        own = jnp.einsum("rhk,rk->rh", mine, new_latent, preferred_element_type=f32) * softmax_scale
        own = own[:, :, None]
        returned = returned.reshape(2, 32, PART).astype(f32)
        others = returned[:, :, 512:513] + returned[:, :, 513:514] + returned[:, :, 514:515]
        top = jnp.maximum(own, others)
        own, others = jnp.exp(own - top), jnp.exp(others - top)
        attended = (others * returned[:, :, :LATENT] + own * new_latent[:, None, :LATENT].astype(f32)) / (own + others)

        scaled = spread * jnp.pad(jnp.repeat(gate_of, 3, axis=1), ((0, 0), (servers, 0)))[None]
        high = lax.reduce_precision(scaled, 8, 7)
        weight = jnp.concatenate([high, scaled - high], axis=1).astype(bf16)
        return combine(weight, back), attended.astype(bf16)

    def held(steps):
        shapes = jax.eval_shape(steps)
        return lax.cond(
            capacity[0, 0] >= 0, steps, lambda: jax.tree.map(lambda leaf: jnp.zeros(leaf.shape, leaf.dtype), shapes)
        )

    arrived, here, down, answer = held(window)
    weights, _ = arrange(part, here, far)
    result = held(experts_part)
    mixed, attended = held(way_back)

    return (attended, mixed)


def solution(mesh):
    placed = (
        P("sec", "tp", None),
        P("sec", None, None),
        P("sec", None),
        P("sec"),
        P("sec", "tp"),
        P("sec", None),
        P("sec", None),
        P("sec", None),
    )
    return jax.shard_map(
        per_device,
        mesh=mesh,
        in_specs=placed,
        out_specs=(P("sec", "tp", None), P("sec", "tp")),
        check_vma=False,
    )
```

time: 179 us -> 170 us (0.950)
  the two profiles are of different devices: /device:TPU:4 before, /device:TPU:8 now
where the time goes in v3:
time: 170 us; the launch traced here: 169 us
  starting transfers between devices  62 us (36%)
  waiting for transfers between devices  50.3 us (30%)
  Pallas kernels  43.6 us (26%)
  local copies, waits for them, and re-layouts  9.3 us (5%)
  other arithmetic  2.34 us (1%)
    ppermute x3, waiting for transfers between devices, way_back(): lax.ppermute(shares[k], 'sec', [(a, k * servers + a) for a in range(serve...  24.1 us
    all_to_all x1, starting transfers between devices, way_back(): lax.all_to_all(result, 'sec', split_axis=0, concat_axis=0, tiled=True)  17.5 us
    all_to_all x1, starting transfers between devices, window(): lax.all_to_all(outgoing, 'sec', split_axis=0, concat_axis=0, tiled=True)  16.7 us
    ppermute x8, starting transfers between devices, across(): lax.ppermute(value, both, [(4 * q + t, 4 * q + (t ^ d)) for q in range(fi...  13.8 us
    ppermute x8, waiting for transfers between devices, across(): lax.ppermute(value, both, [(4 * q + t, 4 * q + (t ^ d)) for q in range(fi...  13.7 us
    pallas_call x1, Pallas kernels, attend(): pl.pallas_call(attend_kernel, grid_spec=pltpu.PrefetchScalarGridSpec(num_...  11.4 us
    pallas_call x2, Pallas kernels, unpack(): pl.pallas_call(unpack_kernel, grid_spec=pltpu.PrefetchScalarGridSpec(num_...  10.2 us
    ppermute x3, starting transfers between devices, way_back(): lax.ppermute(shares[k], 'sec', [(a, k * servers + a) for a in range(serve...  10.1 us
  transfers between devices with their start and end apart: 16, of which 8 were waited for; matrix products, arithmetic and copies ran while one was open for 4% of the time, Pallas kernels for 15%

profile of v3, /device:TPU:8, one launch (start us, length us, event | category | flops | bytes accessed | tf_op | source)
XLA Modules:
  0.0 169.1 jit_solution(6507552155651720772)
XLA Ops:
  13.2 4.2 %collective-permute-done.10.refs_1_ = bf16[592,128]{1,0:T(8,128)(2,1)S(1)} collective-permute-done((bf16[592,128]{1,0:T(8,128)(2,1)}, bf16[592,128]{1,0:T(8,128)(2,1)S(1)}, u32[]{:S(2)}, u32[]{:S(2)}) %collective-permute-start.10) | collective-permute-done | bytes 151584 | tf_op jit(solution)/shard_map/ppermute | solution.py:397
  21.5 2.9 %shard_map.103 = bf16[1792,384]{1,0:T(8,128)(2,1)S(1)} custom-call(s32[1]{0:T(128)} %bitcast.14.tp_ref, bf16[1,1,2359296]{2,1,0:T(2,128)(2,1)} %s_ref.1, bf16[16,128]{1,0:T(8,128)(2,1)S(1)} %slice_bitcast_fusion.1._), custom_call_target="tpu_custom_call" | custom-call | tf_op jit(solution)/shard_map/pallas_call | solution.py:197
  26.0 63.2 %conditional.5 = (bf16[128,48,128]{2,1,0:T(8,128)(2,1)}, bf16[1792,384]{1,0:T(8,128)(2,1)}, bf16[384,1792]{1,0:T(8,128)(2,1)}, bf16[256,640]{1,0:T(8,128)(2,1)}) conditional(s32[]{:T(128)} %bitcast.11, () %tuple.49, (bf16[128,48,128]{2,1,0:T(8,128)(2,1)}, s32[]{:T(128)}, bf16[1,1,2359296]{2,1,0:T(2,128)(2,1)}, s32[]{:T(128)}, ...), branch_computations={%region_2.3_spmd, %region_3.8_spmd} | conditional | flops 2 | bytes 12722536 | solution.py:447
  26.0 16.7 %all-to-all-start = ((bf16[128,48,128]{2,1,0:T(8,128)(2,1)}), bf16[128,48,128]{2,1,0:T(8,128)(2,1)}, u32[]{:S(2)}, u32[]{:S(2)}) async-start(bf16[128,48,128]{2,1,0:T(8,128)(2,1)} %get-tuple-element.95), calls=%async_computation | async-start | bytes 3145728 | tf_op jit(solution)/shard_map/cond/branch_1_fun/all_to_all | solution.py:404
  46.8 11.4 %conditional = ((bf16[256,640]{1,0:T(8,128)(2,1)}, bf16[256,640]{1,0:T(8,128)(2,1)}, bf16[256,640]{1,0:T(8,128)(2,1)}, bf16[256,640]{1,0:T(8,128)(2,1)})) conditional(s32[]{:T(128)} %convert_element_type.43, () %tuple.33, (s32[]{:T(128)}, bf16[1,1,2359296]{2,1,0:T(2,128)(2,1)}, bf16[4,592,128]{2,1,0:T(8,128)(2,1)S(1)}, ...), branch_computations={%region_4.4_spmd, %region_5.5_spmd} | conditional | bytes 1310768 | solution.py:407
  46.8 11.4 %branch_1_fun.8 = (bf16[256,640]{1,0:T(8,128)(2,1)}, bf16[256,640]{1,0:T(8,128)(2,1)}, bf16[256,640]{1,0:T(8,128)(2,1)}, bf16[256,640]{1,0:T(8,128)(2,1)}) custom-call(s32[1]{0:T(128)} %bitcast.tp_ref, bf16[1,1,2359296]{2,1,0:T(2,128)(2,1)} %get-tuple-element.88.s_ref, bf16[4,592,128]{2,1,0:T(8,128)(2,1)S(1)} %get-tuple-element.89.mine_ref, ...), custom_call_target="tpu_custom_call" | custom-call | tf_op jit(solution)/shard_map/cond/branch_1_fun/cond/branch_1_fun/pallas_call | solution.py:146
  60.2 3.6 %collective-permute-start.2 = (bf16[256,640]{1,0:T(8,128)(2,1)}, bf16[256,640]{1,0:T(8,128)(2,1)S(1)}, u32[]{:S(2)}, u32[]{:S(2)}) collective-permute-start(bf16[256,640]{1,0:T(8,128)(2,1)} %get-tuple-element.104), channel_id=1, source_target_pairs={{0,2},{1,3},{2,0},{3,1},{4,6},{5,7},{6,4},{7,5},{8,10},{9,11},{10,... | collective-permute-start | bytes 983048 | tf_op jit(solution)/shard_map/cond/branch_1_fun/ppermute | solution.py:381
  63.8 3.4 %collective-permute-start.3 = (bf16[256,640]{1,0:T(8,128)(2,1)}, bf16[256,640]{1,0:T(8,128)(2,1)S(1)}, u32[]{:S(2)}, u32[]{:S(2)}) collective-permute-start(bf16[256,640]{1,0:T(8,128)(2,1)} %get-tuple-element.105), channel_id=1, source_target_pairs={{0,3},{1,2},{2,1},{3,0},{4,7},{5,6},{6,5},{7,4},{8,11},{9,10},{10,... | collective-permute-start | bytes 983048 | tf_op jit(solution)/shard_map/cond/branch_1_fun/ppermute | solution.py:381
  67.9 7.2 %branch_1_fun.10 = (bf16[1792,384]{1,0:T(8,128)(2,1)}, bf16[384,1792]{1,0:T(8,128)(2,1)}) custom-call(s32[1]{0:T(128)} %bitcast.1.tp_ref, bf16[1,1,2359296]{2,1,0:T(2,128)(2,1)} %get-tuple-element.97.s_ref, bf16[16,128]{1,0:T(8,128)(2,1)S(1)} %slice_bitcast_fusion._), custom_call_target="tpu_custom_call" | custom-call | tf_op jit(solution)/shard_map/cond/branch_1_fun/pallas_call | solution.py:197
  75.2 4.3 %collective-permute-done.2 = bf16[256,640]{1,0:T(8,128)(2,1)S(1)} collective-permute-done((bf16[256,640]{1,0:T(8,128)(2,1)}, bf16[256,640]{1,0:T(8,128)(2,1)S(1)}, u32[]{:S(2)}, u32[]{:S(2)}) %collective-permute-start.2) | collective-permute-done | bytes 327712 | tf_op jit(solution)/shard_map/cond/branch_1_fun/ppermute | solution.py:381
  79.4 7.3 %collective-permute-done.3 = bf16[256,640]{1,0:T(8,128)(2,1)S(1)} collective-permute-done((bf16[256,640]{1,0:T(8,128)(2,1)}, bf16[256,640]{1,0:T(8,128)(2,1)S(1)}, u32[]{:S(2)}, u32[]{:S(2)}) %collective-permute-start.3) | collective-permute-done | bytes 327712 | tf_op jit(solution)/shard_map/cond/branch_1_fun/ppermute | solution.py:381
  86.7 2.5 %conditional.1 = (bf16[256,640]{1,0:T(8,128)(2,1)}) conditional(s32[]{:T(128)} %convert_element_type.43, () %tuple.32, (bf16[256,640]{1,0:T(8,128)(2,1)}, bf16[256,640]{1,0:T(8,128)(2,1)S(1)}, bf16[256,640]{1,0:T(8,128)(2,1)S(1)}, bf16[256,640]{1,0:T(8,128)(2,1)S(1)}) %tuple.35), branch_computations={%region_6.6_spmd, %region_7.7_spmd} | conditional | bytes 327690 | solution.py:413
  86.7 2.5 %branch_1_fun.9 = bf16[256,640]{1,0:T(8,128)(2,1)} custom-call(bf16[256,640]{1,0:T(8,128)(2,1)} %get-tuple-element.91.p0_ref, bf16[256,640]{1,0:T(8,128)(2,1)S(1)} %get-tuple-element.92.p1_ref, bf16[256,640]{1,0:T(8,128)(2,1)S(1)} %get-tuple-element.93.p2_ref, bf16[256,640]{1,0:T(8,128)(2,1)S(1)} %get-tuple-element.94.p3_ref), custom_call_target="tpu_custom_call" | custom-call | tf_op jit(solution)/shard_map/cond/branch_1_fun/cond/branch_1_fun/pallas_call | solution.py:264
  89.2 4.3 %shard_map.104 = (bf16[2,3584,192]{2,1,0:T(8,128)(2,1)}, f32[8,128]{1,0:T(8,128)}) custom-call(s32[1]{0:T(128)} %bitcast.14.tp_ref, bf16[1792,384]{1,0:T(8,128)(2,1)} %get-tuple-element.128.here_ref, bf16[1792,384]{1,0:T(8,128)(2,1)S(1)} %collective-permute-done.13.far_ref), custom_call_target="tpu_custom_call" | custom-call | tf_op jit(solution)/shard_map/pallas_call | solution.py:234
  93.5 11.6 %conditional.6 = (bf16[128,48,128]{2,1,0:T(8,128)(2,1)S(1)}) conditional(s32[]{:T(128)} %bitcast.11, () %tuple.48, (s32[]{:T(128)}, bf16[128,48,128]{2,1,0:T(8,128)(2,1)}, bf16[2,3584,192]{2,1,0:T(8,128)(2,1)}, bf16[384,1792]{1,0:T(8,128)(2,1)}) %tuple.51), branch_computations={%region_8.9_spmd, %region_9.10_spmd} | conditional | flops 884748 | bytes 20201748 | solution.py:447
  93.5 2.6 %branch_1_fun.11.x_ref = bf16[384,1792]{1,0:T(8,128)(2,1)S(1)} custom-call(bf16[128,48,128]{2,1,0:T(8,128)(2,1)} %get-tuple-element.107.x_ref), custom_call_target="tpu_custom_call" | custom-call | tf_op jit(solution)/shard_map/cond/branch_1_fun/pallas_call | solution.py:283
  96.9 2.5 %branch_1_fun.12.refs_0_ = f32[2,384,192]{2,1,0:T(8,128)S(1)} custom-call(s32[1]{0:T(128)} %bitcast.3._.core_ref, bf16[384,1792]{1,0:T(8,128)(2,1)S(1)} %branch_1_fun.11.x_ref, bf16[2,3584,192]{2,1,0:T(8,128)(2,1)} %get-tuple-element.108.w_ref), custom_call_target="tpu_custom_call" | custom-call | tf_op jit(solution)/shard_map/cond/branch_1_fun/pallas_call | solution.py:310
  102.0 2.9 %branch_1_fun.14 = bf16[128,48,128]{2,1,0:T(8,128)(2,1)S(1)} custom-call(s32[1]{0:T(128)} %bitcast.3._.core_ref, bf16[192,384]{1,0:T(8,128)(2,1)S(1)} %fusion.h_ref, bf16[192,384]{1,0:T(8,128)(2,1)S(1)} %collective-permute-done.6.o_ref, bf16[384,1792]{1,0:T(8,128)(2,1)} %get-tuple-element.109.w_ref), custom_call_target="tpu_custom_call" | custom-call | tf_op jit(solution)/shard_map/cond/branch_1_fun/pallas_call | solution.py:342
  105.1 63.3 %conditional.7 = (bf16[16,1792]{1,0:T(8,128)(2,1)S(1)}, bf16[2,32,512]{2,1,0:T(8,128)(2,1)S(1)}) conditional(s32[]{:T(128)} %bitcast.11, () %tuple.47, (f32[16,8]{0,1:T(8,128)S(1)}, pred[16,8,32]{2,1,0:T(8,128)(4,1)S(1)}, f32[3,16,128]{1,2,0:T(8,128)S(1)}, bf16[128,48,128]{2,1,0:T(8,128)(2,1)S(1)}, bf16[256,640]{1,0:T(8,128)(2,1)}, ...), branch_computations={%region_10.11_spmd, %region_11.13_spmd} | conditional | flops 490436 | bytes 14075898 | solution.py:447
  106.3 17.5 %all-to-all-start.1 = ((bf16[128,48,128]{2,1,0:T(8,128)(2,1)}), bf16[128,48,128]{2,1,0:T(8,128)(2,1)S(1)}, u32[]{:S(2)}, u32[]{:S(2)}) async-start(bf16[128,48,128]{2,1,0:T(8,128)(2,1)} %copy-done.3), calls=%async_computation.1 | async-start | bytes 3145728 | tf_op jit(solution)/shard_map/cond/branch_1_fun/all_to_all | solution.py:426
  124.9 7.4 %collective-permute-start.7 = (bf16[64,640]{1,0:T(8,128)(2,1)S(1)}, bf16[64,640]{1,0:T(8,128)(2,1)S(1)}, u32[]{:S(2)}, u32[]{:S(2)}) collective-permute-start(bf16[64,640]{1,0:T(8,128)(2,1)S(1)} %get-tuple-element.175), channel_id=1, source_target_pairs={{0,128},{4,132},{8,136},{12,140},{16,144},{20,148},{24,152},{28,15... | collective-permute-start | bytes 245768 | tf_op jit(solution)/shard_map/cond/branch_1_fun/ppermute | solution.py:430
  136.0 21.0 %collective-permute-done.7 = bf16[64,640]{1,0:T(8,128)(2,1)S(1)} collective-permute-done((bf16[64,640]{1,0:T(8,128)(2,1)S(1)}, bf16[64,640]{1,0:T(8,128)(2,1)S(1)}, u32[]{:S(2)}, u32[]{:S(2)}) %collective-permute-start.7) | collective-permute-done | bytes 81952 | tf_op jit(solution)/shard_map/cond/branch_1_fun/ppermute | solution.py:430
  157.0 3.1 %collective-permute-done.9 = bf16[64,640]{1,0:T(8,128)(2,1)S(1)} collective-permute-done((bf16[64,640]{1,0:T(8,128)(2,1)S(1)}, bf16[64,640]{1,0:T(8,128)(2,1)S(1)}, u32[]{:S(2)}, u32[]{:S(2)}) %collective-permute-start.9) | collective-permute-done | bytes 81952 | tf_op jit(solution)/shard_map/cond/branch_1_fun/ppermute | solution.py:430
  161.3 6.1 %all-to-all-done.1.x_ref = bf16[128,48,128]{2,1,0:T(8,128)(2,1)S(1)} async-done(((bf16[128,48,128]{2,1,0:T(8,128)(2,1)}), bf16[128,48,128]{2,1,0:T(8,128)(2,1)S(1)}, u32[]{:S(2)}, u32[]{:S(2)}) %all-to-all-start.1) | async-done | bytes 1572896 | tf_op jit(solution)/shard_map/cond/branch_1_fun/all_to_all | solution.py:426
  (91 shorter events, 36.9 us)
Async XLA Ops:
  2.9 14.5 %collective-permute-start.10 = (bf16[592,128]{1,0:T(8,128)(2,1)}, bf16[592,128]{1,0:T(8,128)(2,1)S(1)}, u32[]{:S(2)}, u32[]{:S(2)}) collective-permute-start(bf16[592,128]{1,0:T(8,128)(2,1)} %shard_map.101.refs_0_), channel_id=1, source_target_pairs={{128,0},{132,4},{136,8},{140,12},{144,16},{148,20},{152,24},{156,2... | collective-permute-start | bytes 454664 | tf_op jit(solution)/shard_map/ppermute | solution.py:397
  4.2 13.2 %collective-permute-start.11 = (bf16[592,128]{1,0:T(8,128)(2,1)}, bf16[592,128]{1,0:T(8,128)(2,1)S(1)}, u32[]{:S(2)}, u32[]{:S(2)}) collective-permute-start(bf16[592,128]{1,0:T(8,128)(2,1)} %shard_map.101.refs_0_), channel_id=1, source_target_pairs={{256,0},{260,4},{264,8},{268,12},{272,16},{276,20},{280,24},{284,2... | collective-permute-start | bytes 454664 | tf_op jit(solution)/shard_map/ppermute | solution.py:397
  5.5 14.2 %collective-permute-start.12 = (bf16[592,128]{1,0:T(8,128)(2,1)}, bf16[592,128]{1,0:T(8,128)(2,1)S(1)}, u32[]{:S(2)}, u32[]{:S(2)}) collective-permute-start(bf16[592,128]{1,0:T(8,128)(2,1)} %shard_map.101.refs_0_), channel_id=1, source_target_pairs={{384,0},{388,4},{392,8},{396,12},{400,16},{404,20},{408,24},{412,2... | collective-permute-start | bytes 454664 | tf_op jit(solution)/shard_map/ppermute | solution.py:397
  17.4 2.3 %copy-start.6 = (bf16[592,128]{1,0:T(8,128)(2,1)}, bf16[592,128]{1,0:T(8,128)(2,1)S(1)}, u32[]{:S(2)}) copy-start(bf16[592,128]{1,0:T(8,128)(2,1)S(1)} %collective-permute-done.10.refs_1_) | copy-start | bytes 454660
  17.4 2.3 %copy-start.7 = (bf16[592,128]{1,0:T(8,128)(2,1)}, bf16[592,128]{1,0:T(8,128)(2,1)S(1)}, u32[]{:S(2)}) copy-start(bf16[592,128]{1,0:T(8,128)(2,1)S(1)} %collective-permute-done.11.refs_2_) | copy-start | bytes 454660
  21.5 3.7 %copy-start.13 = (s32[1,32]{1,0:T(1,128)S(1)}, s32[1,32]{1,0:T(1,128)}, u32[]{:S(2)}) copy-start(s32[1,32]{1,0:T(1,128)} %param.25) | copy-start | bytes 388
  24.5 64.7 %collective-permute-start.13 = (bf16[1792,384]{1,0:T(8,128)(2,1)S(1)}, bf16[1792,384]{1,0:T(8,128)(2,1)S(1)}, u32[]{:S(2)}, u32[]{:S(2)}) collective-permute-start(bf16[1792,384]{1,0:T(8,128)(2,1)S(1)} %shard_map.103), channel_id=1, source_target_pairs={{128,130},{129,131},{130,128},{131,129},{132,134},{133,135},{134,1... | collective-permute-start | bytes 4128776 | tf_op jit(solution)/shard_map/ppermute | solution.py:381
  26.0 63.2 %all-to-all-start = ((bf16[128,48,128]{2,1,0:T(8,128)(2,1)}), bf16[128,48,128]{2,1,0:T(8,128)(2,1)}, u32[]{:S(2)}, u32[]{:S(2)}) async-start(bf16[128,48,128]{2,1,0:T(8,128)(2,1)} %get-tuple-element.95), calls=%async_computation | async-start | bytes 3145728 | tf_op jit(solution)/shard_map/cond/branch_1_fun/all_to_all | solution.py:404
  42.7 4.1 %collective-permute-start = (bf16[4,592,128]{2,1,0:T(8,128)(2,1)S(1)}, bf16[4,592,128]{2,1,0:T(8,128)(2,1)}, u32[]{:S(2)}, u32[]{:S(2)}) collective-permute-start(bf16[4,592,128]{2,1,0:T(8,128)(2,1)S(1)} %get-tuple-element.101), channel_id=1, source_target_pairs={{0,1},{1,0},{2,3},{3,2},{4,5},{5,4},{6,7},{7,6},{8,9},{9,8},{10,11... | collective-permute-start | bytes 1818632 | tf_op jit(solution)/shard_map/cond/branch_1_fun/ppermute | solution.py:381
  58.1 17.0 %collective-permute-start.1 = (bf16[256,640]{1,0:T(8,128)(2,1)}, bf16[256,640]{1,0:T(8,128)(2,1)S(1)}, u32[]{:S(2)}, u32[]{:S(2)}) collective-permute-start(bf16[256,640]{1,0:T(8,128)(2,1)} %get-tuple-element.103), channel_id=1, source_target_pairs={{0,1},{1,0},{2,3},{3,2},{4,5},{5,4},{6,7},{7,6},{8,9},{9,8},{10,11... | collective-permute-start | bytes 983048 | tf_op jit(solution)/shard_map/cond/branch_1_fun/ppermute | solution.py:381
  60.2 19.2 %collective-permute-start.2 = (bf16[256,640]{1,0:T(8,128)(2,1)}, bf16[256,640]{1,0:T(8,128)(2,1)S(1)}, u32[]{:S(2)}, u32[]{:S(2)}) collective-permute-start(bf16[256,640]{1,0:T(8,128)(2,1)} %get-tuple-element.104), channel_id=1, source_target_pairs={{0,2},{1,3},{2,0},{3,1},{4,6},{5,7},{6,4},{7,5},{8,10},{9,11},{10,... | collective-permute-start | bytes 983048 | tf_op jit(solution)/shard_map/cond/branch_1_fun/ppermute | solution.py:381
  63.8 22.9 %collective-permute-start.3 = (bf16[256,640]{1,0:T(8,128)(2,1)}, bf16[256,640]{1,0:T(8,128)(2,1)S(1)}, u32[]{:S(2)}, u32[]{:S(2)}) collective-permute-start(bf16[256,640]{1,0:T(8,128)(2,1)} %get-tuple-element.105), channel_id=1, source_target_pairs={{0,3},{1,2},{2,1},{3,0},{4,7},{5,6},{6,5},{7,4},{8,11},{9,10},{10,... | collective-permute-start | bytes 983048 | tf_op jit(solution)/shard_map/cond/branch_1_fun/ppermute | solution.py:381
  93.5 11.6 %copy-start.4 = (bf16[2,128,576]{1,2,0:T(8,128)(2,1)S(1)}, bf16[2,128,576]{1,2,0:T(8,128)(2,1)}, u32[]{:S(2)}) copy-start(bf16[2,128,576]{1,2,0:T(8,128)(2,1)} %param.19) | copy-start | bytes 884740
  93.5 11.6 %copy-start.5 = (f32[3,16,128]{1,2,0:T(8,128)S(1)}, f32[3,16,128]{1,2,0:T(8,128)}, u32[]{:S(2)}) copy-start(f32[3,16,128]{1,2,0:T(8,128)} %pad.8) | copy-start | bytes 73732
  93.5 11.6 %copy-start.11 = (bf16[2,576]{1,0:T(2,128)(2,1)S(1)}, bf16[2,576]{1,0:T(2,128)(2,1)}, u32[]{:S(2)}) copy-start(bf16[2,576]{1,0:T(2,128)(2,1)} %param.20) | copy-start | bytes 6916
  93.5 11.6 %copy-start.12 = (f32[16,8]{0,1:T(8,128)S(1)}, f32[16,8]{0,1:T(8,128)}, u32[]{:S(2)}) copy-start(f32[16,8]{0,1:T(8,128)} %param.24) | copy-start | bytes 1540
  96.1 3.3 %collective-permute-start.4 = (bf16[384,1792]{1,0:T(8,128)(2,1)S(1)}, bf16[384,1792]{1,0:T(8,128)(2,1)S(1)}, u32[]{:S(2)}, u32[]{:S(2)}) collective-permute-start(bf16[384,1792]{1,0:T(8,128)(2,1)S(1)} %branch_1_fun.11.x_ref), channel_id=1, source_target_pairs={{128,129},{129,128},{130,131},{131,130},{132,133},{133,132},{134,1... | collective-permute-start | bytes 4128776 | tf_op jit(solution)/shard_map/cond/branch_1_fun/ppermute | solution.py:381
  96.9 2.6 %copy-start.1 = (bf16[2,3584,192]{2,1,0:T(8,128)(2,1)S(1)}, bf16[2,3584,192]{2,1,0:T(8,128)(2,1)}, u32[]{:S(2)}) copy-start(bf16[2,3584,192]{2,1,0:T(8,128)(2,1)} %get-tuple-element.108.w_ref) | copy-start | bytes 8257540 | tf_op jit(solution)/shard_map/cond
  100.4 0.7 collective-permute-start.5
  101.3 0.7 collective-permute-start.6
  106.3 61.0 %all-to-all-start.1 = ((bf16[128,48,128]{2,1,0:T(8,128)(2,1)}), bf16[128,48,128]{2,1,0:T(8,128)(2,1)S(1)}, u32[]{:S(2)}, u32[]{:S(2)}) async-start(bf16[128,48,128]{2,1,0:T(8,128)(2,1)} %copy-done.3), calls=%async_computation.1 | async-start | bytes 3145728 | tf_op jit(solution)/shard_map/cond/branch_1_fun/all_to_all | solution.py:426
  124.9 32.1 %collective-permute-start.7 = (bf16[64,640]{1,0:T(8,128)(2,1)S(1)}, bf16[64,640]{1,0:T(8,128)(2,1)S(1)}, u32[]{:S(2)}, u32[]{:S(2)}) collective-permute-start(bf16[64,640]{1,0:T(8,128)(2,1)S(1)} %get-tuple-element.175), channel_id=1, source_target_pairs={{0,128},{4,132},{8,136},{12,140},{16,144},{20,148},{24,152},{28,15... | collective-permute-start | bytes 245768 | tf_op jit(solution)/shard_map/cond/branch_1_fun/ppermute | solution.py:430
  132.3 24.7 %collective-permute-start.8 = (bf16[64,640]{1,0:T(8,128)(2,1)S(1)}, bf16[64,640]{1,0:T(8,128)(2,1)S(1)}, u32[]{:S(2)}, u32[]{:S(2)}) collective-permute-start(bf16[64,640]{1,0:T(8,128)(2,1)S(1)} %get-tuple-element.176), channel_id=1, source_target_pairs={{0,256},{4,260},{8,264},{12,268},{16,272},{20,276},{24,280},{28,28... | collective-permute-start | bytes 245768 | tf_op jit(solution)/shard_map/cond/branch_1_fun/ppermute | solution.py:430
  133.6 26.5 %collective-permute-start.9 = (bf16[64,640]{1,0:T(8,128)(2,1)S(1)}, bf16[64,640]{1,0:T(8,128)(2,1)S(1)}, u32[]{:S(2)}, u32[]{:S(2)}) collective-permute-start(bf16[64,640]{1,0:T(8,128)(2,1)S(1)} %get-tuple-element.177), channel_id=1, source_target_pairs={{0,384},{4,388},{8,392},{12,396},{16,400},{20,404},{24,408},{28,41... | collective-permute-start | bytes 245768 | tf_op jit(solution)/shard_map/cond/branch_1_fun/ppermute | solution.py:430
  (6 other events, 5.2 us)

commit v4 on v3

--- a/solution.py
+++ b/solution.py
@@ -208,7 +208,7 @@
     )(part.reshape(1).astype(jnp.int32), store, earlier)
 
 
-def weights_kernel(tp_ref, here_ref, far_ref, w_ref, mark_ref):
+def weights_kernel(tp_ref, here_ref, far_ref, _, w_ref, mark_ref):
     mark_ref[...] = jnp.zeros_like(mark_ref)
 
     def fill(refs):
@@ -230,13 +230,13 @@
         fill((far_ref, here_ref))
 
 
-def arrange(part, here, far):
+def arrange(part, here, far, earlier):
     return pl.pallas_call(
         weights_kernel,
-        in_specs=[pl.BlockSpec(memory_space=pltpu.SMEM), whole, whole],
+        in_specs=[pl.BlockSpec(memory_space=pltpu.SMEM), whole, whole, after],
         out_shape=[jax.ShapeDtypeStruct((2, 2 * DQ, 2 * HD), bf16), jax.ShapeDtypeStruct((8, 128), f32)],
         compiler_params=pltpu.CompilerParams(vmem_limit_bytes=VM),
-    )(part.reshape(1).astype(jnp.int32), here, far)
+    )(part.reshape(1).astype(jnp.int32), here, far, earlier)
 
 
 def join_kernel(p0_ref, p1_ref, p2_ref, p3_ref, out_ref):
@@ -388,8 +388,11 @@
     keep = (hits == 1) & (rank < capacity[0][None, :])
     slots = jnp.arange(CAP, dtype=jnp.int32)
     pick = (keep[None] & (rank[None] == slots[:, None, None])).astype(f32)
-    spread = jnp.pad(jnp.repeat(pick, 3, axis=2), ((0, 0), (0, 0), (servers, 0)))
-    sel = jnp.swapaxes(spread, 1, 2).astype(bf16)
+
+    def for_holders(value):
+        return jnp.pad(jnp.repeat(value, 3, axis=2), ((0, 0), (0, 0), (servers, 0)))
+
+    sel = jnp.swapaxes(for_holders(pick), 1, 2).astype(bf16)
 
     asked = ask(part, cached_len, jnp.swapaxes(queries, 1, 2))
     mine = [asked]
@@ -416,6 +419,7 @@
     def experts_part():
         slab = slots_of(arrived)
         beside = across(slab, 1, servers, groups)
+        weights, _ = arrange(part, here, far, slab[:16, :128])
         partial = project(core, slab, weights)
         partial = project(1 - core, beside, weights, partial)
         partial = partial.astype(f32) + across(partial, 2, servers, groups).astype(f32)
@@ -437,7 +441,7 @@
         own, others = jnp.exp(own - top), jnp.exp(others - top)
         attended = (others * returned[:, :, :LATENT] + own * new_latent[:, None, :LATENT].astype(f32)) / (own + others)
 
-        scaled = spread * jnp.pad(jnp.repeat(gate_of, 3, axis=1), ((0, 0), (servers, 0)))[None]
+        scaled = for_holders(pick * gate_of[None])
         high = lax.reduce_precision(scaled, 8, 7)
         weight = jnp.concatenate([high, scaled - high], axis=1).astype(bf16)
         return combine(weight, back), attended.astype(bf16)
@@ -449,7 +453,6 @@
         )
 
     arrived, here, down, answer = held(window)
-    weights, _ = arrange(part, here, far)
     result = held(experts_part)
     mixed, attended = held(way_back)
 

time: 170 us -> 168 us (0.988)
  Pallas kernels: 43.6 us -> 40.9 us
  starting transfers between devices: 62 us -> 64.1 us
  waiting for transfers between devices: 50.3 us -> 48.4 us
    unnamed x25 -> x19, local copies, waits for them, and re-layouts: 4.09 us -> 2.9 us
  transfers between devices with their start and end apart: 16 -> 16, of which waited for: 8 -> 8; matrix products, arithmetic and copies ran while one was open for 4% -> 4% of each run, Pallas kernels for 15% -> 17%
where the time goes in v4:
time: 168 us; the launch traced here: 166 us
  starting transfers between devices  64.1 us (38%)
  waiting for transfers between devices  48.4 us (29%)
  Pallas kernels  40.9 us (24%)
  local copies, waits for them, and re-layouts  9.08 us (5%)
  other arithmetic  2.41 us (1%)
    ppermute x3, waiting for transfers between devices, way_back(): lax.ppermute(shares[k], 'sec', [(a, k * servers + a) for a in range(serve...  22.8 us
    all_to_all x1, starting transfers between devices, way_back(): lax.all_to_all(result, 'sec', split_axis=0, concat_axis=0, tiled=True)  17.6 us
    all_to_all x1, starting transfers between devices, window(): lax.all_to_all(outgoing, 'sec', split_axis=0, concat_axis=0, tiled=True)  17.4 us
    ppermute x8, starting transfers between devices, across(): lax.ppermute(value, both, [(4 * q + t, 4 * q + (t ^ d)) for q in range(fi...  14 us
    ppermute x8, waiting for transfers between devices, across(): lax.ppermute(value, both, [(4 * q + t, 4 * q + (t ^ d)) for q in range(fi...  13.8 us
    pallas_call x1, Pallas kernels, attend(): pl.pallas_call(attend_kernel, grid_spec=pltpu.PrefetchScalarGridSpec(num_...  11.3 us
    ppermute x3, starting transfers between devices, way_back(): lax.ppermute(shares[k], 'sec', [(a, k * servers + a) for a in range(serve...  11.3 us
    pallas_call x2, Pallas kernels, unpack(): pl.pallas_call(unpack_kernel, grid_spec=pltpu.PrefetchScalarGridSpec(num_...  10.1 us
  transfers between devices with their start and end apart: 16, of which 8 were waited for; matrix products, arithmetic and copies ran while one was open for 4% of the time, Pallas kernels for 17%

profile of v4, /device:TPU:8, one launch (start us, length us, event | category | flops | bytes accessed | tf_op | source)
XLA Modules:
  0.0 166.5 jit_solution(16620755635439773754)
XLA Ops:
  9.5 3.1 %shard_map.100 = bf16[128,48,128]{2,1,0:T(8,128)(2,1)} custom-call(bf16[3,128,16]{2,1,0:T(8,128)(2,1)S(1)} %pad_bitcast_fusion.sel_ref, bf16[16,1792]{1,0:T(8,128)(2,1)S(1)} %copy-done), custom_call_target="tpu_custom_call" | custom-call | tf_op jit(solution)/shard_map/pallas_call | solution.py:63
  13.9 3.5 %collective-permute-done.10.refs_1_ = bf16[592,128]{1,0:T(8,128)(2,1)S(1)} collective-permute-done((bf16[592,128]{1,0:T(8,128)(2,1)}, bf16[592,128]{1,0:T(8,128)(2,1)S(1)}, u32[]{:S(2)}, u32[]{:S(2)}) %collective-permute-start.10) | collective-permute-done | bytes 151584 | tf_op jit(solution)/shard_map/ppermute | solution.py:400
  17.4 2.3 %collective-permute-done.12.refs_3_ = bf16[592,128]{1,0:T(8,128)(2,1)S(1)} collective-permute-done((bf16[592,128]{1,0:T(8,128)(2,1)}, bf16[592,128]{1,0:T(8,128)(2,1)S(1)}, u32[]{:S(2)}, u32[]{:S(2)}) %collective-permute-start.12) | collective-permute-done | bytes 151584 | tf_op jit(solution)/shard_map/ppermute | solution.py:400
  21.5 2.9 %shard_map.103 = bf16[1792,384]{1,0:T(8,128)(2,1)S(1)} custom-call(s32[1]{0:T(128)} %bitcast.15.tp_ref, bf16[1,1,2359296]{2,1,0:T(2,128)(2,1)} %s_ref.1, bf16[16,128]{1,0:T(8,128)(2,1)S(1)} %slice_bitcast_fusion.1._), custom_call_target="tpu_custom_call" | custom-call | tf_op jit(solution)/shard_map/pallas_call | solution.py:197
  25.3 63.9 %conditional.5 = (bf16[128,48,128]{2,1,0:T(8,128)(2,1)}, bf16[1792,384]{1,0:T(8,128)(2,1)}, bf16[384,1792]{1,0:T(8,128)(2,1)}, bf16[256,640]{1,0:T(8,128)(2,1)}) conditional(s32[]{:T(128)} %bitcast.12, () %tuple.49, (bf16[128,48,128]{2,1,0:T(8,128)(2,1)}, s32[]{:T(128)}, bf16[1,1,2359296]{2,1,0:T(2,128)(2,1)}, s32[]{:T(128)}, ...), branch_computations={%region_2.3_spmd, %region_3.8_spmd} | conditional | flops 2 | bytes 12722536 | solution.py:451
  25.3 17.4 %all-to-all-start = ((bf16[128,48,128]{2,1,0:T(8,128)(2,1)}), bf16[128,48,128]{2,1,0:T(8,128)(2,1)}, u32[]{:S(2)}, u32[]{:S(2)}) async-start(bf16[128,48,128]{2,1,0:T(8,128)(2,1)} %get-tuple-element.98), calls=%async_computation | async-start | bytes 3145728 | tf_op jit(solution)/shard_map/cond/branch_1_fun/all_to_all | solution.py:407
  46.8 11.3 %conditional = ((bf16[256,640]{1,0:T(8,128)(2,1)}, bf16[256,640]{1,0:T(8,128)(2,1)}, bf16[256,640]{1,0:T(8,128)(2,1)}, bf16[256,640]{1,0:T(8,128)(2,1)})) conditional(s32[]{:T(128)} %convert_element_type.41, () %tuple.33, (s32[]{:T(128)}, bf16[1,1,2359296]{2,1,0:T(2,128)(2,1)}, bf16[4,592,128]{2,1,0:T(8,128)(2,1)S(1)}, ...), branch_computations={%region_4.4_spmd, %region_5.5_spmd} | conditional | bytes 1310768 | solution.py:410
  46.8 11.3 %branch_1_fun.9 = (bf16[256,640]{1,0:T(8,128)(2,1)}, bf16[256,640]{1,0:T(8,128)(2,1)}, bf16[256,640]{1,0:T(8,128)(2,1)}, bf16[256,640]{1,0:T(8,128)(2,1)}) custom-call(s32[1]{0:T(128)} %bitcast.tp_ref, bf16[1,1,2359296]{2,1,0:T(2,128)(2,1)} %get-tuple-element.91.s_ref, bf16[4,592,128]{2,1,0:T(8,128)(2,1)S(1)} %get-tuple-element.92.mine_ref, ...), custom_call_target="tpu_custom_call" | custom-call | tf_op jit(solution)/shard_map/cond/branch_1_fun/cond/branch_1_fun/pallas_call | solution.py:146
  60.2 3.6 %collective-permute-start.2 = (bf16[256,640]{1,0:T(8,128)(2,1)}, bf16[256,640]{1,0:T(8,128)(2,1)S(1)}, u32[]{:S(2)}, u32[]{:S(2)}) collective-permute-start(bf16[256,640]{1,0:T(8,128)(2,1)} %get-tuple-element.107), channel_id=1, source_target_pairs={{0,2},{1,3},{2,0},{3,1},{4,6},{5,7},{6,4},{7,5},{8,10},{9,11},{10,... | collective-permute-start | bytes 983048 | tf_op jit(solution)/shard_map/cond/branch_1_fun/ppermute | solution.py:381
  63.9 3.4 %collective-permute-start.3 = (bf16[256,640]{1,0:T(8,128)(2,1)}, bf16[256,640]{1,0:T(8,128)(2,1)S(1)}, u32[]{:S(2)}, u32[]{:S(2)}) collective-permute-start(bf16[256,640]{1,0:T(8,128)(2,1)} %get-tuple-element.108), channel_id=1, source_target_pairs={{0,3},{1,2},{2,1},{3,0},{4,7},{5,6},{6,5},{7,4},{8,11},{9,10},{10,... | collective-permute-start | bytes 983048 | tf_op jit(solution)/shard_map/cond/branch_1_fun/ppermute | solution.py:381
  67.9 7.2 %branch_1_fun.11 = (bf16[1792,384]{1,0:T(8,128)(2,1)}, bf16[384,1792]{1,0:T(8,128)(2,1)}) custom-call(s32[1]{0:T(128)} %bitcast.1.tp_ref, bf16[1,1,2359296]{2,1,0:T(2,128)(2,1)} %get-tuple-element.100.s_ref, bf16[16,128]{1,0:T(8,128)(2,1)S(1)} %slice_bitcast_fusion._), custom_call_target="tpu_custom_call" | custom-call | tf_op jit(solution)/shard_map/cond/branch_1_fun/pallas_call | solution.py:197
  75.1 4.3 %collective-permute-done.2 = bf16[256,640]{1,0:T(8,128)(2,1)S(1)} collective-permute-done((bf16[256,640]{1,0:T(8,128)(2,1)}, bf16[256,640]{1,0:T(8,128)(2,1)S(1)}, u32[]{:S(2)}, u32[]{:S(2)}) %collective-permute-start.2) | collective-permute-done | bytes 327712 | tf_op jit(solution)/shard_map/cond/branch_1_fun/ppermute | solution.py:381
  79.4 7.3 %collective-permute-done.3 = bf16[256,640]{1,0:T(8,128)(2,1)S(1)} collective-permute-done((bf16[256,640]{1,0:T(8,128)(2,1)}, bf16[256,640]{1,0:T(8,128)(2,1)S(1)}, u32[]{:S(2)}, u32[]{:S(2)}) %collective-permute-start.3) | collective-permute-done | bytes 327712 | tf_op jit(solution)/shard_map/cond/branch_1_fun/ppermute | solution.py:381
  86.7 2.4 %conditional.1 = (bf16[256,640]{1,0:T(8,128)(2,1)}) conditional(s32[]{:T(128)} %convert_element_type.41, () %tuple.32, (bf16[256,640]{1,0:T(8,128)(2,1)}, bf16[256,640]{1,0:T(8,128)(2,1)S(1)}, bf16[256,640]{1,0:T(8,128)(2,1)S(1)}, bf16[256,640]{1,0:T(8,128)(2,1)S(1)}) %tuple.35), branch_computations={%region_6.6_spmd, %region_7.7_spmd} | conditional | bytes 327690 | solution.py:416
  86.7 2.4 %branch_1_fun.10 = bf16[256,640]{1,0:T(8,128)(2,1)} custom-call(bf16[256,640]{1,0:T(8,128)(2,1)} %get-tuple-element.94.p0_ref, bf16[256,640]{1,0:T(8,128)(2,1)S(1)} %get-tuple-element.95.p1_ref, bf16[256,640]{1,0:T(8,128)(2,1)S(1)} %get-tuple-element.96.p2_ref, bf16[256,640]{1,0:T(8,128)(2,1)S(1)} %get-tuple-element.97.p3_ref), custom_call_target="tpu_custom_call" | custom-call | tf_op jit(solution)/shard_map/cond/branch_1_fun/cond/branch_1_fun/pallas_call | solution.py:264
  89.2 13.3 %conditional.6 = (bf16[128,48,128]{2,1,0:T(8,128)(2,1)S(1)}) conditional(s32[]{:T(128)} %bitcast.12, () %tuple.48, (s32[]{:T(128)}, bf16[128,48,128]{2,1,0:T(8,128)(2,1)}, bf16[1792,384]{1,0:T(8,128)(2,1)}, bf16[1792,384]{1,0:T(8,128)(2,1)S(1)}, bf16[384,1792]{1,0:T(8,128)(2,1)}) %tuple.51), branch_computations={%region_8.9_spmd, %region_9.10_spmd} | conditional | flops 884748 | bytes 20209968 | solution.py:451
  90.3 2.5 %branch_1_fun.12.x_ref = bf16[384,1792]{1,0:T(8,128)(2,1)S(1)} custom-call(bf16[128,48,128]{2,1,0:T(8,128)(2,1)} %get-tuple-element.110.x_ref), custom_call_target="tpu_custom_call" | custom-call | tf_op jit(solution)/shard_map/cond/branch_1_fun/pallas_call | solution.py:283
  93.6 3.5 %branch_1_fun.13 = (bf16[2,3584,192]{2,1,0:T(8,128)(2,1)S(1)}, f32[8,128]{1,0:T(8,128)}) custom-call(s32[1]{0:T(128)} %bitcast.5.tp_ref, bf16[1792,384]{1,0:T(8,128)(2,1)} %get-tuple-element.111.here_ref, bf16[1792,384]{1,0:T(8,128)(2,1)} %copy-done.3, bf16[16,128]{1,0:T(8,128)(2,1)S(1)} %slice.57._), custom_call_target="tpu_custom_call" | custom-call | tf_op jit(solution)/shard_map/cond/branch_1_fun/pallas_call | solution.py:234
  102.5 63.3 %conditional.7 = (bf16[16,1792]{1,0:T(8,128)(2,1)S(1)}, bf16[2,32,512]{2,1,0:T(8,128)(2,1)S(1)}) conditional(s32[]{:T(128)} %bitcast.12, () %tuple.47, (f32[16,8]{0,1:T(8,128)S(1)}, pred[16,8,32]{2,1,0:T(8,128)(4,1)S(1)}, f32[3,16,32]{1,2,0:T(8,128)S(1)}, bf16[128,48,128]{2,1,0:T(8,128)(2,1)S(1)}, bf16[256,640]{1,0:T(8,128)(2,1)}, ...), branch_computations={%region_10.11_spmd, %region_11.13_spmd} | conditional | flops 485828 | bytes 15257618 | solution.py:451
  103.7 17.6 %all-to-all-start.1 = ((bf16[128,48,128]{2,1,0:T(8,128)(2,1)}), bf16[128,48,128]{2,1,0:T(8,128)(2,1)S(1)}, u32[]{:S(2)}, u32[]{:S(2)}) async-start(bf16[128,48,128]{2,1,0:T(8,128)(2,1)} %copy-done.1), calls=%async_computation.1 | async-start | bytes 3145728 | tf_op jit(solution)/shard_map/cond/branch_1_fun/all_to_all | solution.py:430
  122.2 8.7 %collective-permute-start.9 = (bf16[64,640]{1,0:T(8,128)(2,1)S(1)}, bf16[64,640]{1,0:T(8,128)(2,1)S(1)}, u32[]{:S(2)}, u32[]{:S(2)}) collective-permute-start(bf16[64,640]{1,0:T(8,128)(2,1)S(1)} %get-tuple-element.180), channel_id=1, source_target_pairs={{0,384},{4,388},{8,392},{12,396},{16,400},{20,404},{24,408},{28,41... | collective-permute-start | bytes 245768 | tf_op jit(solution)/shard_map/cond/branch_1_fun/ppermute | solution.py:434
  134.6 19.7 %collective-permute-done.9 = bf16[64,640]{1,0:T(8,128)(2,1)S(1)} collective-permute-done((bf16[64,640]{1,0:T(8,128)(2,1)S(1)}, bf16[64,640]{1,0:T(8,128)(2,1)S(1)}, u32[]{:S(2)}, u32[]{:S(2)}) %collective-permute-start.9) | collective-permute-done | bytes 81952 | tf_op jit(solution)/shard_map/cond/branch_1_fun/ppermute | solution.py:434
  154.4 3.1 %collective-permute-done.7 = bf16[64,640]{1,0:T(8,128)(2,1)S(1)} collective-permute-done((bf16[64,640]{1,0:T(8,128)(2,1)S(1)}, bf16[64,640]{1,0:T(8,128)(2,1)S(1)}, u32[]{:S(2)}, u32[]{:S(2)}) %collective-permute-start.7) | collective-permute-done | bytes 81952 | tf_op jit(solution)/shard_map/cond/branch_1_fun/ppermute | solution.py:434
  158.7 6.1 %all-to-all-done.1.x_ref = bf16[128,48,128]{2,1,0:T(8,128)(2,1)S(1)} async-done(((bf16[128,48,128]{2,1,0:T(8,128)(2,1)}), bf16[128,48,128]{2,1,0:T(8,128)(2,1)S(1)}, u32[]{:S(2)}, u32[]{:S(2)}) %all-to-all-start.1) | async-done | bytes 1572896 | tf_op jit(solution)/shard_map/cond/branch_1_fun/all_to_all | solution.py:430
  (88 shorter events, 35.1 us)
Async XLA Ops:
  2.9 14.5 %collective-permute-start.10 = (bf16[592,128]{1,0:T(8,128)(2,1)}, bf16[592,128]{1,0:T(8,128)(2,1)S(1)}, u32[]{:S(2)}, u32[]{:S(2)}) collective-permute-start(bf16[592,128]{1,0:T(8,128)(2,1)} %shard_map.101.refs_0_), channel_id=1, source_target_pairs={{128,0},{132,4},{136,8},{140,12},{144,16},{148,20},{152,24},{156,2... | collective-permute-start | bytes 454664 | tf_op jit(solution)/shard_map/ppermute | solution.py:400
  4.2 13.2 %collective-permute-start.11 = (bf16[592,128]{1,0:T(8,128)(2,1)}, bf16[592,128]{1,0:T(8,128)(2,1)S(1)}, u32[]{:S(2)}, u32[]{:S(2)}) collective-permute-start(bf16[592,128]{1,0:T(8,128)(2,1)} %shard_map.101.refs_0_), channel_id=1, source_target_pairs={{256,0},{260,4},{264,8},{268,12},{272,16},{276,20},{280,24},{284,2... | collective-permute-start | bytes 454664 | tf_op jit(solution)/shard_map/ppermute | solution.py:400
  5.5 14.2 %collective-permute-start.12 = (bf16[592,128]{1,0:T(8,128)(2,1)}, bf16[592,128]{1,0:T(8,128)(2,1)S(1)}, u32[]{:S(2)}, u32[]{:S(2)}) collective-permute-start(bf16[592,128]{1,0:T(8,128)(2,1)} %shard_map.101.refs_0_), channel_id=1, source_target_pairs={{384,0},{388,4},{392,8},{396,12},{400,16},{404,20},{408,24},{412,2... | collective-permute-start | bytes 454664 | tf_op jit(solution)/shard_map/ppermute | solution.py:400
  17.4 2.3 %copy-start.5 = (bf16[592,128]{1,0:T(8,128)(2,1)}, bf16[592,128]{1,0:T(8,128)(2,1)S(1)}, u32[]{:S(2)}) copy-start(bf16[592,128]{1,0:T(8,128)(2,1)S(1)} %collective-permute-done.10.refs_1_) | copy-start | bytes 454660
  17.4 2.3 %copy-start.6 = (bf16[592,128]{1,0:T(8,128)(2,1)}, bf16[592,128]{1,0:T(8,128)(2,1)S(1)}, u32[]{:S(2)}) copy-start(bf16[592,128]{1,0:T(8,128)(2,1)S(1)} %collective-permute-done.11.refs_2_) | copy-start | bytes 454660
  21.5 3.7 %copy-start.12 = (s32[1,32]{1,0:T(1,128)S(1)}, s32[1,32]{1,0:T(1,128)}, u32[]{:S(2)}) copy-start(s32[1,32]{1,0:T(1,128)} %param.25) | copy-start | bytes 388
  24.5 64.7 %collective-permute-start.13 = (bf16[1792,384]{1,0:T(8,128)(2,1)S(1)}, bf16[1792,384]{1,0:T(8,128)(2,1)S(1)}, u32[]{:S(2)}, u32[]{:S(2)}) collective-permute-start(bf16[1792,384]{1,0:T(8,128)(2,1)S(1)} %shard_map.103), channel_id=1, source_target_pairs={{128,130},{129,131},{130,128},{131,129},{132,134},{133,135},{134,1... | collective-permute-start | bytes 4128776 | tf_op jit(solution)/shard_map/ppermute | solution.py:381
  25.3 63.8 %all-to-all-start = ((bf16[128,48,128]{2,1,0:T(8,128)(2,1)}), bf16[128,48,128]{2,1,0:T(8,128)(2,1)}, u32[]{:S(2)}, u32[]{:S(2)}) async-start(bf16[128,48,128]{2,1,0:T(8,128)(2,1)} %get-tuple-element.98), calls=%async_computation | async-start | bytes 3145728 | tf_op jit(solution)/shard_map/cond/branch_1_fun/all_to_all | solution.py:407
  42.7 4.1 %collective-permute-start = (bf16[4,592,128]{2,1,0:T(8,128)(2,1)S(1)}, bf16[4,592,128]{2,1,0:T(8,128)(2,1)}, u32[]{:S(2)}, u32[]{:S(2)}) collective-permute-start(bf16[4,592,128]{2,1,0:T(8,128)(2,1)S(1)} %get-tuple-element.104), channel_id=1, source_target_pairs={{0,1},{1,0},{2,3},{3,2},{4,5},{5,4},{6,7},{7,6},{8,9},{9,8},{10,11... | collective-permute-start | bytes 1818632 | tf_op jit(solution)/shard_map/cond/branch_1_fun/ppermute | solution.py:381
  58.1 17.0 %collective-permute-start.1 = (bf16[256,640]{1,0:T(8,128)(2,1)}, bf16[256,640]{1,0:T(8,128)(2,1)S(1)}, u32[]{:S(2)}, u32[]{:S(2)}) collective-permute-start(bf16[256,640]{1,0:T(8,128)(2,1)} %get-tuple-element.106), channel_id=1, source_target_pairs={{0,1},{1,0},{2,3},{3,2},{4,5},{5,4},{6,7},{7,6},{8,9},{9,8},{10,11... | collective-permute-start | bytes 983048 | tf_op jit(solution)/shard_map/cond/branch_1_fun/ppermute | solution.py:381
  60.2 19.2 %collective-permute-start.2 = (bf16[256,640]{1,0:T(8,128)(2,1)}, bf16[256,640]{1,0:T(8,128)(2,1)S(1)}, u32[]{:S(2)}, u32[]{:S(2)}) collective-permute-start(bf16[256,640]{1,0:T(8,128)(2,1)} %get-tuple-element.107), channel_id=1, source_target_pairs={{0,2},{1,3},{2,0},{3,1},{4,6},{5,7},{6,4},{7,5},{8,10},{9,11},{10,... | collective-permute-start | bytes 983048 | tf_op jit(solution)/shard_map/cond/branch_1_fun/ppermute | solution.py:381
  63.9 22.9 %collective-permute-start.3 = (bf16[256,640]{1,0:T(8,128)(2,1)}, bf16[256,640]{1,0:T(8,128)(2,1)S(1)}, u32[]{:S(2)}, u32[]{:S(2)}) collective-permute-start(bf16[256,640]{1,0:T(8,128)(2,1)} %get-tuple-element.108), channel_id=1, source_target_pairs={{0,3},{1,2},{2,1},{3,0},{4,7},{5,6},{6,5},{7,4},{8,11},{9,10},{10,... | collective-permute-start | bytes 983048 | tf_op jit(solution)/shard_map/cond/branch_1_fun/ppermute | solution.py:381
  89.1 13.3 %copy-start.10 = (bf16[2,576]{1,0:T(2,128)(2,1)S(1)}, bf16[2,576]{1,0:T(2,128)(2,1)}, u32[]{:S(2)}) copy-start(bf16[2,576]{1,0:T(2,128)(2,1)} %param.20) | copy-start | bytes 6916
  89.2 13.3 %copy-start.11 = (f32[16,8]{0,1:T(8,128)S(1)}, f32[16,8]{0,1:T(8,128)}, u32[]{:S(2)}) copy-start(f32[16,8]{0,1:T(8,128)} %param.24) | copy-start | bytes 1540
  92.8 5.1 %collective-permute-start.4 = (bf16[384,1792]{1,0:T(8,128)(2,1)S(1)}, bf16[384,1792]{1,0:T(8,128)(2,1)S(1)}, u32[]{:S(2)}, u32[]{:S(2)}) collective-permute-start(bf16[384,1792]{1,0:T(8,128)(2,1)S(1)} %branch_1_fun.12.x_ref), channel_id=1, source_target_pairs={{128,129},{129,128},{130,131},{131,130},{132,133},{133,132},{134,1... | collective-permute-start | bytes 4128776 | tf_op jit(solution)/shard_map/cond/branch_1_fun/ppermute | solution.py:381
  99.0 1.7 %copy-start.2 = (bf16[384,1792]{1,0:T(8,128)(2,1)S(1)}, bf16[384,1792]{1,0:T(8,128)(2,1)}, u32[]{:S(2)}) copy-start(bf16[384,1792]{1,0:T(8,128)(2,1)} %get-tuple-element.114.w_ref) | copy-start | bytes 4128772 | tf_op jit(solution)/shard_map/cond
  99.0 0.8 collective-permute-start.5
  100.0 0.7 collective-permute-start.6
  102.5 1.2 copy-start.1
  103.7 30.3 %copy-start.4 = (bf16[2,128,576]{1,2,0:T(8,128)(2,1)S(1)}, bf16[2,128,576]{1,2,0:T(8,128)(2,1)}, u32[]{:S(2)}) copy-start(bf16[2,128,576]{1,2,0:T(8,128)(2,1)} %get-tuple-element.173) | copy-start | bytes 884740 | tf_op jit(solution)/shard_map/cond
  103.7 61.0 %all-to-all-start.1 = ((bf16[128,48,128]{2,1,0:T(8,128)(2,1)}), bf16[128,48,128]{2,1,0:T(8,128)(2,1)S(1)}, u32[]{:S(2)}, u32[]{:S(2)}) async-start(bf16[128,48,128]{2,1,0:T(8,128)(2,1)} %copy-done.1), calls=%async_computation.1 | async-start | bytes 3145728 | tf_op jit(solution)/shard_map/cond/branch_1_fun/all_to_all | solution.py:430
  122.2 32.1 %collective-permute-start.9 = (bf16[64,640]{1,0:T(8,128)(2,1)S(1)}, bf16[64,640]{1,0:T(8,128)(2,1)S(1)}, u32[]{:S(2)}, u32[]{:S(2)}) collective-permute-start(bf16[64,640]{1,0:T(8,128)(2,1)S(1)} %get-tuple-element.180), channel_id=1, source_target_pairs={{0,384},{4,388},{8,392},{12,396},{16,400},{20,404},{24,408},{28,41... | collective-permute-start | bytes 245768 | tf_op jit(solution)/shard_map/cond/branch_1_fun/ppermute | solution.py:434
  131.0 23.4 %collective-permute-start.8 = (bf16[64,640]{1,0:T(8,128)(2,1)S(1)}, bf16[64,640]{1,0:T(8,128)(2,1)S(1)}, u32[]{:S(2)}, u32[]{:S(2)}) collective-permute-start(bf16[64,640]{1,0:T(8,128)(2,1)S(1)} %get-tuple-element.179), channel_id=1, source_target_pairs={{0,256},{4,260},{8,264},{12,268},{16,272},{20,276},{24,280},{28,28... | collective-permute-start | bytes 245768 | tf_op jit(solution)/shard_map/cond/branch_1_fun/ppermute | solution.py:434
  132.3 25.2 %collective-permute-start.7 = (bf16[64,640]{1,0:T(8,128)(2,1)S(1)}, bf16[64,640]{1,0:T(8,128)(2,1)S(1)}, u32[]{:S(2)}, u32[]{:S(2)}) collective-permute-start(bf16[64,640]{1,0:T(8,128)(2,1)S(1)} %get-tuple-element.178), channel_id=1, source_target_pairs={{0,128},{4,132},{8,136},{12,140},{16,144},{20,148},{24,152},{28,15... | collective-permute-start | bytes 245768 | tf_op jit(solution)/shard_map/cond/branch_1_fun/ppermute | solution.py:434
  (5 other events, 3.9 us)

commit v5 on v4

--- a/solution.py
+++ b/solution.py
@@ -399,17 +399,18 @@
     for k in range(1, 4):
         mine.append(lax.ppermute(asked, "sec", [(k * servers + a, a) for a in range(servers)]))
     outgoing = dispatch(sel, rows)
-    mine = stack(mine, outgoing[0, :16])
-    (far,) = unpack(store, part, True, mine[0, :16])
+    received = jnp.concatenate([row[:16] for row in mine[1:]] + [outgoing[0, :16]], axis=0)
+    (far,) = unpack(store, part, True, received)
     far = across(far, 2, servers, groups)
 
     def window():
         arrived = lax.all_to_all(outgoing, "sec", split_axis=0, concat_axis=0, tiled=True)
-        other = across(mine, 1, 0, servers)
+        rows_here = stack(mine, received)
+        other = across(rows_here, 1, 0, servers)
         here, down = unpack(store, part, False, outgoing[0, :16])
         parts = lax.cond(
             serving,
-            lambda: tuple(attend(store, mine, other, part)),
+            lambda: tuple(attend(store, rows_here, other, part)),
             lambda: (jnp.zeros((256, PART), bf16),) * 4,
         )
         parts = [parts[0]] + [across(parts[d], d, 0, servers) for d in range(1, 4)]

time: 168 us -> 165 us (0.982)
  transfers between devices with their start and end apart: 16 -> 16, of which waited for: 8 -> 7; matrix products, arithmetic and copies ran while one was open for 4% -> 4% of each run, Pallas kernels for 17% -> 18%
where the time goes in v5:
time: 165 us; the launch traced here: 164 us
  starting transfers between devices  62.7 us (38%)
  waiting for transfers between devices  48.1 us (29%)
  Pallas kernels  40.2 us (24%)
  local copies, waits for them, and re-layouts  8.55 us (5%)
  other arithmetic  3.03 us (2%)
    ppermute x3, waiting for transfers between devices, way_back(): lax.ppermute(shares[k], 'sec', [(a, k * servers + a) for a in range(serve...  22.8 us
    all_to_all x1, starting transfers between devices, window(): lax.all_to_all(outgoing, 'sec', split_axis=0, concat_axis=0, tiled=True)  16.9 us
    all_to_all x1, starting transfers between devices, way_back(): lax.all_to_all(result, 'sec', split_axis=0, concat_axis=0, tiled=True)  16.6 us
    ppermute x8, starting transfers between devices, across(): lax.ppermute(value, both, [(4 * q + t, 4 * q + (t ^ d)) for q in range(fi...  14 us
    ppermute x8, waiting for transfers between devices, across(): lax.ppermute(value, both, [(4 * q + t, 4 * q + (t ^ d)) for q in range(fi...  13.6 us
    pallas_call x1, Pallas kernels, attend(): pl.pallas_call(attend_kernel, grid_spec=pltpu.PrefetchScalarGridSpec(num_...  11.3 us
    ppermute x3, starting transfers between devices, way_back(): lax.ppermute(shares[k], 'sec', [(a, k * servers + a) for a in range(serve...  11.3 us
    pallas_call x2, Pallas kernels, unpack(): pl.pallas_call(unpack_kernel, grid_spec=pltpu.PrefetchScalarGridSpec(num_...  10.1 us
  transfers between devices with their start and end apart: 16, of which 7 were waited for; matrix products, arithmetic and copies ran while one was open for 4% of the time, Pallas kernels for 18%

profile of v5, /device:TPU:8, one launch (start us, length us, event | category | flops | bytes accessed | tf_op | source)
XLA Modules:
  0.0 164.0 jit_solution(14977405557204338512)
XLA Ops:
  9.5 3.1 %shard_map.100 = bf16[128,48,128]{2,1,0:T(8,128)(2,1)} custom-call(bf16[3,128,16]{2,1,0:T(8,128)(2,1)S(1)} %pad_bitcast_fusion.sel_ref, bf16[16,1792]{1,0:T(8,128)(2,1)S(1)} %copy-done), custom_call_target="tpu_custom_call" | custom-call | tf_op jit(solution)/shard_map/pallas_call | solution.py:63
  13.2 5.6 %collective-permute-done.12 = bf16[592,128]{1,0:T(8,128)(2,1)S(1)} collective-permute-done((bf16[592,128]{1,0:T(8,128)(2,1)S(1)}, bf16[592,128]{1,0:T(8,128)(2,1)S(1)}, u32[]{:S(2)}, u32[]{:S(2)}) %collective-permute-start.12) | collective-permute-done | bytes 151584 | tf_op jit(solution)/shard_map/ppermute | solution.py:400
  19.6 2.9 %shard_map.102 = bf16[1792,384]{1,0:T(8,128)(2,1)S(1)} custom-call(s32[1]{0:T(128)} %bitcast.15.tp_ref, bf16[1,1,2359296]{2,1,0:T(2,128)(2,1)} %s_ref.1, bf16[64,128]{1,0:T(8,128)(2,1)S(1)} %pad_maximum_fusion.1._), custom_call_target="tpu_custom_call" | custom-call | tf_op jit(solution)/shard_map/pallas_call | solution.py:197
  23.3 64.3 %conditional.5 = (bf16[128,48,128]{2,1,0:T(8,128)(2,1)}, bf16[1792,384]{1,0:T(8,128)(2,1)}, bf16[384,1792]{1,0:T(8,128)(2,1)}, bf16[256,640]{1,0:T(8,128)(2,1)}) conditional(s32[]{:T(128)} %bitcast.12, () %tuple.49, (bf16[128,48,128]{2,1,0:T(8,128)(2,1)}, s32[]{:T(128)}, bf16[1,1,2359296]{2,1,0:T(2,128)(2,1)}, s32[]{:T(128)}, ...), branch_computations={%region_2.3_spmd, %region_3.8_spmd} | conditional | flops 2 | bytes 12722536 | solution.py:452
  23.4 16.9 %all-to-all-start = ((bf16[128,48,128]{2,1,0:T(8,128)(2,1)}), bf16[128,48,128]{2,1,0:T(8,128)(2,1)}, u32[]{:S(2)}, u32[]{:S(2)}) async-start(bf16[128,48,128]{2,1,0:T(8,128)(2,1)} %get-tuple-element.106), calls=%async_computation | async-start | bytes 3145728 | tf_op jit(solution)/shard_map/cond/branch_1_fun/all_to_all | solution.py:407
  43.3 2.1 %collective-permute-done = bf16[4,592,128]{2,1,0:T(8,128)(2,1)} collective-permute-done((bf16[4,592,128]{2,1,0:T(8,128)(2,1)S(1)}, bf16[4,592,128]{2,1,0:T(8,128)(2,1)}, u32[]{:S(2)}, u32[]{:S(2)}) %collective-permute-start) | collective-permute-done | bytes 606240 | tf_op jit(solution)/shard_map/cond/branch_1_fun/ppermute | solution.py:381
  45.4 11.3 %conditional = ((bf16[256,640]{1,0:T(8,128)(2,1)}, bf16[256,640]{1,0:T(8,128)(2,1)}, bf16[256,640]{1,0:T(8,128)(2,1)}, bf16[256,640]{1,0:T(8,128)(2,1)})) conditional(s32[]{:T(128)} %convert_element_type.41, () %tuple.33, (s32[]{:T(128)}, bf16[1,1,2359296]{2,1,0:T(2,128)(2,1)}, bf16[4,592,128]{2,1,0:T(8,128)(2,1)S(1)}, ...), branch_computations={%region_4.4_spmd, %region_5.5_spmd} | conditional | bytes 1310768 | solution.py:411
  45.4 11.3 %branch_1_fun.10 = (bf16[256,640]{1,0:T(8,128)(2,1)}, bf16[256,640]{1,0:T(8,128)(2,1)}, bf16[256,640]{1,0:T(8,128)(2,1)}, bf16[256,640]{1,0:T(8,128)(2,1)}) custom-call(s32[1]{0:T(128)} %bitcast.tp_ref, bf16[1,1,2359296]{2,1,0:T(2,128)(2,1)} %get-tuple-element.99.s_ref, bf16[4,592,128]{2,1,0:T(8,128)(2,1)S(1)} %get-tuple-element.100.mine_ref, ...), custom_call_target="tpu_custom_call" | custom-call | tf_op jit(solution)/shard_map/cond/branch_1_fun/cond/branch_1_fun/pallas_call | solution.py:146
  58.9 3.6 %collective-permute-start.2 = (bf16[256,640]{1,0:T(8,128)(2,1)}, bf16[256,640]{1,0:T(8,128)(2,1)S(1)}, u32[]{:S(2)}, u32[]{:S(2)}) collective-permute-start(bf16[256,640]{1,0:T(8,128)(2,1)} %get-tuple-element.119), channel_id=1, source_target_pairs={{0,2},{1,3},{2,0},{3,1},{4,6},{5,7},{6,4},{7,5},{8,10},{9,11},{10,... | collective-permute-start | bytes 983048 | tf_op jit(solution)/shard_map/cond/branch_1_fun/ppermute | solution.py:381
  62.5 3.4 %collective-permute-start.3 = (bf16[256,640]{1,0:T(8,128)(2,1)}, bf16[256,640]{1,0:T(8,128)(2,1)S(1)}, u32[]{:S(2)}, u32[]{:S(2)}) collective-permute-start(bf16[256,640]{1,0:T(8,128)(2,1)} %get-tuple-element.120), channel_id=1, source_target_pairs={{0,3},{1,2},{2,1},{3,0},{4,7},{5,6},{6,5},{7,4},{8,11},{9,10},{10,... | collective-permute-start | bytes 983048 | tf_op jit(solution)/shard_map/cond/branch_1_fun/ppermute | solution.py:381
  66.6 7.2 %branch_1_fun.12 = (bf16[1792,384]{1,0:T(8,128)(2,1)}, bf16[384,1792]{1,0:T(8,128)(2,1)}) custom-call(s32[1]{0:T(128)} %bitcast.1.tp_ref, bf16[1,1,2359296]{2,1,0:T(2,128)(2,1)} %get-tuple-element.108.s_ref, bf16[16,128]{1,0:T(8,128)(2,1)S(1)} %slice_bitcast_fusion._), custom_call_target="tpu_custom_call" | custom-call | tf_op jit(solution)/shard_map/cond/branch_1_fun/pallas_call | solution.py:197
  73.7 3.8 %collective-permute-done.2 = bf16[256,640]{1,0:T(8,128)(2,1)S(1)} collective-permute-done((bf16[256,640]{1,0:T(8,128)(2,1)}, bf16[256,640]{1,0:T(8,128)(2,1)S(1)}, u32[]{:S(2)}, u32[]{:S(2)}) %collective-permute-start.2) | collective-permute-done | bytes 327712 | tf_op jit(solution)/shard_map/cond/branch_1_fun/ppermute | solution.py:381
  77.5 7.7 %collective-permute-done.3 = bf16[256,640]{1,0:T(8,128)(2,1)S(1)} collective-permute-done((bf16[256,640]{1,0:T(8,128)(2,1)}, bf16[256,640]{1,0:T(8,128)(2,1)S(1)}, u32[]{:S(2)}, u32[]{:S(2)}) %collective-permute-start.3) | collective-permute-done | bytes 327712 | tf_op jit(solution)/shard_map/cond/branch_1_fun/ppermute | solution.py:381
  85.2 2.4 %conditional.1 = (bf16[256,640]{1,0:T(8,128)(2,1)}) conditional(s32[]{:T(128)} %convert_element_type.41, () %tuple.32, (bf16[256,640]{1,0:T(8,128)(2,1)}, bf16[256,640]{1,0:T(8,128)(2,1)S(1)}, bf16[256,640]{1,0:T(8,128)(2,1)S(1)}, bf16[256,640]{1,0:T(8,128)(2,1)S(1)}) %tuple.35), branch_computations={%region_6.6_spmd, %region_7.7_spmd} | conditional | bytes 327690 | solution.py:417
  85.2 2.4 %branch_1_fun.11 = bf16[256,640]{1,0:T(8,128)(2,1)} custom-call(bf16[256,640]{1,0:T(8,128)(2,1)} %get-tuple-element.102.p0_ref, bf16[256,640]{1,0:T(8,128)(2,1)S(1)} %get-tuple-element.103.p1_ref, bf16[256,640]{1,0:T(8,128)(2,1)S(1)} %get-tuple-element.104.p2_ref, bf16[256,640]{1,0:T(8,128)(2,1)S(1)} %get-tuple-element.105.p3_ref), custom_call_target="tpu_custom_call" | custom-call | tf_op jit(solution)/shard_map/cond/branch_1_fun/cond/branch_1_fun/pallas_call | solution.py:264
  87.7 13.3 %conditional.6 = (bf16[128,48,128]{2,1,0:T(8,128)(2,1)S(1)}) conditional(s32[]{:T(128)} %bitcast.12, () %tuple.48, (s32[]{:T(128)}, bf16[128,48,128]{2,1,0:T(8,128)(2,1)}, bf16[1792,384]{1,0:T(8,128)(2,1)}, bf16[1792,384]{1,0:T(8,128)(2,1)S(1)}, bf16[384,1792]{1,0:T(8,128)(2,1)}) %tuple.51), branch_computations={%region_8.9_spmd, %region_9.10_spmd} | conditional | flops 884748 | bytes 20209968 | solution.py:452
  88.8 2.5 %branch_1_fun.14.x_ref = bf16[384,1792]{1,0:T(8,128)(2,1)S(1)} custom-call(bf16[128,48,128]{2,1,0:T(8,128)(2,1)} %get-tuple-element.122.x_ref), custom_call_target="tpu_custom_call" | custom-call | tf_op jit(solution)/shard_map/cond/branch_1_fun/pallas_call | solution.py:283
  92.1 3.5 %branch_1_fun.15 = (bf16[2,3584,192]{2,1,0:T(8,128)(2,1)S(1)}, f32[8,128]{1,0:T(8,128)}) custom-call(s32[1]{0:T(128)} %bitcast.5.tp_ref, bf16[1792,384]{1,0:T(8,128)(2,1)} %get-tuple-element.123.here_ref, bf16[1792,384]{1,0:T(8,128)(2,1)} %copy-done.3, bf16[16,128]{1,0:T(8,128)(2,1)S(1)} %slice.65._), custom_call_target="tpu_custom_call" | custom-call | tf_op jit(solution)/shard_map/cond/branch_1_fun/pallas_call | solution.py:234
  101.0 62.4 %conditional.7 = (bf16[16,1792]{1,0:T(8,128)(2,1)S(1)}, bf16[2,32,512]{2,1,0:T(8,128)(2,1)S(1)}) conditional(s32[]{:T(128)} %bitcast.12, () %tuple.47, (f32[16,8]{0,1:T(8,128)S(1)}, pred[16,8,32]{2,1,0:T(8,128)(4,1)S(1)}, f32[3,16,32]{1,2,0:T(8,128)S(1)}, bf16[128,48,128]{2,1,0:T(8,128)(2,1)S(1)}, bf16[256,640]{1,0:T(8,128)(2,1)}, ...), branch_computations={%region_10.11_spmd, %region_11.13_spmd} | conditional | flops 485828 | bytes 15257618 | solution.py:452
  102.2 16.6 %all-to-all-start.1 = ((bf16[128,48,128]{2,1,0:T(8,128)(2,1)}), bf16[128,48,128]{2,1,0:T(8,128)(2,1)S(1)}, u32[]{:S(2)}, u32[]{:S(2)}) async-start(bf16[128,48,128]{2,1,0:T(8,128)(2,1)} %copy-done.1), calls=%async_computation.1 | async-start | bytes 3145728 | tf_op jit(solution)/shard_map/cond/branch_1_fun/all_to_all | solution.py:431
  119.8 8.7 %collective-permute-start.9 = (bf16[64,640]{1,0:T(8,128)(2,1)S(1)}, bf16[64,640]{1,0:T(8,128)(2,1)S(1)}, u32[]{:S(2)}, u32[]{:S(2)}) collective-permute-start(bf16[64,640]{1,0:T(8,128)(2,1)S(1)} %get-tuple-element.192), channel_id=1, source_target_pairs={{0,384},{4,388},{8,392},{12,396},{16,400},{20,404},{24,408},{28,41... | collective-permute-start | bytes 245768 | tf_op jit(solution)/shard_map/cond/branch_1_fun/ppermute | solution.py:435
  132.2 19.7 %collective-permute-done.9 = bf16[64,640]{1,0:T(8,128)(2,1)S(1)} collective-permute-done((bf16[64,640]{1,0:T(8,128)(2,1)S(1)}, bf16[64,640]{1,0:T(8,128)(2,1)S(1)}, u32[]{:S(2)}, u32[]{:S(2)}) %collective-permute-start.9) | collective-permute-done | bytes 81952 | tf_op jit(solution)/shard_map/cond/branch_1_fun/ppermute | solution.py:435
  151.9 3.1 %collective-permute-done.7 = bf16[64,640]{1,0:T(8,128)(2,1)S(1)} collective-permute-done((bf16[64,640]{1,0:T(8,128)(2,1)S(1)}, bf16[64,640]{1,0:T(8,128)(2,1)S(1)}, u32[]{:S(2)}, u32[]{:S(2)}) %collective-permute-start.7) | collective-permute-done | bytes 81952 | tf_op jit(solution)/shard_map/cond/branch_1_fun/ppermute | solution.py:435
  156.2 6.1 %all-to-all-done.1.x_ref = bf16[128,48,128]{2,1,0:T(8,128)(2,1)S(1)} async-done(((bf16[128,48,128]{2,1,0:T(8,128)(2,1)}), bf16[128,48,128]{2,1,0:T(8,128)(2,1)S(1)}, u32[]{:S(2)}, u32[]{:S(2)}) %all-to-all-start.1) | async-done | bytes 1572896 | tf_op jit(solution)/shard_map/cond/branch_1_fun/all_to_all | solution.py:431
  (93 shorter events, 32.4 us)
Async XLA Ops:
  2.2 16.6 %collective-permute-start.10 = (bf16[592,128]{1,0:T(8,128)(2,1)S(1)}, bf16[592,128]{1,0:T(8,128)(2,1)S(1)}, u32[]{:S(2)}, u32[]{:S(2)}) collective-permute-start(bf16[592,128]{1,0:T(8,128)(2,1)S(1)} %shard_map.101), channel_id=1, source_target_pairs={{128,0},{132,4},{136,8},{140,12},{144,16},{148,20},{152,24},{156,2... | collective-permute-start | bytes 454664 | tf_op jit(solution)/shard_map/ppermute | solution.py:400
  3.5 15.3 %collective-permute-start.11 = (bf16[592,128]{1,0:T(8,128)(2,1)S(1)}, bf16[592,128]{1,0:T(8,128)(2,1)S(1)}, u32[]{:S(2)}, u32[]{:S(2)}) collective-permute-start(bf16[592,128]{1,0:T(8,128)(2,1)S(1)} %shard_map.101), channel_id=1, source_target_pairs={{256,0},{260,4},{264,8},{268,12},{272,16},{276,20},{280,24},{284,2... | collective-permute-start | bytes 454664 | tf_op jit(solution)/shard_map/ppermute | solution.py:400
  4.8 14.0 %collective-permute-start.12 = (bf16[592,128]{1,0:T(8,128)(2,1)S(1)}, bf16[592,128]{1,0:T(8,128)(2,1)S(1)}, u32[]{:S(2)}, u32[]{:S(2)}) collective-permute-start(bf16[592,128]{1,0:T(8,128)(2,1)S(1)} %shard_map.101), channel_id=1, source_target_pairs={{384,0},{388,4},{392,8},{396,12},{400,16},{404,20},{408,24},{412,2... | collective-permute-start | bytes 454664 | tf_op jit(solution)/shard_map/ppermute | solution.py:400
  19.6 3.7 %copy-start.13 = (s32[1,32]{1,0:T(1,128)S(1)}, s32[1,32]{1,0:T(1,128)}, u32[]{:S(2)}) copy-start(s32[1,32]{1,0:T(1,128)} %param.25) | copy-start | bytes 388
  22.5 65.1 %collective-permute-start.13 = (bf16[1792,384]{1,0:T(8,128)(2,1)S(1)}, bf16[1792,384]{1,0:T(8,128)(2,1)S(1)}, u32[]{:S(2)}, u32[]{:S(2)}) collective-permute-start(bf16[1792,384]{1,0:T(8,128)(2,1)S(1)} %shard_map.102), channel_id=1, source_target_pairs={{128,130},{129,131},{130,128},{131,129},{132,134},{133,135},{134,1... | collective-permute-start | bytes 4128776 | tf_op jit(solution)/shard_map/ppermute | solution.py:381
  23.4 64.3 %all-to-all-start = ((bf16[128,48,128]{2,1,0:T(8,128)(2,1)}), bf16[128,48,128]{2,1,0:T(8,128)(2,1)}, u32[]{:S(2)}, u32[]{:S(2)}) async-start(bf16[128,48,128]{2,1,0:T(8,128)(2,1)} %get-tuple-element.106), calls=%async_computation | async-start | bytes 3145728 | tf_op jit(solution)/shard_map/cond/branch_1_fun/all_to_all | solution.py:407
  41.4 4.1 %collective-permute-start = (bf16[4,592,128]{2,1,0:T(8,128)(2,1)S(1)}, bf16[4,592,128]{2,1,0:T(8,128)(2,1)}, u32[]{:S(2)}, u32[]{:S(2)}) collective-permute-start(bf16[4,592,128]{2,1,0:T(8,128)(2,1)S(1)} %branch_1_fun.13), channel_id=1, source_target_pairs={{0,1},{1,0},{2,3},{3,2},{4,5},{5,4},{6,7},{7,6},{8,9},{9,8},{10,11... | collective-permute-start | bytes 1818632 | tf_op jit(solution)/shard_map/cond/branch_1_fun/ppermute | solution.py:381
  56.8 16.9 %collective-permute-start.1 = (bf16[256,640]{1,0:T(8,128)(2,1)}, bf16[256,640]{1,0:T(8,128)(2,1)S(1)}, u32[]{:S(2)}, u32[]{:S(2)}) collective-permute-start(bf16[256,640]{1,0:T(8,128)(2,1)} %get-tuple-element.118), channel_id=1, source_target_pairs={{0,1},{1,0},{2,3},{3,2},{4,5},{5,4},{6,7},{7,6},{8,9},{9,8},{10,11... | collective-permute-start | bytes 983048 | tf_op jit(solution)/shard_map/cond/branch_1_fun/ppermute | solution.py:381
  58.9 18.6 %collective-permute-start.2 = (bf16[256,640]{1,0:T(8,128)(2,1)}, bf16[256,640]{1,0:T(8,128)(2,1)S(1)}, u32[]{:S(2)}, u32[]{:S(2)}) collective-permute-start(bf16[256,640]{1,0:T(8,128)(2,1)} %get-tuple-element.119), channel_id=1, source_target_pairs={{0,2},{1,3},{2,0},{3,1},{4,6},{5,7},{6,4},{7,5},{8,10},{9,11},{10,... | collective-permute-start | bytes 983048 | tf_op jit(solution)/shard_map/cond/branch_1_fun/ppermute | solution.py:381
  62.5 22.7 %collective-permute-start.3 = (bf16[256,640]{1,0:T(8,128)(2,1)}, bf16[256,640]{1,0:T(8,128)(2,1)S(1)}, u32[]{:S(2)}, u32[]{:S(2)}) collective-permute-start(bf16[256,640]{1,0:T(8,128)(2,1)} %get-tuple-element.120), channel_id=1, source_target_pairs={{0,3},{1,2},{2,1},{3,0},{4,7},{5,6},{6,5},{7,4},{8,11},{9,10},{10,... | collective-permute-start | bytes 983048 | tf_op jit(solution)/shard_map/cond/branch_1_fun/ppermute | solution.py:381
  87.6 13.3 %copy-start.5 = (f32[3,16,32]{1,2,0:T(8,128)S(1)}, f32[3,16,32]{1,2,0:T(8,128)}, u32[]{:S(2)}) copy-start(f32[3,16,32]{1,2,0:T(8,128)} %get-tuple-element.196) | copy-start | bytes 18436
  87.6 13.3 %copy-start.11 = (bf16[2,576]{1,0:T(2,128)(2,1)S(1)}, bf16[2,576]{1,0:T(2,128)(2,1)}, u32[]{:S(2)}) copy-start(bf16[2,576]{1,0:T(2,128)(2,1)} %param.20) | copy-start | bytes 6916
  87.7 13.3 %copy-start.12 = (f32[16,8]{0,1:T(8,128)S(1)}, f32[16,8]{0,1:T(8,128)}, u32[]{:S(2)}) copy-start(f32[16,8]{0,1:T(8,128)} %param.24) | copy-start | bytes 1540
  87.7 1.1 copy-start.3
  91.3 5.1 %collective-permute-start.4 = (bf16[384,1792]{1,0:T(8,128)(2,1)S(1)}, bf16[384,1792]{1,0:T(8,128)(2,1)S(1)}, u32[]{:S(2)}, u32[]{:S(2)}) collective-permute-start(bf16[384,1792]{1,0:T(8,128)(2,1)S(1)} %branch_1_fun.14.x_ref), channel_id=1, source_target_pairs={{128,129},{129,128},{130,131},{131,130},{132,133},{133,132},{134,1... | collective-permute-start | bytes 4128776 | tf_op jit(solution)/shard_map/cond/branch_1_fun/ppermute | solution.py:381
  97.5 1.7 %copy-start.2 = (bf16[384,1792]{1,0:T(8,128)(2,1)S(1)}, bf16[384,1792]{1,0:T(8,128)(2,1)}, u32[]{:S(2)}) copy-start(bf16[384,1792]{1,0:T(8,128)(2,1)} %get-tuple-element.126.w_ref) | copy-start | bytes 4128772 | tf_op jit(solution)/shard_map/cond
  97.5 0.8 collective-permute-start.5
  98.5 0.7 collective-permute-start.6
  101.0 1.2 copy-start.1
  102.2 29.4 %copy-start.4 = (bf16[2,128,576]{1,2,0:T(8,128)(2,1)S(1)}, bf16[2,128,576]{1,2,0:T(8,128)(2,1)}, u32[]{:S(2)}) copy-start(bf16[2,128,576]{1,2,0:T(8,128)(2,1)} %get-tuple-element.185) | copy-start | bytes 884740 | tf_op jit(solution)/shard_map/cond
  102.2 60.1 %all-to-all-start.1 = ((bf16[128,48,128]{2,1,0:T(8,128)(2,1)}), bf16[128,48,128]{2,1,0:T(8,128)(2,1)S(1)}, u32[]{:S(2)}, u32[]{:S(2)}) async-start(bf16[128,48,128]{2,1,0:T(8,128)(2,1)} %copy-done.1), calls=%async_computation.1 | async-start | bytes 3145728 | tf_op jit(solution)/shard_map/cond/branch_1_fun/all_to_all | solution.py:431
  119.8 32.1 %collective-permute-start.9 = (bf16[64,640]{1,0:T(8,128)(2,1)S(1)}, bf16[64,640]{1,0:T(8,128)(2,1)S(1)}, u32[]{:S(2)}, u32[]{:S(2)}) collective-permute-start(bf16[64,640]{1,0:T(8,128)(2,1)S(1)} %get-tuple-element.192), channel_id=1, source_target_pairs={{0,384},{4,388},{8,392},{12,396},{16,400},{20,404},{24,408},{28,41... | collective-permute-start | bytes 245768 | tf_op jit(solution)/shard_map/cond/branch_1_fun/ppermute | solution.py:435
  128.6 23.4 %collective-permute-start.8 = (bf16[64,640]{1,0:T(8,128)(2,1)S(1)}, bf16[64,640]{1,0:T(8,128)(2,1)S(1)}, u32[]{:S(2)}, u32[]{:S(2)}) collective-permute-start(bf16[64,640]{1,0:T(8,128)(2,1)S(1)} %get-tuple-element.191), channel_id=1, source_target_pairs={{0,256},{4,260},{8,264},{12,268},{16,272},{20,276},{24,280},{28,28... | collective-permute-start | bytes 245768 | tf_op jit(solution)/shard_map/cond/branch_1_fun/ppermute | solution.py:435
  129.9 25.2 %collective-permute-start.7 = (bf16[64,640]{1,0:T(8,128)(2,1)S(1)}, bf16[64,640]{1,0:T(8,128)(2,1)S(1)}, u32[]{:S(2)}, u32[]{:S(2)}) collective-permute-start(bf16[64,640]{1,0:T(8,128)(2,1)S(1)} %get-tuple-element.190), channel_id=1, source_target_pairs={{0,128},{4,132},{8,136},{12,140},{16,144},{20,148},{24,152},{28,15... | collective-permute-start | bytes 245768 | tf_op jit(solution)/shard_map/cond/branch_1_fun/ppermute | solution.py:435
  (6 other events, 4.2 us)
